TPU v7x, 32 devices: a whole 2x2x4 slice. The times are simulated.
32 devices in a mesh: dp: 4 (over z), row: 2 (over y), col: 4 (over x, core).
Axes of the slice: x: 2, y: 2, z: 4, core: 2. Of those that a mesh axis runs over, the one named last changes fastest.
Arguments:
- tokens_in: bfloat16 [16384, 1536], P(('dp', 'col'), 'row'), may hold values from -6 to 6
- norm1_gain: float32 [1536], P('row'), may hold values from 0.1 to 1.9
- w_query: bfloat16 [1536, 1536], P('row', 'col'), may hold values from -0.15625 to 0.15625
- w_keyval: bfloat16 [1536, 256], P('row'), may hold values from -0.15625 to 0.15625
- w_attn_out: bfloat16 [1536, 1536], P('col', 'row'), may hold values from -1.25 to 1.25
- norm2_gain: float32 [1536], P('row'), may hold values from 0.1 to 1.9
- w_gate: bfloat16 [1536, 4608], P('row', 'col'), may hold values from -0.15625 to 0.15625
- w_up: bfloat16 [1536, 4608], P('row', 'col'), may hold values from -0.15625 to 0.15625
- w_down: bfloat16 [4608, 1536], P('col', 'row'), may hold values from -0.1875 to 0.1875
- segment_ids: int32 [8, 2048], P(('dp', 'row')), may hold values from 0 to 5, never falling along the last dimension, each value on 1 to 800 neighbouring positions
- out_cotangent: bfloat16 [16384, 1536], P(('dp', 'col'), 'row'), may hold values from -6 to 6
Outputs:
- output: float32 [16384, 1536], P(('dp', 'col'), 'row')
- input_grad: float32 [16384, 1536], P(('dp', 'col'), 'row')
- w_query_grad: float32 [1536, 1536], P('row', 'col')
- w_keyval_grad: float32 [1536, 256], P('row')
- w_attn_out_grad: float32 [1536, 1536], P('col', 'row')
- w_gate_grad: float32 [1536, 4608], P('row', 'col')
- w_up_grad: float32 [1536, 4608], P('row', 'col')
- w_down_grad: float32 [4608, 1536], P('col', 'row')
- norm1_gain_grad: float32 [1536], P('row')
- norm2_gain_grad: float32 [1536], P('row')
Inputs may be any that keep to these rules, and one draw needn't show every extreme that they name: `segment_ids`: document numbers never fall along a sequence; a run of equal numbers has at most 800 tokens.
All inputs are finite; a program needn't handle non-finite values.
Results may differ from a plain program's by a relative error of at most 0.018.
Values may be sent and summed in bfloat16 or wider, within the bound.
No kernel may reach another device: no remote copies, remote signals or barrier semaphores. Data moves between devices by JAX's collectives and lax.ppermute only.
A program may use at most 256 MiB of HBM per device.

v0:
```python
import math

import jax
import jax.numpy as jnp
from jax import lax
from jax.sharding import PartitionSpec as P

D = 1536
HD = 128
WINDOW = 1024


EPSILON = 1e-06
NEGATIVE = -1e30


def feature_total(values):
    return lax.psum(values, "row")


def project_in(normed, weight):
    gathered = lax.all_gather(normed, "col", axis=0, tiled=True)

    def partial_term(first_row, row_count):
        return jnp.dot(gathered, weight, preferred_element_type=jnp.float32)

    result = lax.psum_scatter(
        partial_term(
            jnp.int32(0), gathered.shape[0] // lax.axis_size("row") * lax.axis_size("row")
        ),
        "row",
        scatter_dimension=0,
        tiled=True,
    )
    return (gathered, result)


def project_out(activation, weight):
    gathered = lax.all_gather(activation, "row", axis=0, tiled=True)

    def partial_term(first_row, row_count):
        return jnp.dot(gathered, weight, preferred_element_type=jnp.float32)

    result = lax.psum_scatter(
        partial_term(
            jnp.int32(0), gathered.shape[0] // lax.axis_size("col") * lax.axis_size("col")
        ),
        "col",
        scatter_dimension=0,
        tiled=True,
    )
    return (gathered, result)


def grad_from_in(grad_local, gathered, weight):
    grad_full = lax.all_gather(grad_local, "row", axis=0, tiled=True)
    weight_grad = lax.dot_general(
        gathered, grad_full, (((0,), (0,)), ((), ())), preferred_element_type=jnp.float32
    )

    def partial_term(first_row, row_count):
        return lax.dot_general(
            grad_full, weight, (((1,), (1,)), ((), ())), preferred_element_type=jnp.float32
        )

    grad_input = lax.psum_scatter(
        partial_term(
            jnp.int32(0), grad_full.shape[0] // lax.axis_size("col") * lax.axis_size("col")
        ),
        "col",
        scatter_dimension=0,
        tiled=True,
    )
    return (weight_grad, grad_input)


def grad_from_out(grad_local, gathered, weight):
    grad_full = lax.all_gather(grad_local, "col", axis=0, tiled=True)
    weight_grad = lax.dot_general(
        gathered, grad_full, (((0,), (0,)), ((), ())), preferred_element_type=jnp.float32
    )

    def partial_term(first_row, row_count):
        return lax.dot_general(
            grad_full, weight, (((1,), (1,)), ((), ())), preferred_element_type=jnp.float32
        )

    grad_input = lax.psum_scatter(
        partial_term(
            jnp.int32(0), grad_full.shape[0] // lax.axis_size("row") * lax.axis_size("row")
        ),
        "row",
        scatter_dimension=0,
        tiled=True,
    )
    return (weight_grad, grad_input)


def norm_backward(grad_normed, values, inverse, gain, width):
    scaled = grad_normed * gain
    projection = feature_total(jnp.sum(scaled * values, axis=1)) / width
    cubed = inverse * inverse * inverse
    grad_values = inverse[:, None] * scaled - values * (cubed * projection)[:, None]
    gain_part = jnp.sum(grad_normed * values * inverse[:, None], axis=0)
    return (grad_values, gain_part)


def masked_scores(queries, key_rows, segment_row, first_query):
    scale = 1.0 / math.sqrt(key_rows.shape[1])
    block_rows = queries.shape[0]
    scores = (
        jnp.einsum("qhd,kd->hqk", queries, key_rows, preferred_element_type=jnp.float32) * scale
    )
    query_pos = first_query + lax.iota(jnp.int32, block_rows)
    key_pos = lax.iota(jnp.int32, key_rows.shape[0])
    query_seg = lax.dynamic_slice_in_dim(segment_row, first_query, block_rows, 0)
    distance = query_pos[:, None] - key_pos[None, :]
    allowed = (query_seg[:, None] == segment_row[None, :]) & (distance >= 0) & (distance < WINDOW)
    return jnp.where(allowed[None], scores, NEGATIVE)


def attend_forward(inputs):
    queries, keyval, segment_row = inputs
    seq_length, head_count, head_width = queries.shape
    block_rows = min(512, seq_length)
    nblocks = seq_length // block_rows
    key_rows = keyval[:, :head_width]
    value_rows = keyval[:, head_width:]
    blocked = queries.reshape(nblocks, block_rows, head_count, head_width)
    firsts = lax.iota(jnp.int32, nblocks) * block_rows

    def one_block(block_inputs):
        query_block, first_query = block_inputs
        scores = masked_scores(query_block, key_rows, segment_row, first_query)
        row_max = jnp.max(scores, axis=-1, keepdims=True)
        exps = jnp.exp(scores - row_max)
        totals = jnp.sum(exps, axis=-1, keepdims=True)
        attn_probs = (exps / totals).astype(jnp.bfloat16)
        context = jnp.einsum(
            "hqk,kd->qhd", attn_probs, value_rows, preferred_element_type=jnp.float32
        )
        return (context.astype(jnp.bfloat16), (row_max + jnp.log(totals))[..., 0])

    context, log_totals = lax.map(one_block, (blocked, firsts))
    return (context.reshape(seq_length, head_count * head_width), log_totals)


def attend_backward(inputs):
    queries, keyval, segment_row, log_totals, grad_context = inputs
    seq_length, head_count, head_width = queries.shape
    block_rows = min(512, seq_length)
    nblocks = seq_length // block_rows
    scale = 1.0 / math.sqrt(head_width)
    key_rows = keyval[:, :head_width]
    value_rows = keyval[:, head_width:]
    blocked = queries.reshape(nblocks, block_rows, head_count, head_width)
    grad_blocked = grad_context.reshape(nblocks, block_rows, head_count, head_width)
    firsts = lax.iota(jnp.int32, nblocks) * block_rows

    def one_block(carry, block_inputs):
        query_block, first_query, log_block, grad_block = block_inputs
        scores = masked_scores(query_block, key_rows, segment_row, first_query)
        attn_probs = jnp.exp(scores - log_block[..., None])
        grad_probs = jnp.einsum(
            "qhd,kd->hqk", grad_block, value_rows, preferred_element_type=jnp.float32
        )
        inner = jnp.sum(attn_probs * grad_probs, axis=-1, keepdims=True)
        grad_scores = (attn_probs * (grad_probs - inner)).astype(jnp.bfloat16)
        grad_queries = (
            jnp.einsum("hqk,kd->qhd", grad_scores, key_rows, preferred_element_type=jnp.float32)
            * scale
        )
        grad_keys = (
            carry[0]
            + jnp.einsum(
                "hqk,qhd->kd", grad_scores, query_block, preferred_element_type=jnp.float32
            )
            * scale
        )
        grad_values = carry[1] + jnp.einsum(
            "hqk,qhd->kd",
            attn_probs.astype(jnp.bfloat16),
            grad_block,
            preferred_element_type=jnp.float32,
        )
        return ((grad_keys, grad_values), grad_queries)

    zero_rows = jnp.zeros((seq_length, head_width), jnp.float32)
    (grad_keys, grad_values), grad_queries = lax.scan(
        one_block, (zero_rows, zero_rows), (blocked, firsts, log_totals, grad_blocked)
    )
    return (
        grad_queries.reshape(seq_length, head_count * head_width),
        jnp.concatenate([grad_keys, grad_values], axis=1),
    )


def per_device(
    tokens_in,
    norm1_gain,
    w_query,
    w_keyval,
    w_attn_out,
    norm2_gain,
    w_gate,
    w_up,
    w_down,
    segment_ids,
    out_cotangent,
):
    width = D
    tokens = tokens_in.astype(jnp.float32)
    inverse_one = lax.rsqrt(feature_total(jnp.sum(tokens * tokens, axis=1)) / width + EPSILON)
    normed_one = (tokens * inverse_one[:, None] * norm1_gain).astype(jnp.bfloat16)
    query_width = w_query.shape[1]
    w_qkv = jnp.concatenate([w_query, w_keyval], axis=1)
    gathered_one, projected = project_in(normed_one, w_qkv)
    projected = projected.astype(jnp.bfloat16)
    seq_count, seq_length = segment_ids.shape
    head_count = query_width // HD
    queries = projected[:, :query_width].reshape(seq_count, seq_length, head_count, HD)
    keyval = projected[:, query_width:].reshape(seq_count, seq_length, 2 * HD)
    context, log_totals = lax.map(attend_forward, (queries, keyval, segment_ids))
    context = context.reshape(seq_count * seq_length, query_width)
    gathered_ctx, attn_branch = project_out(context, w_attn_out)
    middle = tokens + attn_branch
    inverse_two = lax.rsqrt(feature_total(jnp.sum(middle * middle, axis=1)) / width + EPSILON)
    normed_two = (middle * inverse_two[:, None] * norm2_gain).astype(jnp.bfloat16)
    hidden_width = w_gate.shape[1]
    w_gate_up = jnp.concatenate([w_gate, w_up], axis=1)
    gathered_two, gate_up = project_in(normed_two, w_gate_up)
    gate = gate_up[:, :hidden_width]
    upward = gate_up[:, hidden_width:]
    activated, gelu_back = jax.vjp(jax.nn.gelu, gate)
    hidden = (activated * upward).astype(jnp.bfloat16)
    gathered_hid, ffn_branch = project_out(hidden, w_down)
    output = middle + ffn_branch
    grad_output = out_cotangent.astype(jnp.float32)
    down_grad, grad_hidden = grad_from_out(grad_output.astype(jnp.bfloat16), gathered_hid, w_down)
    grad_gate = gelu_back(grad_hidden * upward)[0]
    grad_upward = grad_hidden * activated
    grad_gate_up = jnp.concatenate([grad_gate, grad_upward], axis=1).astype(jnp.bfloat16)
    gate_up_grad, grad_normed_two = grad_from_in(grad_gate_up, gathered_two, w_gate_up)
    grad_back_two, gain_two_part = norm_backward(
        grad_normed_two, middle, inverse_two, norm2_gain, width
    )
    grad_middle = grad_output + grad_back_two
    attn_out_grad, grad_context = grad_from_out(
        grad_middle.astype(jnp.bfloat16), gathered_ctx, w_attn_out
    )
    grad_context = grad_context.astype(jnp.bfloat16).reshape(seq_count, seq_length, head_count, HD)
    grad_queries, grad_keyval = lax.map(
        attend_backward, (queries, keyval, segment_ids, log_totals, grad_context)
    )
    grad_qkv = jnp.concatenate(
        [grad_queries.reshape(-1, query_width), grad_keyval.reshape(-1, 2 * HD)], axis=1
    ).astype(jnp.bfloat16)
    qkv_grad, grad_normed_one = grad_from_in(grad_qkv, gathered_one, w_qkv)
    grad_back_one, gain_one_part = norm_backward(
        grad_normed_one, tokens, inverse_one, norm1_gain, width
    )
    input_grad = grad_middle + grad_back_one
    keyval_grad, gain_one_grad, gain_two_grad = lax.psum(
        (qkv_grad[:, query_width:], gain_one_part, gain_two_part), ("dp", "col")
    )
    query_grad, attn_grad, gate_grad, up_grad, down_total = (
        lax.psum(qkv_grad[:, :query_width].astype(jnp.bfloat16), "dp").astype(jnp.float32),
        lax.psum(attn_out_grad.astype(jnp.bfloat16), "dp").astype(jnp.float32),
        lax.psum(gate_up_grad[:, :hidden_width].astype(jnp.bfloat16), "dp").astype(jnp.float32),
        lax.psum(gate_up_grad[:, hidden_width:].astype(jnp.bfloat16), "dp").astype(jnp.float32),
        lax.psum(down_grad.astype(jnp.bfloat16), "dp").astype(jnp.float32),
    )
    return (
        output,
        input_grad,
        query_grad,
        keyval_grad,
        attn_grad,
        gate_grad,
        up_grad,
        down_total,
        gain_one_grad,
        gain_two_grad,
    )


def solution(mesh):
    return jax.shard_map(
        per_device,
        mesh=mesh,
        in_specs=(
            P(("dp", "col"), "row"),
            P("row"),
            P("row", "col"),
            P("row", None),
            P("col", "row"),
            P("row"),
            P("row", "col"),
            P("row", "col"),
            P("col", "row"),
            P(("dp", "row"), None),
            P(("dp", "col"), "row"),
        ),
        out_specs=(
            P(("dp", "col"), "row"),
            P(("dp", "col"), "row"),
            P("row", "col"),
            P("row", None),
            P("col", "row"),
            P("row", "col"),
            P("row", "col"),
            P("col", "row"),
            P("row"),
            P("row"),
        ),
        check_vma=False,
    )
```

profile of v0, /device:TPU:0, one launch (start us, length us, event | category | flops | bytes accessed | tf_op | source)
XLA Modules:
  0.0 2538.4 jit_solution(6550105694619491602)
XLA Ops:
  20.4 46.5 %all-gather.9.cloned.1.call-done = bf16[4096,768]{1,0:T(8,128)(2,1)} async-done(((bf16[1024,768]{1,0:T(8,128)(2,1)}), bf16[4096,768]{1,0:T(8,128)(2,1)}) %all-gather.9.cloned.1.call-update) | async-done | bytes 6291472 | tf_op jit(solution)/shard_map/all_gather | solution.py:22
  67.0 9.8 fusion.79
  76.9 121.9 %reduce-scatter.9.cloned.1.call-done = f32[2048,640]{1,0:T(8,128)} async-done(((f32[4096,640]{1,0:T(8,128)}), f32[2048,640]{1,0:T(8,128)}) %reduce-scatter.9.cloned.1.call-update) | async-done | bytes 5242896 | tf_op jit(solution)/shard_map/reduce_scatter | solution.py:27
  206.8 109.3 %while.46 = (s32[]{:T(128)}, bf16[4,512,3,128]{3,1,2,0:T(8,128)(2,1)}, f32[4,3,512]{2,1,0:T(4,128)}, s32[4]{0:T(128)S(1)}, s32[2048]{0:T(1024)S(1)}, /*index=5*/...) while((s32[]{:T(128)}, ...), condition=%wide.region_6.7_spmd, body=%wide.region_3.6_spmd.sunk | while | flops 1654848512 | bytes 45946048 | solution.py:144
  323.6 44.8 %all-gather.11.cloned.1.call-done = bf16[4096,384]{0,1:T(8,128)(2,1)} async-done(((bf16[2048,384]{0,1:T(8,128)(2,1)}), bf16[4096,384]{0,1:T(8,128)(2,1)}) %all-gather.11.cloned.1.call-update) | async-done | bytes 3145744 | tf_op jit(solution)/shard_map/all_gather | solution.py:39
  368.5 10.0 fusion.80
  379.1 98.5 %reduce-scatter.11.cloned.1.call-done = f32[1024,768]{1,0:T(8,128)} async-done(((f32[4096,768]{1,0:T(8,128)}), f32[1024,768]{1,0:T(8,128)}) %reduce-scatter.11.cloned.1.call-update) | async-done | bytes 3145744 | tf_op jit(solution)/shard_map/reduce_scatter | solution.py:44
  490.4 35.1 %all-gather.17.cloned.1.call-done = bf16[4096,768]{1,0:T(8,128)(2,1)} async-done(((bf16[1024,768]{1,0:T(8,128)(2,1)}), bf16[4096,768]{1,0:T(8,128)(2,1)}) %all-gather.17.cloned.1.call-update) | async-done | bytes 6291472 | tf_op jit(solution)/shard_map/all_gather | solution.py:78
  525.5 14.7 fusion.83
  545.1 28.8 %all-gather.13.cloned.1.call-done = bf16[4096,768]{1,0:T(8,128)(2,1)} async-done(((bf16[1024,768]{1,0:T(8,128)(2,1)}), bf16[4096,768]{1,0:T(8,128)(2,1)}) %all-gather.13.cloned.1.call-update) | async-done | bytes 6291472 | tf_op jit(solution)/shard_map/all_gather | solution.py:22
  573.9 23.1 fusion.81
  597.1 190.8 %reduce-scatter.17.cloned.1.call-done = f32[2048,1152]{1,0:T(8,128)} async-done(((f32[4096,1152]{1,0:T(8,128)}), f32[2048,1152]{1,0:T(8,128)}) %reduce-scatter.17.cloned.1.call-update) | async-done | bytes 9437200 | tf_op jit(solution)/shard_map/reduce_scatter | solution.py:88
  787.9 416.3 %reduce-scatter.13.cloned.1.call-done = f32[2048,2304]{1,0:T(8,128)} async-done(((f32[4096,2304]{1,0:T(8,128)}), f32[2048,2304]{1,0:T(8,128)}) %reduce-scatter.13.cloned.1.call-update) | async-done | bytes 18874384 | tf_op jit(solution)/shard_map/reduce_scatter | solution.py:27
  1204.2 15.2 fusion.65
  1224.2 224.3 %all-gather.19.cloned.1.call-done = bf16[4096,2304]{1,0:T(8,128)(2,1)} async-done(((bf16[2048,2304]{1,0:T(8,128)(2,1)}), bf16[4096,2304]{1,0:T(8,128)(2,1)}) %all-gather.19.cloned.1.call-update) | async-done | bytes 18874384 | tf_op jit(solution)/shard_map/all_gather | solution.py:56
  1448.5 21.4 fusion.84
  1470.1 99.1 %reduce-scatter.19.cloned.1.call-done = f32[1024,768]{1,0:T(8,128)} async-done(((f32[4096,768]{1,0:T(8,128)}), f32[1024,768]{1,0:T(8,128)}) %reduce-scatter.19.cloned.1.call-update) | async-done | bytes 3145744 | tf_op jit(solution)/shard_map/reduce_scatter | solution.py:66
  1583.1 46.5 %all-gather.21.cloned.1.call-done = bf16[4096,768]{1,0:T(8,128)(2,1)} async-done(((bf16[1024,768]{1,0:T(8,128)(2,1)}), bf16[4096,768]{1,0:T(8,128)(2,1)}) %all-gather.21.cloned.1.call-update) | async-done | bytes 6291472 | tf_op jit(solution)/shard_map/all_gather | solution.py:78
  1639.5 76.4 %reduce-scatter.21.cloned.1.call-done = f32[2048,384]{1,0:T(8,128)} async-done(((f32[4096,384]{1,0:T(8,128)}), f32[2048,384]{1,0:T(8,128)}) %reduce-scatter.21.cloned.1.call-update) | async-done | bytes 3145744 | tf_op jit(solution)/shard_map/reduce_scatter | solution.py:88
  1727.7 180.8 %while.47 = (s32[]{:T(128)}, f32[2048,128]{1,0:T(8,128)}, f32[2048,128]{1,0:T(8,128)}, bf16[4,512,3,128]{3,1,2,0:T(8,128)(2,1)}, s32[4]{0:T(128)S(1)}, /*index=5...) while((s32[]{:T(128)}, f32[2048,128]{1,0:T(8,128)}, ...), condition=%wide.region_19.20_spmd.clone, body=%wide.region_17.19_spmd.clone.sunk | while | flops 4081515520 | bytes 184351520 | solution.py:189
  1808.4 9.6 fusion.150
  1853.6 9.6 fusion.150
  1920.5 12.7 convolution_convert_fusion.1
  1933.1 20.5 convolution_convert_fusion
  1960.3 28.8 %all-gather.23.cloned.1.call-done = bf16[4096,640]{0,1:T(8,128)(2,1)} async-done(((bf16[2048,640]{0,1:T(8,128)(2,1)}), bf16[4096,640]{0,1:T(8,128)(2,1)}) %all-gather.23.cloned.1.call-update) | async-done | bytes 5242896 | tf_op jit(solution)/shard_map/all_gather | solution.py:56
  2000.2 10.0 fusion.86
  2010.3 13.5 fusion.82
  2026.0 204.9 %all-reduce.7.cloned.1.call-done = (bf16[768,384]{1,0:T(8,128)(2,1)}, bf16[384,768]{1,0:T(8,128)(2,1)}, bf16[768,1152]{1,0:T(8,128)(2,1)}, bf16[768,1152]{1,0:T(8,128)(2,1)}, bf16[1152,768]{1,0:T(8,128)(2,1)}) async-done(((bf16[768,384]{1,0:T(8,128)(2,1)}, bf16[384,768]{1,0:T(8,128)(2,1)}, bf16[768,1152]{1,0:T(8,128)(2,1)}, bf16[768,1152]{1,0:T(8,128)(2,1)}, bf16[1152,768]{1,0:T(8,128)(2,1)}), ...) | async-done | bytes 6488080 | tf_op jit(solution)/shard_map/psum | solution.py:267
  2241.0 90.3 %reduce-scatter.23.cloned.1.call-done = f32[1024,768]{1,0:T(8,128)} async-done(((f32[4096,768]{1,0:T(8,128)}), f32[1024,768]{1,0:T(8,128)}) %reduce-scatter.23.cloned.1.call-update) | async-done | bytes 3145744 | tf_op jit(solution)/shard_map/reduce_scatter | solution.py:66
  2339.3 32.4 %all-reduce = (f32[768]{0:T(1024)}, f32[768]{0:T(1024)}) all-reduce(f32[768]{0:T(1024)S(1)} %get-tuple-element.235, f32[768]{0:T(1024)S(1)} %copy-done.35), channel_id=1, replica_groups=mesh['dp'=4,'row'=2,'col'=4] {'dp','col'}, use_global_device_ids=true, to_apply=%region_30.31 | all-reduce | flops 1536 | bytes 12288 | tf_op jit(solution)/shard_map/psum | solution.py:263
  2371.6 61.4 %reduce-scatter.15.cloned.1.call-done = f32[1024,768]{1,0:T(8,128)} async-done(((f32[4096,768]{1,0:T(8,128)}), f32[1024,768]{1,0:T(8,128)}) %reduce-scatter.15.cloned.1.call-update) | async-done | bytes 3145744 | tf_op jit(solution)/shard_map/reduce_scatter | solution.py:44
  2441.2 87.8 %all-reduce.5.cloned.1.call-done = f32[768,256]{1,0:T(8,128)} async-done(((f32[768,256]{1,0:T(8,128)}), f32[768,256]{1,0:T(8,128)}) %all-reduce.5.cloned.1.call-update) | async-done | bytes 786448 | tf_op jit(solution)/shard_map/psum | solution.py:263
  (270 shorter events, 402.0 us)
Async XLA Ops:
  7.2 518.3 %copy-start = (bf16[1152,768]{1,0:T(8,128)(2,1)S(1)}, bf16[1152,768]{1,0:T(8,128)(2,1)}, u32[]{:S(2)}) copy-start(bf16[1152,768]{1,0:T(8,128)(2,1)} %param.23) | copy-start | bytes 5308420
  7.2 59.8 %all-gather.9.cloned.1.call-start = ((), (), s32[]{:S(2)}) async-start(), calls=%async_computation.8 | async-start | bytes 7864320 | tf_op jit(solution)/shard_map/all_gather | solution.py:22
  18.7 180.2 %reduce-scatter.9.cloned.1.call-start = ((), (), s32[]{:S(2)}) async-start(), calls=%async_computation.9 | async-start | bytes 15728640 | tf_op jit(solution)/shard_map/reduce_scatter | solution.py:27
  76.8 291.6 %all-gather.11.cloned.1.call-start = ((), (), s32[]{:S(2)}) async-start(), calls=%async_computation.10 | async-start | bytes 4718592 | tf_op jit(solution)/shard_map/all_gather | solution.py:39
  323.4 154.3 %reduce-scatter.11.cloned.1.call-start = ((), (), s32[]{:S(2)}) async-start(), calls=%async_computation.11 | async-start | bytes 15728640 | tf_op jit(solution)/shard_map/reduce_scatter | solution.py:44
  378.5 99.2 %copy-start.4 = (bf16[1024,768]{1,0:T(8,128)(2,1)S(1)}, bf16[1024,768]{1,0:T(8,128)(2,1)}, u32[]{:S(2)}) copy-start(bf16[1024,768]{1,0:T(8,128)(2,1)} %param.15) | copy-start | bytes 4718596
  378.5 147.0 %all-gather.17.cloned.1.call-start = ((), (), s32[]{:S(2)}) async-start(), calls=%async_computation.16 | async-start | bytes 7864320 | tf_op jit(solution)/shard_map/all_gather | solution.py:78
  379.1 107.5 %copy-start.24 = (f32[768]{0:T(1024)S(1)}, f32[768]{0:T(1024)}, u32[]{:S(2)}) copy-start(f32[768]{0:T(1024)} %param.20) | copy-start | bytes 9220
  379.1 194.8 %all-gather.13.cloned.1.call-start = ((), (), s32[]{:S(2)}) async-start(), calls=%async_computation.12 | async-start | bytes 7864320 | tf_op jit(solution)/shard_map/all_gather | solution.py:22
  486.6 1091.8 %copy-start.22 = (f32[1024]{0:T(1024)}, f32[1024]{0:T(1024)S(1)}, u32[]{:S(2)}) copy-start(f32[1024]{0:T(1024)S(1)} %add_rsqrt_fusion) | copy-start | bytes 12292
  490.4 297.6 %reduce-scatter.17.cloned.1.call-start = ((), (), s32[]{:S(2)}) async-start(), calls=%async_computation.17 | async-start | bytes 28311552 | tf_op jit(solution)/shard_map/reduce_scatter | solution.py:88
  540.2 664.0 %reduce-scatter.13.cloned.1.call-start = ((), (), s32[]{:S(2)}) async-start(), calls=%async_computation.13 | async-start | bytes 56623104 | tf_op jit(solution)/shard_map/reduce_scatter | solution.py:27
  597.1 851.4 %all-gather.19.cloned.1.call-start = ((), (), s32[]{:S(2)}) async-start(), calls=%async_computation.18 | async-start | bytes 28311552 | tf_op jit(solution)/shard_map/all_gather | solution.py:56
  1224.0 345.2 %reduce-scatter.19.cloned.1.call-start = ((), (), s32[]{:S(2)}) async-start(), calls=%async_computation.19 | async-start | bytes 15728640 | tf_op jit(solution)/shard_map/reduce_scatter | solution.py:66
  1470.0 108.3 %copy-start.34 = (f32[1024]{0:T(1024)S(1)}, f32[1024]{0:T(1024)}, u32[]{:S(2)}) copy-start(f32[1024]{0:T(1024)} %copy-done.33) | copy-start | bytes 12292
  1470.0 108.3 %copy-start.10 = (bf16[1024,768]{1,0:T(8,128)(2,1)S(1)}, bf16[1024,768]{1,0:T(8,128)(2,1)}, u32[]{:S(2)}) copy-start(bf16[1024,768]{1,0:T(8,128)(2,1)} %param.25) | copy-start | bytes 4718596
  1470.0 159.6 %all-gather.21.cloned.1.call-start = ((), (), s32[]{:S(2)}) async-start(), calls=%async_computation.20 | async-start | bytes 7864320 | tf_op jit(solution)/shard_map/all_gather | solution.py:78
  1583.1 132.8 %reduce-scatter.21.cloned.1.call-start = ((), (), s32[]{:S(2)}) async-start(), calls=%async_computation.21 | async-start | bytes 9437184 | tf_op jit(solution)/shard_map/reduce_scatter | solution.py:88
  1638.7 281.8 %all-gather.15.cloned.1.call-start = ((), (), s32[]{:S(2)}) async-start(), calls=%async_computation.14 | async-start | bytes 14155776 | tf_op jit(solution)/shard_map/all_gather | solution.py:39
  1639.4 349.6 %all-gather.23.cloned.1.call-start = ((), (), s32[]{:S(2)}) async-start(), calls=%async_computation.22 | async-start | bytes 7864320 | tf_op jit(solution)/shard_map/all_gather | solution.py:56
  1920.4 310.5 %all-reduce.7.cloned.1.call-start = ((), (), s32[]{:S(2)}) async-start(), calls=%async_computation.25 | async-start | bytes 12976128 | tf_op jit(solution)/shard_map/psum | solution.py:267
  2000.2 331.1 %reduce-scatter.23.cloned.1.call-start = ((), (), s32[]{:S(2)}) async-start(), calls=%async_computation.23 | async-start | bytes 15728640 | tf_op jit(solution)/shard_map/reduce_scatter | solution.py:66
  2010.2 422.8 %reduce-scatter.15.cloned.1.call-start = ((), (), s32[]{:S(2)}) async-start(), calls=%async_computation.15 | async-start | bytes 15728640 | tf_op jit(solution)/shard_map/reduce_scatter | solution.py:44
  2023.8 505.2 %all-reduce.5.cloned.1.call-start = ((), (), s32[]{:S(2)}) async-start(), calls=%async_computation.24 | async-start | bytes 1572864 | tf_op jit(solution)/shard_map/psum | solution.py:263
  2236.6 94.7 %copy-start.5 = (bf16[1024,768]{1,0:T(8,128)(2,1)S(1)}, bf16[1024,768]{1,0:T(8,128)(2,1)}, u32[]{:S(2)}) copy-start(bf16[1024,768]{1,0:T(8,128)(2,1)} %param.15) | copy-start | bytes 4718596
  2236.6 94.7 %copy-start.27 = (f32[1024]{0:T(1024)S(1)}, f32[1024]{0:T(1024)}, u32[]{:S(2)}) copy-start(f32[1024]{0:T(1024)} %copy-done.26) | copy-start | bytes 12292
  2236.6 94.7 %copy-start.30 = (f32[768]{0:T(1024)S(1)}, f32[768]{0:T(1024)}, u32[]{:S(2)}) copy-start(f32[768]{0:T(1024)} %param.16) | copy-start | bytes 9220
  2238.8 100.5 %copy-start.32 = (f32[1024]{0:T(1024)S(1)}, f32[1024]{0:T(1024)}, u32[]{:S(2)}) copy-start(f32[1024]{0:T(1024)} %copy-done.31) | copy-start | bytes 12292
  2238.8 100.5 %copy-start.35 = (f32[768]{0:T(1024)S(1)}, f32[768]{0:T(1024)}, u32[]{:S(2)}) copy-start(f32[768]{0:T(1024)} %get-tuple-element.233) | copy-start | bytes 9220
  2238.8 194.3 %copy-start.23 = (f32[1024]{0:T(1024)S(1)}, f32[1024]{0:T(1024)}, u32[]{:S(2)}) copy-start(f32[1024]{0:T(1024)} %copy-done.22) | copy-start | bytes 12292
  2238.8 194.3 %copy-start.25 = (f32[768]{0:T(1024)S(1)}, f32[768]{0:T(1024)}, u32[]{:S(2)}) copy-start(f32[768]{0:T(1024)} %param.20) | copy-start | bytes 9220
  2238.8 194.3 %copy-start.29 = (f32[1024]{0:T(1024)S(1)}, f32[1024]{0:T(1024)}, u32[]{:S(2)}) copy-start(f32[1024]{0:T(1024)} %copy-done.28) | copy-start | bytes 12292
  (38 other events, 495.1 us)
Sparse Core Ops, SparseCore 0:
  18.8 48.1 all-gather.8
  76.9 121.8 reduce-scatter.8
  323.5 44.9 all-gather.10
  378.6 99.0 reduce-scatter.10
  479.1 46.3 all-gather.16
  527.5 46.3 all-gather.12
  576.2 211.6 reduce-scatter.16
  790.2 413.9 reduce-scatter.12
  1224.1 224.3 all-gather.18
  1470.1 99.0 reduce-scatter.18
  1583.2 46.3 all-gather.20
  1638.8 77.0 reduce-scatter.20
  1717.5 118.0 all-gather.14
  1920.5 68.5 all-gather.22
  2000.3 230.5 all-reduce.6
  2233.3 97.8 reduce-scatter.22
  2333.7 99.3 reduce-scatter.14
  2436.9 92.1 all-reduce.4
where the time goes:
time: 2550 us; the launch traced here: 2540 us
  waiting for transfers between devices  1900 us (75%)
  matrix products  330 us (13%)
  other arithmetic  153 us (6%)
  local copies, waits for them, and re-layouts  65.1 us (3%)
  blocking collectives  53 us (2%)
    reduce_scatter x2, waiting for transfers between devices, project_in(): lax.psum_scatter(partial_term(jnp.int32(0), gathered.shape[0] // lax.axis...  538 us
    reduce_scatter x2, waiting for transfers between devices, grad_from_out(): lax.psum_scatter(partial_term(jnp.int32(0), grad_full.shape[0] // lax.axi...  267 us
    all_gather x2, waiting for transfers between devices, grad_from_in(): grad_full = lax.all_gather(grad_local, 'row', axis=0, tiled=True)  253 us
    psum x1, waiting for transfers between devices, per_device(): lax.psum(qkv_grad[:, :query_width].astype(jnp.bfloat16), 'dp')  205 us
    reduce_scatter x2, waiting for transfers between devices, grad_from_in(): lax.psum_scatter(partial_term(jnp.int32(0), grad_full.shape[0] // lax.axi...  189 us
    reduce_scatter x2, waiting for transfers between devices, project_out(): lax.psum_scatter(partial_term(jnp.int32(0), gathered.shape[0] // lax.axis...  160 us
    psum x1, waiting for transfers between devices, per_device(): lax.psum((qkv_grad[:, query_width:], gain_one_part, gain_two_part), ('dp'...  87.8 us
    all_gather x2, waiting for transfers between devices, grad_from_out(): grad_full = lax.all_gather(grad_local, 'col', axis=0, tiled=True)  81.6 us
  transfers between devices with their start and end apart: 18, of which 17 were waited for; matrix products, arithmetic and copies ran while one was open for 13% of the time, Pallas kernels for 0%

commit v1 on v0

v1 whole, which is shorter than its diff:
```python
import functools
import math

import jax
import jax.numpy as jnp
from jax import lax
from jax.experimental import pallas as pl
from jax.experimental.pallas import tpu as pltpu
from jax.sharding import PartitionSpec as P

D = 1536
HD = 128
WINDOW = 1024
EPSILON = 1e-06
NEGATIVE = -1e30
BF16 = jnp.bfloat16
F32 = jnp.float32
VMEM_BYTES = 56 * 1024 * 1024


def after(value, *earlier):
    return lax.optimization_barrier((value, *earlier))[0]


def swap_row(value):
    return lax.ppermute(value, "row", [(0, 1), (1, 0)])


def swap_core(value):
    return lax.ppermute(value, "col", [(0, 1), (1, 0), (2, 3), (3, 2)])


def swap_far(value):
    return lax.ppermute(value, "col", [(0, 2), (2, 0), (1, 3), (3, 1)])


def dot(left, right, out=F32):
    return jnp.dot(left, right, preferred_element_type=F32).astype(out)


def dot_t(left, right, out=F32):
    return lax.dot_general(
        left, right, (((1,), (1,)), ((), ())), preferred_element_type=F32
    ).astype(out)


def t_dot(left, right, out=F32):
    return lax.dot_general(
        left, right, (((0,), (0,)), ((), ())), preferred_element_type=F32
    ).astype(out)


def total_over_dp(part):
    count = lax.axis_size("dp")
    if count != 4:
        return lax.psum(part, "dp").astype(F32)
    place = lax.axis_index("dp")
    inward = lax.ppermute(part, "dp", [(0, 1), (3, 2)])
    pair = part + inward
    across = lax.ppermute(pair, "dp", [(1, 2), (2, 1)])
    both = pair + across
    back = lax.ppermute(both, "dp", [(1, 0), (2, 3)])
    outer = (place == 0) | (place == 3)
    return jnp.where(outer, back, both).astype(F32)


def gather_col(block):
    far = swap_far(block)
    near = swap_core(block)
    diagonal = swap_core(far)
    return (block, near, far, diagonal)


def scatter_col(own, near, far, diagonal):
    near_in = swap_core(near)
    diagonal_in = swap_core(diagonal)
    for_far = (far.astype(F32) + diagonal_in.astype(F32)).astype(BF16)
    far_in = swap_far(for_far)
    return own.astype(F32) + near_in.astype(F32) + far_in.astype(F32)


def block_bias(first_query, first_key, rows, cols, query_segs, key_segs):
    query_pos = first_query + lax.broadcasted_iota(jnp.int32, (rows, cols), 0)
    key_pos = first_key + lax.broadcasted_iota(jnp.int32, (rows, cols), 1)
    distance = query_pos - key_pos
    allowed = (query_segs == key_segs) & (distance >= 0) & (distance < WINDOW)
    return jnp.where(allowed, 0.0, NEGATIVE)


def first_block(first_query, query_segs, key_segs, tile_k):
    earlier = jnp.sum((key_segs < query_segs[0:1, 0:1]).astype(jnp.int32))
    return lax.div(jnp.maximum(earlier, first_query - (WINDOW - 1)), tile_k)


def attend_forward_kernel(start, q, kv, seg_q, seg_k, ctx, lse, m_s, l_s, acc_s, *, tq, tk, heads):
    first_query = start[0] + pl.program_id(0) * tq
    query_segs = seg_q[...]
    low_block = first_block(first_query, query_segs, seg_k[...], tk)
    high_block = lax.div(first_query + tq - 1, tk)
    scale = 1.0 / math.sqrt(HD)

    def step(block, first):
        first_key = pl.multiple_of(block * tk, tk)
        keys = kv[pl.ds(first_key, tk), :HD]
        values = kv[pl.ds(first_key, tk), HD:]
        bias = block_bias(first_query, first_key, tq, tk, query_segs, seg_k[:, pl.ds(first_key, tk)])
        for h in range(heads):
            cols = slice(h * HD, (h + 1) * HD)
            scores = dot_t(q[:, cols], keys) * scale + bias
            top = jnp.max(scores, axis=1, keepdims=True)
            if first:
                new = jnp.broadcast_to(top, (tq, HD))
                exps = jnp.exp(scores - top)
                l_s[:, cols] = jnp.broadcast_to(jnp.sum(exps, axis=1, keepdims=True), (tq, HD))
                acc_s[:, cols] = dot(exps.astype(BF16), values)
                m_s[:, cols] = new
            else:
                old = m_s[:, cols]
                new = jnp.maximum(old, top)
                fade = jnp.exp(old - new)
                exps = jnp.exp(scores - jnp.tile(new, (1, tk // HD)))
                l_s[:, cols] = l_s[:, cols] * fade + jnp.sum(exps, axis=1, keepdims=True)
                acc_s[:, cols] = acc_s[:, cols] * fade + dot(exps.astype(BF16), values)
                m_s[:, cols] = new

    step(high_block, True)

    def body(i, _):
        step(high_block - i, False)
        return 0

    lax.fori_loop(1, high_block - low_block + 1, body, 0)
    lane = lax.broadcasted_iota(jnp.int32, (tq, HD), 1)
    logs = jnp.zeros((tq, HD), F32)
    for h in range(heads):
        cols = slice(h * HD, (h + 1) * HD)
        total = l_s[:, cols]
        ctx[:, cols] = (acc_s[:, cols] / total).astype(BF16)
        logs = jnp.where(lane == h, m_s[:, cols] + jnp.log(total), logs)
    lse[...] = logs


def attend_forward(start, q, kv, seg_q, seg_k):
    rows, width = q.shape
    heads = width // HD
    tq = tk = 256
    length = kv.shape[0]
    return pl.pallas_call(
        functools.partial(attend_forward_kernel, tq=tq, tk=tk, heads=heads),
        grid=(rows // tq,),
        in_specs=[
            pl.BlockSpec(memory_space=pltpu.SMEM),
            pl.BlockSpec((tq, width), lambda i: (i, 0)),
            pl.BlockSpec((length, 2 * HD), lambda i: (0, 0)),
            pl.BlockSpec((tq, 1), lambda i: (i, 0)),
            pl.BlockSpec((1, length), lambda i: (0, 0)),
        ],
        out_specs=[
            pl.BlockSpec((tq, width), lambda i: (i, 0)),
            pl.BlockSpec((tq, HD), lambda i: (i, 0)),
        ],
        out_shape=[
            jax.ShapeDtypeStruct((rows, width), BF16),
            jax.ShapeDtypeStruct((rows, HD), F32),
        ],
        scratch_shapes=[
            pltpu.VMEM((tq, width), F32),
            pltpu.VMEM((tq, width), F32),
            pltpu.VMEM((tq, width), F32),
        ],
        compiler_params=pltpu.CompilerParams(vmem_limit_bytes=VMEM_BYTES),
        name="attend_forward",
    )(start, q, kv, seg_q, seg_k)


def attend_backward_kernel(
    start, q, kv, seg_q, seg_k, ctx, lse, dctx, dq, dkv, dq_s, *, tq, tk, heads
):
    first_query = start[0] + pl.program_id(0) * tq
    query_segs = seg_q[...]
    low_block = first_block(first_query, query_segs, seg_k[...], tk)
    high_block = lax.div(first_query + tq - 1, tk)
    scale = 1.0 / math.sqrt(HD)

    @pl.when(pl.program_id(0) == 0)
    def _():
        dkv[...] = jnp.zeros_like(dkv)

    dq_s[...] = jnp.zeros_like(dq_s)
    logs = lse[...]

    def body(i, _):
        first_key = pl.multiple_of((high_block - i) * tk, tk)
        keys = kv[pl.ds(first_key, tk), :HD]
        values = kv[pl.ds(first_key, tk), HD:]
        bias = block_bias(first_query, first_key, tq, tk, query_segs, seg_k[:, pl.ds(first_key, tk)])
        dk = jnp.zeros((tk, HD), F32)
        dv = jnp.zeros((tk, HD), F32)
        for h in range(heads):
            cols = slice(h * HD, (h + 1) * HD)
            q_h = q[:, cols]
            do_h = dctx[:, cols]
            inner = jnp.sum(do_h.astype(F32) * ctx[:, cols].astype(F32), axis=1, keepdims=True)
            scores = dot_t(q_h, keys) * scale + bias
            probs = jnp.exp(scores - logs[:, h : h + 1])
            dprobs = dot_t(do_h, values)
            dscores = (probs * (dprobs - inner)).astype(BF16)
            dq_s[:, cols] += dot(dscores, keys)
            dk = dk + t_dot(dscores, q_h)
            dv = dv + t_dot(probs.astype(BF16), do_h)
        dkv[pl.ds(first_key, tk), :HD] += dk * scale
        dkv[pl.ds(first_key, tk), HD:] += dv
        return 0

    lax.fori_loop(0, high_block - low_block + 1, body, 0)
    dq[...] = (dq_s[...] * scale).astype(BF16)


def attend_backward(start, q, kv, seg_q, seg_k, ctx, lse, dctx):
    rows, width = q.shape
    heads = width // HD
    tq = tk = 256
    length = kv.shape[0]
    return pl.pallas_call(
        functools.partial(attend_backward_kernel, tq=tq, tk=tk, heads=heads),
        grid=(rows // tq,),
        in_specs=[
            pl.BlockSpec(memory_space=pltpu.SMEM),
            pl.BlockSpec((tq, width), lambda i: (i, 0)),
            pl.BlockSpec((length, 2 * HD), lambda i: (0, 0)),
            pl.BlockSpec((tq, 1), lambda i: (i, 0)),
            pl.BlockSpec((1, length), lambda i: (0, 0)),
            pl.BlockSpec((tq, width), lambda i: (i, 0)),
            pl.BlockSpec((tq, HD), lambda i: (i, 0)),
            pl.BlockSpec((tq, width), lambda i: (i, 0)),
        ],
        out_specs=[
            pl.BlockSpec((tq, width), lambda i: (i, 0)),
            pl.BlockSpec((length, 2 * HD), lambda i: (0, 0)),
        ],
        out_shape=[
            jax.ShapeDtypeStruct((rows, width), BF16),
            jax.ShapeDtypeStruct((length, 2 * HD), F32),
        ],
        scratch_shapes=[pltpu.VMEM((tq, width), F32)],
        compiler_params=pltpu.CompilerParams(vmem_limit_bytes=VMEM_BYTES),
        name="attend_backward",
    )(start, q, kv, seg_q, seg_k, ctx, lse, dctx)


def feed_kernel(n2, dy, wg, wu, wd, hidden, dgate, dup):
    gate = dot(n2[...], wg[...])
    up = dot(n2[...], wu[...])
    dh = dot_t(dy[...], wd[...])
    root = math.sqrt(2.0 / math.pi)
    square = gate * gate
    tanh = jnp.tanh(root * (gate + 0.044715 * gate * square))
    half = 0.5 * (1.0 + tanh)
    act = gate * half
    slope = half + 0.5 * gate * (1.0 - tanh * tanh) * (root * (1.0 + 3.0 * 0.044715 * square))
    hidden[...] = (act * up).astype(BF16)
    dgate[...] = (dh * up * slope).astype(BF16)
    dup[...] = (dh * act).astype(BF16)


def feed(n2, dy, wg, wu, wd):
    rows, width = n2.shape
    units = wg.shape[1]
    tm, tn = 512, 384
    out = jax.ShapeDtypeStruct((rows, units), BF16)
    return pl.pallas_call(
        feed_kernel,
        grid=(units // tn, rows // tm),
        in_specs=[
            pl.BlockSpec((tm, width), lambda j, i: (i, 0)),
            pl.BlockSpec((tm, width), lambda j, i: (i, 0)),
            pl.BlockSpec((width, tn), lambda j, i: (0, j)),
            pl.BlockSpec((width, tn), lambda j, i: (0, j)),
            pl.BlockSpec((tn, width), lambda j, i: (j, 0)),
        ],
        out_specs=[pl.BlockSpec((tm, tn), lambda j, i: (i, j))] * 3,
        out_shape=[out] * 3,
        compiler_params=pltpu.CompilerParams(vmem_limit_bytes=VMEM_BYTES),
        name="feed",
    )(n2, dy, wg, wu, wd)


def per_device(
    tokens_in,
    norm1_gain,
    w_query,
    w_keyval,
    w_attn_out,
    norm2_gain,
    w_gate,
    w_up,
    w_down,
    segment_ids,
    out_cotangent,
):
    width = D
    row = lax.axis_index("row")
    col = lax.axis_index("col")
    local = tokens_in.shape[0]
    mine = local // 2
    feats = tokens_in.shape[1]
    length = segment_ids.shape[1]
    spans = length // local

    def keep(value):
        return lax.dynamic_slice_in_dim(value, row * mine, mine, 0)

    def give(value):
        return lax.dynamic_slice_in_dim(value, (1 - row) * mine, mine, 0)

    x_in = swap_row(give(tokens_in))
    gains = jnp.stack([norm1_gain, norm2_gain])
    gains_in = swap_row(gains)
    gain_one = jnp.concatenate([norm1_gain, gains_in[0]])
    gain_two = jnp.concatenate([norm2_gain, gains_in[1]])
    segs_in = swap_row(segment_ids)
    is_low = row == 0
    segs_all = jnp.concatenate(
        [jnp.where(is_low, segment_ids, segs_in), jnp.where(is_low, segs_in, segment_ids)], axis=0
    )
    wkv_in = swap_row(w_keyval)
    wq_in = swap_row(w_query)
    wo_in = swap_row(after(w_attn_out, wq_in))
    dy_in = swap_row(after(give(out_cotangent), wo_in))
    wg_in = swap_row(after(w_gate, dy_in))
    wu_in = swap_row(after(w_up, wg_in))
    wd_in = swap_row(after(w_down, wu_in))

    wq_own = jnp.concatenate([w_query, wq_in], axis=0)
    wo_own = jnp.concatenate([w_attn_out, wo_in], axis=1)
    wq_all = jnp.concatenate(gather_col(wq_own), axis=1)
    wo_all = jnp.concatenate(gather_col(after(wo_own, wq_all)), axis=0)
    wkv = jnp.concatenate([w_keyval, wkv_in], axis=0)
    wg = jnp.concatenate([w_gate, wg_in], axis=0)
    wu = jnp.concatenate([w_up, wu_in], axis=0)
    wd = jnp.concatenate([w_down, wd_in], axis=1)

    x = jnp.concatenate([keep(tokens_in), x_in], axis=1).astype(F32)
    inverse_one = lax.rsqrt(jnp.mean(x * x, axis=1, keepdims=True) + EPSILON)
    normed_one = (x * inverse_one * gain_one).astype(BF16)
    kv_own = dot(normed_one, wkv, BF16)
    kv_in = swap_row(kv_own)
    kv_pair = jnp.concatenate(
        [jnp.where(is_low, kv_own, kv_in), jnp.where(is_low, kv_in, kv_own)], axis=0
    )
    place = col % spans
    if spans == 2:
        kv_far = swap_core(kv_pair)
        first = place == 0
        kv = jnp.concatenate(
            [jnp.where(first, kv_pair, kv_far), jnp.where(first, kv_far, kv_pair)], axis=0
        )
    else:
        kv = kv_pair
    seg_row = lax.dynamic_slice_in_dim(segs_all, col // spans, 1, 0)
    first_token = place * local + row * mine
    seg_q = lax.dynamic_slice_in_dim(seg_row[0], first_token, mine, 0)[:, None]
    start = jnp.reshape(first_token, (1,)).astype(jnp.int32)

    q = dot(normed_one, wq_all, BF16)
    ctx, lse = attend_forward(start, q, kv, seg_q, seg_row)
    middle = x + dot(ctx, wo_all)
    inverse_two = lax.rsqrt(jnp.mean(middle * middle, axis=1, keepdims=True) + EPSILON)
    normed_two = (middle * inverse_two * gain_two).astype(BF16)

    dy = jnp.concatenate([keep(out_cotangent), dy_in], axis=1)
    dy_all = jnp.concatenate(gather_col(dy), axis=0)
    n2_all = jnp.concatenate(gather_col(normed_two), axis=0)
    hidden, dgate, dup = feed(n2_all, dy_all, wg, wu, wd)
    dn2 = dot_t(dgate, wg) + dot_t(dup, wu)
    dn2 = dn2.astype(BF16)
    down_part = t_dot(hidden, dy_all, BF16)
    gate_part = t_dot(n2_all, dgate, BF16)
    up_part = t_dot(n2_all, dup, BF16)
    ffn = dot(hidden, wd, BF16)

    def rows_from_row(part):
        return part[:feats] + swap_row(part[feats:])

    def cols_from_row(part):
        return part[:, :feats] + swap_row(part[:, feats:])

    down_total = total_over_dp(cols_from_row(down_part))
    gate_total = total_over_dp(rows_from_row(gate_part))
    up_total = total_over_dp(rows_from_row(up_part))

    def blocks(value):
        return [value[i * mine : (i + 1) * mine] for i in range(4)]

    dnormed_two = scatter_col(*blocks(dn2))
    scaled = dnormed_two * gain_two
    projection = jnp.mean(scaled * middle, axis=1, keepdims=True)
    dmiddle = dy.astype(F32) + inverse_two * scaled - middle * (inverse_two**3 * projection)
    gain_two_part = jnp.sum(dnormed_two * middle * inverse_two, axis=0)

    dattn = dmiddle.astype(BF16)
    dctx = dot_t(dattn, wo_all, BF16)
    dq, dkv_all = attend_backward(start, q, kv, seg_q, seg_row, ctx, lse, dctx)
    if spans == 2:
        low_half, high_half = dkv_all[:local], dkv_all[local:]
        ours = jnp.where(place == 0, low_half, high_half)
        theirs = jnp.where(place == 0, high_half, low_half)
        dkv_pair = ours + swap_core(theirs.astype(BF16)).astype(F32)
    else:
        dkv_pair = dkv_all
    dkv = keep(dkv_pair) + swap_row(give(dkv_pair).astype(BF16)).astype(F32)
    dkv = dkv.astype(BF16)
    dnormed_one = dot_t(dq, wq_all) + dot_t(dkv, wkv)
    scaled = dnormed_one * gain_one
    projection = jnp.mean(scaled * x, axis=1, keepdims=True)
    dx = dmiddle + inverse_one * scaled - x * (inverse_one**3 * projection)
    gain_one_part = jnp.sum(dnormed_one * x * inverse_one, axis=0)

    heads_own = w_query.shape[1]

    def scatter_four(parts):
        return scatter_col(*parts).astype(BF16)

    out_part = t_dot(ctx, dattn, BF16)
    out_mine = scatter_four([out_part[i * heads_own : (i + 1) * heads_own] for i in range(4)])
    out_total = total_over_dp(cols_from_row(out_mine))
    query_part = t_dot(normed_one, dq, BF16)
    query_mine = scatter_four([query_part[:, i * heads_own : (i + 1) * heads_own] for i in range(4)])
    query_total = total_over_dp(rows_from_row(query_mine))
    kv_part = t_dot(normed_one, dkv)
    kv_mine = rows_from_row(kv_part)
    gain_parts = jnp.stack([gain_one_part, gain_two_part], axis=1)
    gain_mine = rows_from_row(gain_parts)
    kv_total, gain_total = lax.psum((kv_mine, gain_mine), ("dp", "col"))

    ffn_own = scatter_col(*blocks(ffn))
    y = middle + ffn_own

    def put_back(value):
        other = swap_row(value[:, feats:].astype(BF16)).astype(F32)
        own = value[:, :feats]
        return jnp.concatenate(
            [jnp.where(is_low, own, other), jnp.where(is_low, other, own)], axis=0
        )

    return (
        put_back(y),
        put_back(dx),
        query_total,
        kv_total,
        out_total,
        gate_total,
        up_total,
        down_total,
        gain_total[:, 0],
        gain_total[:, 1],
    )


def solution(mesh):
    return jax.shard_map(
        per_device,
        mesh=mesh,
        in_specs=(
            P(("dp", "col"), "row"),
            P("row"),
            P("row", "col"),
            P("row", None),
            P("col", "row"),
            P("row"),
            P("row", "col"),
            P("row", "col"),
            P("col", "row"),
            P(("dp", "row"), None),
            P(("dp", "col"), "row"),
        ),
        out_specs=(
            P(("dp", "col"), "row"),
            P(("dp", "col"), "row"),
            P("row", "col"),
            P("row", None),
            P("col", "row"),
            P("row", "col"),
            P("row", "col"),
            P("col", "row"),
            P("row"),
            P("row"),
        ),
        check_vma=False,
    )
```

time: 2550 us -> 841 us (0.33)
  waiting for transfers between devices: 1900 us -> 329 us
  matrix products: 330 us -> 110 us
  starting transfers between devices: 1.54 us -> 116 us
  Pallas kernels: 0 us -> 64.4 us
  other arithmetic: 153 us -> 95.2 us
    reduce_scatter x8 -> x0, waiting for transfers between devices: 1150 us -> none  [the longest x2 538 us: project_in(): lax.psum_scatter(partial_term(jnp.int32(0), gathered.shape[0] // lax.axis...]
    all_gather x8 -> x0, waiting for transfers between devices: 455 us -> none  [the longest x2 253 us: grad_from_in(): grad_full = lax.all_gather(grad_local, 'row', axis=0, tiled=True)]
    ppermute x0 -> x62, waiting for transfers between devices: none -> 329 us  [the longest x21 132 us: swap_row(): return lax.ppermute(value, 'row', [(0, 1), (1, 0)])]
    psum x2 -> x1, waiting for transfers between devices: 293 us -> 0.01 us  [per_device(): kv_total, gain_total = lax.psum((kv_mine, gain_mine), ('dp', 'col'))]
    dot_general x40 -> x15, matrix products: 330 us -> 110 us  [the longest x6 50.8 us: t_dot(): lax.dot_general(left, right, (((0,), (0,)), ((), ())), preferred_element_...]
    ppermute x0 -> x62, starting transfers between devices: none -> 116 us  [the longest x21 38.9 us: swap_row(): return lax.ppermute(value, 'row', [(0, 1), (1, 0)])]
    pallas_call x0 -> x3, Pallas kernels: none -> 64.4 us  [the longest x1 37.2 us: feed(): pl.pallas_call(feed_kernel, grid=(units // tn, rows // tm), in_specs=[pl....]
    reduce_sum x8 -> x2, other arithmetic: 40.5 us -> 1.7 us  [the longest x1 1.32 us: per_device(): gain_two_part = jnp.sum(dnormed_two * middle * inverse_two, axis=0)]
  transfers between devices with their start and end apart: 18 -> 63, of which waited for: 17 -> 23; matrix products, arithmetic and copies ran while one was open for 13% -> 26% of each run, Pallas kernels for 0% -> 3%
where the time goes in v1:
time: 841 us; the launch traced here: 834 us
  waiting for transfers between devices  329 us (39%)
  starting transfers between devices  116 us (14%)
  matrix products  110 us (13%)
  other arithmetic  95.2 us (11%)
  Pallas kernels  64.4 us (8%)
  blocking collectives  52.4 us (6%)
  local copies, waits for them, and re-layouts  51.4 us (6%)
  between operations  15.5 us (2%)
    ppermute x21, waiting for transfers between devices, swap_row(): return lax.ppermute(value, 'row', [(0, 1), (1, 0)])  132 us
    ppermute x8, waiting for transfers between devices, swap_far(): return lax.ppermute(value, 'col', [(0, 2), (2, 0), (1, 3), (3, 1)])  80.3 us
    ppermute x5, waiting for transfers between devices, total_over_dp(): back = lax.ppermute(both, 'dp', [(1, 0), (2, 3)])  64.4 us
    psum x1, blocking collectives, per_device(): kv_total, gain_total = lax.psum((kv_mine, gain_mine), ('dp', 'col'))  52.4 us
    ppermute x5, waiting for transfers between devices, total_over_dp(): inward = lax.ppermute(part, 'dp', [(0, 1), (3, 2)])  51.6 us
    dot_general x6, matrix products, t_dot(): lax.dot_general(left, right, (((0,), (0,)), ((), ())), preferred_element_...  50.8 us
    ppermute x21, starting transfers between devices, swap_row(): return lax.ppermute(value, 'row', [(0, 1), (1, 0)])  38.9 us
    pallas_call x1, Pallas kernels, feed(): pl.pallas_call(feed_kernel, grid=(units // tn, rows // tm), in_specs=[pl....  37.2 us
  transfers between devices with their start and end apart: 63, of which 23 were waited for; matrix products, arithmetic and copies ran while one was open for 26% of the time, Pallas kernels for 3%

profile of v1, /device:TPU:0, one launch (start us, length us, event | category | flops | bytes accessed | tf_op | source)
XLA Modules:
  0.0 834.4 jit_solution(8985365173726386616)
XLA Ops:
  25.7 11.6 %collective-permute-done.2 = bf16[768,384]{1,0:T(8,128)(2,1)} collective-permute-done((bf16[768,384]{1,0:T(8,128)(2,1)}, bf16[768,384]{1,0:T(8,128)(2,1)}, u32[]{:S(2)}, u32[]{:S(2)}) %collective-permute-start.2) | collective-permute-done | bytes 589856 | tf_op jit(solution)/shard_map/ppermute | solution.py:26
  39.2 14.9 %collective-permute-done = bf16[512,768]{1,0:T(8,128)(2,1)S(1)} collective-permute-done((bf16[512,768]{1,0:T(8,128)(2,1)}, bf16[512,768]{1,0:T(8,128)(2,1)S(1)}, u32[]{:S(2)}, u32[]{:S(2)}) %collective-permute-start) | collective-permute-done | bytes 786464 | tf_op jit(solution)/shard_map/ppermute | solution.py:26
  61.3 9.6 %collective-permute-done.7 = bf16[512,256]{1,0:T(8,128)(2,1)S(1)} collective-permute-done((bf16[512,256]{1,0:T(8,128)(2,1)S(1)}, bf16[512,256]{1,0:T(8,128)(2,1)S(1)}, u32[]{:S(2)}, u32[]{:S(2)}) %collective-permute-start.7) | collective-permute-done | bytes 262176 | tf_op jit(solution)/shard_map/ppermute | solution.py:26
  78.4 10.6 %collective-permute-done.4 = bf16[1536,384]{1,0:T(8,128)(2,1)} collective-permute-done((bf16[1536,384]{1,0:T(8,128)(2,1)}, bf16[1536,384]{1,0:T(8,128)(2,1)}, u32[]{:S(2)}, u32[]{:S(2)}) %collective-permute-start.4) | collective-permute-done | bytes 1179680 | tf_op jit(solution)/shard_map/ppermute | solution.py:34
  96.2 18.0 %collective-permute-done.12 = bf16[384,1536]{1,0:T(8,128)(2,1)} collective-permute-done((bf16[384,1536]{1,0:T(8,128)(2,1)S(1)}, bf16[384,1536]{1,0:T(8,128)(2,1)}, u32[]{:S(2)}, u32[]{:S(2)}) %collective-permute-start.12) | collective-permute-done | bytes 1179680 | tf_op jit(solution)/shard_map/ppermute | solution.py:34
  119.4 6.4 convolution_convert_fusion.7.q
  125.8 8.6 %attend_forward.1 = (bf16[512,1536]{1,0:T(8,128)(2,1)}, f32[512,128]{1,0:T(8,128)}) custom-call(s32[1]{0:T(128)} %bitcast.start, bf16[512,1536]{1,0:T(8,128)(2,1)} %convolution_convert_fusion.7.q, bf16[2048,256]{1,0:T(8,128)(2,1)} %pad_maximum_fusion.8.kv, s32[512,1]{1,0:T(8,128)} %copy.21.seg_q, s32[1,2048]{1,0:T(1,128)} %fusion.9.seg_k), custom_call_target="tpu_custom_call" | custom-call | tf_op jit(solution)/shard_map/attend_forward/pallas_call | solution.py:148
  156.6 17.9 %collective-permute-done.15 = bf16[512,1536]{1,0:T(8,128)(2,1)} collective-permute-done((bf16[512,1536]{1,0:T(8,128)(2,1)}, bf16[512,1536]{1,0:T(8,128)(2,1)}, u32[]{:S(2)}, u32[]{:S(2)}) %collective-permute-start.15) | collective-permute-done | bytes 1572896 | tf_op jit(solution)/shard_map/ppermute | solution.py:34
  189.5 8.6 %pad_maximum_fusion.1.dy = bf16[2048,1536]{1,0:T(8,128)(2,1)} fusion(bf16[512,1536]{1,0:T(8,128)(2,1)} %collective-permute-done.20, bf16[512,1536]{1,0:T(8,128)(2,1)} %collective-permute-done.19, bf16[512,1536]{1,0:T(8,128)(2,1)} %collective-permute-done.18, bf16[512,768]{1,0:T(8,128)(2,1)S(1)} %copy-done.11, bf16[512,768]{1,0:T(8,128)(2,1)S(1)} %copy-done.1), kind=kLoop, calls=%fused_computation.14 | loop fusion | flops 31457280 | bytes 12582912 | tf_op jit(solution)/shard_map/concatenate | solution.py:372
  199.9 7.6 pad_maximum_fusion.n2
  207.5 20.6 %collective-permute-done.23 = bf16[1152,768]{1,0:T(8,128)(2,1)S(1)} collective-permute-done((bf16[1152,768]{1,0:T(8,128)(2,1)S(1)}, bf16[1152,768]{1,0:T(8,128)(2,1)S(1)}, u32[]{:S(2)}, u32[]{:S(2)}) %collective-permute-start.23) | collective-permute-done | bytes 1769504 | tf_op jit(solution)/shard_map/ppermute | solution.py:26
  229.4 37.2 %feed.1 = (bf16[2048,1152]{1,0:T(8,128)(2,1)}, bf16[2048,1152]{1,0:T(8,128)(2,1)}, bf16[2048,1152]{1,0:T(8,128)(2,1)}) custom-call(bf16[2048,1536]{1,0:T(8,128)(2,1)} %pad_maximum_fusion.n2, bf16[2048,1536]{1,0:T(8,128)(2,1)} %pad_maximum_fusion.1.dy, bf16[1536,1152]{1,0:T(8,128)(2,1)} %constant_dynamic-update-slice_fusion.8.wg, ...), custom_call_target="tpu_custom_call" | custom-call | tf_op jit(solution)/shard_map/feed/pallas_call | solution.py:271
  266.6 11.6 %convolution_convert_fusion.5 = bf16[2048,1536]{1,0:T(8,128)(2,1)S(1)} fusion(bf16[2048,1152]{1,0:T(8,128)(2,1)} %get-tuple-element.30, bf16[1152,1536]{1,0:T(8,128)(2,1)} %constant_dynamic-update-slice_fusion.12.wd), kind=kOutput, calls=%fused_computation.6 | convolution fusion | flops 7250903040 | bytes 14548992 | tf_op jit(solution)/shard_map/dot_general | solution.py:38
  278.2 15.7 %convolution_convert_fusion = bf16[1152,1536]{1,0:T(8,128)(2,1)S(1)} fusion(bf16[2048,1152]{1,0:T(8,128)(2,1)} %get-tuple-element.30, bf16[512,1536]{1,0:T(8,128)(2,1)} %collective-permute-done.20, bf16[512,1536]{1,0:T(8,128)(2,1)} %collective-permute-done.19, bf16[512,1536]{1,0:T(8,128)(2,1)} %collective-permute-done.18, ...), kind=kOutput, calls=%fused_computation.1 | convolution fusion | flops 7280984064 | bytes 14548992 | tf_op jit(solution)/shard_map/dot_general | solution.py:48
  301.3 11.2 %fusion.25 = f32[2048,1536]{1,0:T(8,128)} fusion(bf16[2048,1152]{1,0:T(8,128)(2,1)S(1)} %bitcast.29, bf16[1536,1152]{1,0:T(8,128)(2,1)S(1)} %copy-done.5), kind=kOutput, calls=%fused_computation.124 | convolution fusion | flops 7247757312 | bytes 20840448 | tf_op jit(solution)/shard_map/dot_general | solution.py:42
  312.4 14.0 %add_convert_fusion = bf16[2048,1536]{1,0:T(8,128)(2,1)S(1)} fusion(f32[2048,1536]{1,0:T(8,128)} %fusion.25, bf16[2048,1152]{1,0:T(8,128)(2,1)} %get-tuple-element.31, bf16[1536,1152]{1,0:T(8,128)(2,1)} %constant_dynamic-update-slice_fusion.8.wg), kind=kOutput, calls=%fused_computation | convolution fusion | flops 7254048768 | bytes 27131904 | tf_op jit(solution)/shard_map/dot_general | solution.py:42
  328.4 13.3 %convolution_convert_fusion.2 = bf16[1536,1152]{1,0:T(8,128)(2,1)} fusion(bf16[2048,1152]{1,0:T(8,128)(2,1)} %get-tuple-element.31, bf16[512,1536]{1,0:T(8,128)(2,1)} %collective-permute-done.16, bf16[512,1536]{1,0:T(8,128)(2,1)} %collective-permute-done.15, bf16[512,1536]{1,0:T(8,128)(2,1)} %collective-permute-done.14, ...), kind=kOutput, calls=%fused_computation.3 | convolution fusion | flops 7274692608 | bytes 14548992 | tf_op jit(solution)/shard_map/dot_general | solution.py:48
  341.6 12.2 %convolution_convert_fusion.1 = bf16[1536,1152]{1,0:T(8,128)(2,1)S(1)} fusion(bf16[2048,1152]{1,0:T(8,128)(2,1)} %get-tuple-element.32, bf16[512,1536]{1,0:T(8,128)(2,1)} %collective-permute-done.16, bf16[512,1536]{1,0:T(8,128)(2,1)} %collective-permute-done.15, bf16[512,1536]{1,0:T(8,128)(2,1)} %collective-permute-done.14, ...), kind=kOutput, calls=%fused_computation.2 | convolution fusion | flops 7274692608 | bytes 14548992 | tf_op jit(solution)/shard_map/dot_general | solution.py:48
  367.7 31.0 %collective-permute-done.49 = bf16[768,1152]{1,0:T(8,128)(2,1)S(1)} collective-permute-done((bf16[768,1152]{1,0:T(8,128)(2,1)S(1)}, bf16[768,1152]{1,0:T(8,128)(2,1)S(1)}, u32[]{:S(2)}, u32[]{:S(2)}) %collective-permute-start.49) | collective-permute-done | bytes 1769504 | tf_op jit(solution)/shard_map/ppermute | solution.py:26
  401.7 34.5 %collective-permute-done.53 = bf16[768,1152]{1,0:T(8,128)(2,1)S(1)} collective-permute-done((bf16[768,1152]{1,0:T(8,128)(2,1)S(1)}, bf16[768,1152]{1,0:T(8,128)(2,1)S(1)}, u32[]{:S(2)}, u32[]{:S(2)}) %collective-permute-start.53) | collective-permute-done | bytes 1769504 | tf_op jit(solution)/shard_map/ppermute | solution.py:26
  461.3 18.7 %attend_backward.1 = (bf16[512,1536]{1,0:T(8,128)(2,1)}, f32[2048,256]{1,0:T(8,128)}) custom-call(s32[1]{0:T(128)} %bitcast.start, bf16[512,1536]{1,0:T(8,128)(2,1)} %convolution_convert_fusion.7.q, bf16[2048,256]{1,0:T(8,128)(2,1)} %pad_maximum_fusion.8.kv, s32[512,1]{1,0:T(8,128)} %copy.21.seg_q, s32[1,2048]{1,0:T(1,128)} %fusion.9.seg_k, ...), custom_call_target="tpu_custom_call" | custom-call | tf_op jit(solution)/shard_map/attend_backward/pallas_call | solution.py:224
  481.8 8.7 %collective-permute-start.31 = (bf16[1024,256]{1,0:T(8,128)(2,1)S(1)}, bf16[1024,256]{1,0:T(8,128)(2,1)S(1)}, u32[]{:S(2)}, u32[]{:S(2)}) collective-permute-start(bf16[1024,256]{1,0:T(8,128)(2,1)S(1)} %select_convert_fusion.3), channel_id=1, source_target_pairs={{0,1},{1,0},{2,3},{3,2},{4,5},{5,4},{6,7},{7,6},{8,9},{9,8},{10,11... | collective-permute-start | bytes 1572872 | tf_op jit(solution)/shard_map/ppermute | solution.py:30
  497.8 9.9 %collective-permute-start.32 = (bf16[512,256]{1,0:T(8,128)(2,1)S(1)}, bf16[512,256]{1,0:T(8,128)(2,1)S(1)}, u32[]{:S(2)}, u32[]{:S(2)}) collective-permute-start(bf16[512,256]{1,0:T(8,128)(2,1)S(1)} %dynamic-slice_convert_fusion), channel_id=1, source_target_pairs={{0,4},{4,0},{1,5},{5,1},{2,6},{6,2},{3,7},{7,3},{8,12},{12,8},{9,1... | collective-permute-start | bytes 786440 | tf_op jit(solution)/shard_map/ppermute | solution.py:26
  518.6 34.2 %collective-permute-done.54 = bf16[768,1152]{1,0:T(8,128)(2,1)} collective-permute-done((bf16[768,1152]{1,0:T(8,128)(2,1)}, bf16[768,1152]{1,0:T(8,128)(2,1)}, u32[]{:S(2)}, u32[]{:S(2)}) %collective-permute-start.54) | collective-permute-done | bytes 1769504 | tf_op jit(solution)/shard_map/ppermute | solution.py:58
  585.6 14.0 %collective-permute-done.36 = bf16[1536,384]{1,0:T(8,128)(2,1)S(1)} collective-permute-done((bf16[1536,384]{1,0:T(8,128)(2,1)S(1)}, bf16[1536,384]{1,0:T(8,128)(2,1)S(1)}, u32[]{:S(2)}, u32[]{:S(2)}) %collective-permute-start.36) | collective-permute-done | bytes 1179680 | tf_op jit(solution)/shard_map/ppermute | solution.py:34
  604.2 19.7 %collective-permute-done.44 = bf16[384,1536]{1,0:T(8,128)(2,1)S(1)} collective-permute-done((bf16[384,1536]{1,0:T(8,128)(2,1)S(1)}, bf16[384,1536]{1,0:T(8,128)(2,1)S(1)}, u32[]{:S(2)}, u32[]{:S(2)}) %collective-permute-start.44) | collective-permute-done | bytes 1179680 | tf_op jit(solution)/shard_map/ppermute | solution.py:34
  628.6 52.4 %psum.15 = f32[768,2]{0,1:T(2,128)S(1)} all-reduce(f32[768,2]{0,1:T(2,128)S(1)} %fusion.11), channel_id=1, replica_groups=mesh['dp'=4,'row'=2,'col'=4] {'dp','col'}, use_global_device_ids=true, to_apply=%region_7.8 | all-reduce | flops 1536 | bytes 12288 | tf_op jit(solution)/shard_map/psum | solution.py:434
  692.0 23.9 %collective-permute-start.38 = (bf16[768,384]{1,0:T(8,128)(2,1)}, bf16[768,384]{1,0:T(8,128)(2,1)}, u32[]{:S(2)}, u32[]{:S(2)}) collective-permute-start(bf16[768,384]{1,0:T(8,128)(2,1)} %slice_add_fusion.5), channel_id=1, source_target_pairs={{0,8},{24,16},{1,9},{25,17},{2,10},{26,18},{3,11},{27,19},{4,12},{... | collective-permute-start | bytes 1769480 | tf_op jit(solution)/shard_map/ppermute | solution.py:58
  732.0 12.4 %collective-permute-done.46 = bf16[384,768]{1,0:T(8,128)(2,1)} collective-permute-done((bf16[384,768]{1,0:T(8,128)(2,1)}, bf16[384,768]{1,0:T(8,128)(2,1)}, u32[]{:S(2)}, u32[]{:S(2)}) %collective-permute-start.46) | collective-permute-done | bytes 589856 | tf_op jit(solution)/shard_map/ppermute | solution.py:58
  761.1 33.5 %collective-permute-done.56 = bf16[768,1152]{1,0:T(8,128)(2,1)S(1)} collective-permute-done((bf16[768,1152]{1,0:T(8,128)(2,1)S(1)}, bf16[768,1152]{1,0:T(8,128)(2,1)S(1)}, u32[]{:S(2)}, u32[]{:S(2)}) %collective-permute-start.56) | collective-permute-done | bytes 1769504 | tf_op jit(solution)/shard_map/ppermute | solution.py:62
  796.7 14.3 %collective-permute-done.40 = bf16[768,384]{1,0:T(8,128)(2,1)S(1)} collective-permute-done((bf16[768,384]{1,0:T(8,128)(2,1)S(1)}, bf16[768,384]{1,0:T(8,128)(2,1)S(1)}, u32[]{:S(2)}, u32[]{:S(2)}) %collective-permute-start.40) | collective-permute-done | bytes 589856 | tf_op jit(solution)/shard_map/ppermute | solution.py:62
  812.1 11.9 %collective-permute-done.48 = bf16[384,768]{1,0:T(8,128)(2,1)S(1)} collective-permute-done((bf16[384,768]{1,0:T(8,128)(2,1)S(1)}, bf16[384,768]{1,0:T(8,128)(2,1)S(1)}, u32[]{:S(2)}, u32[]{:S(2)}) %collective-permute-start.48) | collective-permute-done | bytes 589856 | tf_op jit(solution)/shard_map/ppermute | solution.py:62
  (346 shorter events, 250.3 us)
Async XLA Ops:
  7.2 817.8 %all-reduce.2.cloned.1.call-start = ((), (), s32[]{:S(2)}) async-start(), calls=%async_computation | async-start | bytes 1572864 | tf_op jit(solution)/shard_map/psum | solution.py:434
  12.2 44.9 %collective-permute-start.9 = (s32[1,2048]{1,0:T(1,128)}, s32[1,2048]{1,0:T(1,128)}, u32[]{:S(2)}, u32[]{:S(2)}) collective-permute-start(s32[1,2048]{1,0:T(1,128)} %param.20), channel_id=1, source_target_pairs={{0,4},{4,0},{1,5},{5,1},{2,6},{6,2},{3,7},{7,3},{8,12},{12,8},{9,1... | collective-permute-start | bytes 24584 | tf_op jit(solution)/shard_map/ppermute | solution.py:26
  72.0 42.3 %collective-permute-start.12 = (bf16[384,1536]{1,0:T(8,128)(2,1)S(1)}, bf16[384,1536]{1,0:T(8,128)(2,1)}, u32[]{:S(2)}, u32[]{:S(2)}) collective-permute-start(bf16[384,1536]{1,0:T(8,128)(2,1)S(1)} %pad_maximum_fusion.7), channel_id=1, source_target_pairs={{0,2},{2,0},{1,3},{3,1},{4,6},{6,4},{5,7},{7,5},{8,10},{10,8},{9,1... | collective-permute-start | bytes 3538952 | tf_op jit(solution)/shard_map/ppermute | solution.py:34
  95.8 56.1 %collective-permute-start.19 = (bf16[512,1536]{1,0:T(8,128)(2,1)}, bf16[512,1536]{1,0:T(8,128)(2,1)}, u32[]{:S(2)}, u32[]{:S(2)}) collective-permute-start(bf16[512,1536]{1,0:T(8,128)(2,1)} %pad_maximum_fusion.6), channel_id=1, source_target_pairs={{0,2},{2,0},{1,3},{3,1},{4,6},{6,4},{5,7},{7,5},{8,10},{10,8},{9,1... | collective-permute-start | bytes 4718600 | tf_op jit(solution)/shard_map/ppermute | solution.py:34
  145.6 41.4 %collective-permute-start.22 = (bf16[768,1152]{1,0:T(8,128)(2,1)}, bf16[768,1152]{1,0:T(8,128)(2,1)}, u32[]{:S(2)}, u32[]{:S(2)}) collective-permute-start(bf16[768,1152]{1,0:T(8,128)(2,1)} %param.18), channel_id=1, source_target_pairs={{0,4},{4,0},{1,5},{5,1},{2,6},{6,2},{3,7},{7,3},{8,12},{12,8},{9,1... | collective-permute-start | bytes 5308424 | tf_op jit(solution)/shard_map/ppermute | solution.py:26
  156.1 43.7 %collective-permute-start.14 = (bf16[512,1536]{1,0:T(8,128)(2,1)}, bf16[512,1536]{1,0:T(8,128)(2,1)}, u32[]{:S(2)}, u32[]{:S(2)}) collective-permute-start(bf16[512,1536]{1,0:T(8,128)(2,1)} %multiply_convert_fusion), channel_id=1, source_target_pairs={{0,1},{1,0},{2,3},{3,2},{4,5},{5,4},{6,7},{7,6},{8,9},{9,8},{10,11... | collective-permute-start | bytes 4718600 | tf_op jit(solution)/shard_map/ppermute | solution.py:30
  297.0 66.3 %collective-permute-start.57 = (bf16[1152,768]{1,0:T(8,128)(2,1)}, bf16[1152,768]{1,0:T(8,128)(2,1)}, u32[]{:S(2)}, u32[]{:S(2)}) collective-permute-start(bf16[1152,768]{1,0:T(8,128)(2,1)} %slice.195), channel_id=1, source_target_pairs={{0,4},{4,0},{1,5},{5,1},{2,6},{6,2},{3,7},{7,3},{8,12},{12,8},{9,1... | collective-permute-start | bytes 5308424 | tf_op jit(solution)/shard_map/ppermute | solution.py:26
  300.7 147.2 %collective-permute-start.24 = (bf16[512,1536]{1,0:T(8,128)(2,1)}, bf16[512,1536]{1,0:T(8,128)(2,1)}, u32[]{:S(2)}, u32[]{:S(2)}) collective-permute-start(bf16[512,1536]{1,0:T(8,128)(2,1)} %get-tuple-element.46), channel_id=1, source_target_pairs={{0,1},{1,0},{2,3},{3,2},{4,5},{5,4},{6,7},{7,6},{8,9},{9,8},{10,11... | collective-permute-start | bytes 4718600 | tf_op jit(solution)/shard_map/ppermute | solution.py:30
  300.8 57.5 %collective-permute-start.25 = (bf16[512,1536]{1,0:T(8,128)(2,1)S(1)}, bf16[512,1536]{1,0:T(8,128)(2,1)}, u32[]{:S(2)}, u32[]{:S(2)}) collective-permute-start(bf16[512,1536]{1,0:T(8,128)(2,1)S(1)} %get-tuple-element.47), channel_id=1, source_target_pairs={{0,1},{1,0},{2,3},{3,2},{4,5},{5,4},{6,7},{7,6},{8,9},{9,8},{10,11... | collective-permute-start | bytes 4718600 | tf_op jit(solution)/shard_map/ppermute | solution.py:30
  357.3 41.5 %collective-permute-start.49 = (bf16[768,1152]{1,0:T(8,128)(2,1)S(1)}, bf16[768,1152]{1,0:T(8,128)(2,1)S(1)}, u32[]{:S(2)}, u32[]{:S(2)}) collective-permute-start(bf16[768,1152]{1,0:T(8,128)(2,1)S(1)} %slice.191), channel_id=1, source_target_pairs={{0,4},{4,0},{1,5},{5,1},{2,6},{6,2},{3,7},{7,3},{8,12},{12,8},{9,1... | collective-permute-start | bytes 5308424 | tf_op jit(solution)/shard_map/ppermute | solution.py:26
  358.3 77.9 %collective-permute-start.53 = (bf16[768,1152]{1,0:T(8,128)(2,1)S(1)}, bf16[768,1152]{1,0:T(8,128)(2,1)S(1)}, u32[]{:S(2)}, u32[]{:S(2)}) collective-permute-start(bf16[768,1152]{1,0:T(8,128)(2,1)S(1)} %slice.193), channel_id=1, source_target_pairs={{0,4},{4,0},{1,5},{5,1},{2,6},{6,2},{3,7},{7,3},{8,12},{12,8},{9,1... | collective-permute-start | bytes 5308424 | tf_op jit(solution)/shard_map/ppermute | solution.py:26
  361.2 80.3 %collective-permute-start.28 = (bf16[512,1536]{1,0:T(8,128)(2,1)S(1)}, bf16[512,1536]{1,0:T(8,128)(2,1)S(1)}, u32[]{:S(2)}, u32[]{:S(2)}) collective-permute-start(bf16[512,1536]{1,0:T(8,128)(2,1)S(1)} %copy-done.40), channel_id=1, source_target_pairs={{0,1},{1,0},{2,3},{3,2},{4,5},{5,4},{6,7},{7,6},{8,9},{9,8},{10,11... | collective-permute-start | bytes 4718600 | tf_op jit(solution)/shard_map/ppermute | solution.py:30
  363.3 80.8 %collective-permute-start.30 = (bf16[512,1536]{1,0:T(8,128)(2,1)S(1)}, bf16[512,1536]{1,0:T(8,128)(2,1)S(1)}, u32[]{:S(2)}, u32[]{:S(2)}) collective-permute-start(bf16[512,1536]{1,0:T(8,128)(2,1)S(1)} %add_convert_fusion.1), channel_id=1, source_target_pairs={{0,2},{2,0},{1,3},{3,1},{4,6},{6,4},{5,7},{7,5},{8,10},{10,8},{9,1... | collective-permute-start | bytes 4718600 | tf_op jit(solution)/shard_map/ppermute | solution.py:34
  398.8 49.1 %collective-permute-start.26 = (bf16[512,1536]{1,0:T(8,128)(2,1)S(1)}, bf16[512,1536]{1,0:T(8,128)(2,1)}, u32[]{:S(2)}, u32[]{:S(2)}) collective-permute-start(bf16[512,1536]{1,0:T(8,128)(2,1)S(1)} %add_convert_fusion.2), channel_id=1, source_target_pairs={{0,2},{2,0},{1,3},{3,1},{4,6},{6,4},{5,7},{7,5},{8,10},{10,8},{9,1... | collective-permute-start | bytes 4718600 | tf_op jit(solution)/shard_map/ppermute | solution.py:34
  436.2 75.1 %collective-permute-start.58 = (bf16[1152,768]{1,0:T(8,128)(2,1)}, bf16[1152,768]{1,0:T(8,128)(2,1)}, u32[]{:S(2)}, u32[]{:S(2)}) collective-permute-start(bf16[1152,768]{1,0:T(8,128)(2,1)} %slice_add_fusion), channel_id=1, source_target_pairs={{0,8},{24,16},{1,9},{25,17},{2,10},{26,18},{3,11},{27,19},{4,12},{... | collective-permute-start | bytes 5308424 | tf_op jit(solution)/shard_map/ppermute | solution.py:58
  441.5 74.6 %collective-permute-start.50 = (bf16[768,1152]{1,0:T(8,128)(2,1)}, bf16[768,1152]{1,0:T(8,128)(2,1)}, u32[]{:S(2)}, u32[]{:S(2)}) collective-permute-start(bf16[768,1152]{1,0:T(8,128)(2,1)} %slice_add_fusion.2), channel_id=1, source_target_pairs={{0,8},{24,16},{1,9},{25,17},{2,10},{26,18},{3,11},{27,19},{4,12},{... | collective-permute-start | bytes 5308424 | tf_op jit(solution)/shard_map/ppermute | solution.py:58
  444.0 108.7 %collective-permute-start.54 = (bf16[768,1152]{1,0:T(8,128)(2,1)}, bf16[768,1152]{1,0:T(8,128)(2,1)}, u32[]{:S(2)}, u32[]{:S(2)}) collective-permute-start(bf16[768,1152]{1,0:T(8,128)(2,1)} %slice_add_fusion.1), channel_id=1, source_target_pairs={{0,8},{24,16},{1,9},{25,17},{2,10},{26,18},{3,11},{27,19},{4,12},{... | collective-permute-start | bytes 5308424 | tf_op jit(solution)/shard_map/ppermute | solution.py:58
  497.8 58.7 %collective-permute-start.32 = (bf16[512,256]{1,0:T(8,128)(2,1)S(1)}, bf16[512,256]{1,0:T(8,128)(2,1)S(1)}, u32[]{:S(2)}, u32[]{:S(2)}) collective-permute-start(bf16[512,256]{1,0:T(8,128)(2,1)S(1)} %dynamic-slice_convert_fusion), channel_id=1, source_target_pairs={{0,4},{4,0},{1,5},{5,1},{2,6},{6,2},{3,7},{7,3},{8,12},{12,8},{9,1... | collective-permute-start | bytes 786440 | tf_op jit(solution)/shard_map/ppermute | solution.py:26
  510.2 62.7 %collective-permute-start.27 = (bf16[512,768]{1,0:T(8,128)(2,1)}, bf16[512,768]{1,0:T(8,128)(2,1)}, u32[]{:S(2)}, u32[]{:S(2)}) collective-permute-start(bf16[512,768]{1,0:T(8,128)(2,1)} %slice.243), channel_id=1, source_target_pairs={{0,4},{4,0},{1,5},{5,1},{2,6},{6,2},{3,7},{7,3},{8,12},{12,8},{9,1... | collective-permute-start | bytes 2359304 | tf_op jit(solution)/shard_map/ppermute | solution.py:26
  511.3 72.3 %collective-permute-start.34 = (bf16[1536,384]{1,0:T(8,128)(2,1)}, bf16[1536,384]{1,0:T(8,128)(2,1)}, u32[]{:S(2)}, u32[]{:S(2)}) collective-permute-start(bf16[1536,384]{1,0:T(8,128)(2,1)} %get-tuple-element.50), channel_id=1, source_target_pairs={{0,1},{1,0},{2,3},{3,2},{4,5},{5,4},{6,7},{7,6},{8,9},{9,8},{10,11... | collective-permute-start | bytes 3538952 | tf_op jit(solution)/shard_map/ppermute | solution.py:30
  516.1 52.4 %collective-permute-start.35 = (bf16[1536,384]{1,0:T(8,128)(2,1)}, bf16[1536,384]{1,0:T(8,128)(2,1)}, u32[]{:S(2)}, u32[]{:S(2)}) collective-permute-start(bf16[1536,384]{1,0:T(8,128)(2,1)} %get-tuple-element.51), channel_id=1, source_target_pairs={{0,1},{1,0},{2,3},{3,2},{4,5},{5,4},{6,7},{7,6},{8,9},{9,8},{10,11... | collective-permute-start | bytes 3538952 | tf_op jit(solution)/shard_map/ppermute | solution.py:30
  573.0 51.0 %collective-permute-start.44 = (bf16[384,1536]{1,0:T(8,128)(2,1)S(1)}, bf16[384,1536]{1,0:T(8,128)(2,1)S(1)}, u32[]{:S(2)}, u32[]{:S(2)}) collective-permute-start(bf16[384,1536]{1,0:T(8,128)(2,1)S(1)} %add_convert_fusion.4), channel_id=1, source_target_pairs={{0,2},{2,0},{1,3},{3,1},{4,6},{6,4},{5,7},{7,5},{8,10},{10,8},{9,1... | collective-permute-start | bytes 3538952 | tf_op jit(solution)/shard_map/ppermute | solution.py:34
  576.4 51.0 %collective-permute-start.51 = (bf16[768,1152]{1,0:T(8,128)(2,1)S(1)}, bf16[768,1152]{1,0:T(8,128)(2,1)S(1)}, u32[]{:S(2)}, u32[]{:S(2)}) collective-permute-start(bf16[768,1152]{1,0:T(8,128)(2,1)S(1)} %add.199), channel_id=1, source_target_pairs={{8,16},{16,8},{9,17},{17,9},{10,18},{18,10},{11,19},{19,11},{12,20... | collective-permute-start | bytes 5308424 | tf_op jit(solution)/shard_map/ppermute | solution.py:60
  583.6 132.4 %collective-permute-start.55 = (bf16[768,1152]{1,0:T(8,128)(2,1)}, bf16[768,1152]{1,0:T(8,128)(2,1)}, u32[]{:S(2)}, u32[]{:S(2)}) collective-permute-start(bf16[768,1152]{1,0:T(8,128)(2,1)} %add.202), channel_id=1, source_target_pairs={{8,16},{16,8},{9,17},{17,9},{10,18},{18,10},{11,19},{19,11},{12,20... | collective-permute-start | bytes 5308424 | tf_op jit(solution)/shard_map/ppermute | solution.py:60
  603.0 143.5 %collective-permute-start.60 = (bf16[1152,768]{1,0:T(8,128)(2,1)}, bf16[1152,768]{1,0:T(8,128)(2,1)}, u32[]{:S(2)}, u32[]{:S(2)}) collective-permute-start(bf16[1152,768]{1,0:T(8,128)(2,1)} %add.206), channel_id=1, source_target_pairs={{8,0},{16,24},{9,1},{17,25},{10,2},{18,26},{11,3},{19,27},{12,4},{... | collective-permute-start | bytes 5308424 | tf_op jit(solution)/shard_map/ppermute | solution.py:62
  624.0 61.4 %collective-permute-start.37 = (bf16[768,384]{1,0:T(8,128)(2,1)}, bf16[768,384]{1,0:T(8,128)(2,1)}, u32[]{:S(2)}, u32[]{:S(2)}) collective-permute-start(bf16[768,384]{1,0:T(8,128)(2,1)} %slice.181), channel_id=1, source_target_pairs={{0,4},{4,0},{1,5},{5,1},{2,6},{6,2},{3,7},{7,3},{8,12},{12,8},{9,1... | collective-permute-start | bytes 1769480 | tf_op jit(solution)/shard_map/ppermute | solution.py:26
  625.9 66.1 %collective-permute-start.41 = (f32[768,256]{1,0:T(8,128)}, f32[768,256]{1,0:T(8,128)}, u32[]{:S(2)}, u32[]{:S(2)}) collective-permute-start(f32[768,256]{1,0:T(8,128)} %slice.183), channel_id=1, source_target_pairs={{0,4},{4,0},{1,5},{5,1},{2,6},{6,2},{3,7},{7,3},{8,12},{12,8},{9,1... | collective-permute-start | bytes 2359304 | tf_op jit(solution)/shard_map/ppermute | solution.py:26
  627.4 61.4 %collective-permute-start.45 = (bf16[384,768]{1,0:T(8,128)(2,1)}, bf16[384,768]{1,0:T(8,128)(2,1)}, u32[]{:S(2)}, u32[]{:S(2)}) collective-permute-start(bf16[384,768]{1,0:T(8,128)(2,1)} %slice.189), channel_id=1, source_target_pairs={{0,4},{4,0},{1,5},{5,1},{2,6},{6,2},{3,7},{7,3},{8,12},{12,8},{9,1... | collective-permute-start | bytes 1769480 | tf_op jit(solution)/shard_map/ppermute | solution.py:26
  688.8 66.0 %collective-permute-start.52 = (bf16[768,1152]{1,0:T(8,128)(2,1)}, bf16[768,1152]{1,0:T(8,128)(2,1)}, u32[]{:S(2)}, u32[]{:S(2)}) collective-permute-start(bf16[768,1152]{1,0:T(8,128)(2,1)} %add.200), channel_id=1, source_target_pairs={{8,0},{16,24},{9,1},{17,25},{10,2},{18,26},{11,3},{19,27},{12,4},{... | collective-permute-start | bytes 5308424 | tf_op jit(solution)/shard_map/ppermute | solution.py:62
  722.7 72.0 %collective-permute-start.56 = (bf16[768,1152]{1,0:T(8,128)(2,1)S(1)}, bf16[768,1152]{1,0:T(8,128)(2,1)S(1)}, u32[]{:S(2)}, u32[]{:S(2)}) collective-permute-start(bf16[768,1152]{1,0:T(8,128)(2,1)S(1)} %add.203), channel_id=1, source_target_pairs={{8,0},{16,24},{9,1},{17,25},{10,2},{18,26},{11,3},{19,27},{12,4},{... | collective-permute-start | bytes 5308424 | tf_op jit(solution)/shard_map/ppermute | solution.py:62
  758.4 52.6 %collective-permute-start.40 = (bf16[768,384]{1,0:T(8,128)(2,1)S(1)}, bf16[768,384]{1,0:T(8,128)(2,1)S(1)}, u32[]{:S(2)}, u32[]{:S(2)}) collective-permute-start(bf16[768,384]{1,0:T(8,128)(2,1)S(1)} %add.190), channel_id=1, source_target_pairs={{8,0},{16,24},{9,1},{17,25},{10,2},{18,26},{11,3},{19,27},{12,4},{... | collective-permute-start | bytes 1769480 | tf_op jit(solution)/shard_map/ppermute | solution.py:62
  759.8 64.1 %collective-permute-start.48 = (bf16[384,768]{1,0:T(8,128)(2,1)S(1)}, bf16[384,768]{1,0:T(8,128)(2,1)S(1)}, u32[]{:S(2)}, u32[]{:S(2)}) collective-permute-start(bf16[384,768]{1,0:T(8,128)(2,1)S(1)} %add.197), channel_id=1, source_target_pairs={{8,0},{16,24},{9,1},{17,25},{10,2},{18,26},{11,3},{19,27},{12,4},{... | collective-permute-start | bytes 1769480 | tf_op jit(solution)/shard_map/ppermute | solution.py:62
  (97 other events, 1992.2 us)
Sparse Core Ops, SparseCore 0:
  720.3 97.3 all-reduce.1

commit v2 on v1

v2 whole, which is shorter than its diff:
```python
import functools
import math

import jax
import jax.numpy as jnp
from jax import lax
from jax.experimental import pallas as pl
from jax.experimental.pallas import tpu as pltpu
from jax.sharding import PartitionSpec as P

D = 1536
HD = 128
WINDOW = 1024
EPSILON = 1e-06
NEGATIVE = -1e30
BF16 = jnp.bfloat16
F32 = jnp.float32
VMEM_BYTES = 56 * 1024 * 1024
HEAVY = pl.CostEstimate(flops=10**12, bytes_accessed=10**9, transcendentals=0)


def after(value, *earlier):
    return lax.optimization_barrier((value, *earlier))[0]


def swap_row(value):
    return lax.ppermute(value, "row", [(0, 1), (1, 0)])


def swap_core(value):
    return lax.ppermute(value, "col", [(0, 1), (1, 0), (2, 3), (3, 2)])


def swap_far(value):
    return lax.ppermute(value, "col", [(0, 2), (2, 0), (1, 3), (3, 1)])


def dot(left, right, out=F32):
    return jnp.dot(left, right, preferred_element_type=F32).astype(out)


def dot_t(left, right, out=F32):
    return lax.dot_general(
        left, right, (((1,), (1,)), ((), ())), preferred_element_type=F32
    ).astype(out)


def t_dot(left, right, out=F32):
    return lax.dot_general(
        left, right, (((0,), (0,)), ((), ())), preferred_element_type=F32
    ).astype(out)


def swap_pair(value):
    count = lax.axis_size("dp")
    return lax.ppermute(value, "dp", [(i, i ^ 1) for i in range(count)])


def swap_mirror(value):
    count = lax.axis_size("dp")
    return lax.ppermute(value, "dp", [(i, count - 1 - i) for i in range(count)])


class Steps:
    def __init__(self):
        self.last = ()

    def __call__(self, function, first, *rest):
        result = function(after(first, *self.last) if self.last else first, *rest)
        self.last = tuple(result) if isinstance(result, (tuple, list)) else (result,)
        return result


class DpTotal:
    def __init__(self, steps):
        self.steps = steps
        self.staged = lax.axis_size("dp") == 4
        self.side = (lax.axis_index("dp") + 1) // 2 % 2

    def begin(self, own, other):
        if not self.staged:
            self.value = lax.psum(own + other, "dp")
            return
        span = own.shape[0] // 2

        def both(other):
            def half(which):
                at = which * span
                return lax.dynamic_slice_in_dim(own, at, span, 0) + lax.dynamic_slice_in_dim(
                    other, at, span, 0
                )

            return half(1 - self.side), half(self.side)

        give, self.keep = self.steps(both, other)
        self.inward = swap_pair(give)

    def middle(self):
        if self.staged:
            self.pair = self.steps(jnp.add, self.inward, self.keep)
            self.across = swap_mirror(self.pair)

    def end(self):
        if self.staged:
            self.total = self.steps(jnp.add, self.across, self.pair)
            self.rest = swap_pair(self.total)

    def result(self):
        if not self.staged:
            return self.value.astype(F32)
        first = self.side == 0

        def join(rest):
            return jnp.concatenate(
                [jnp.where(first, self.total, rest), jnp.where(first, rest, self.total)], axis=0
            ).astype(F32)

        return self.steps(join, self.rest)


def fence_kernel(value, out):
    out[...] = value[...]


class Rounds:
    def __init__(self):
        self.token = jnp.zeros((8, 128), F32)

    def send(self, move, value):
        return move(after(value, self.token))

    def wait(self, *results):
        token = pl.pallas_call(
            fence_kernel,
            out_shape=jax.ShapeDtypeStruct((8, 128), F32),
            cost_estimate=HEAVY,
            name="fence",
        )(self.token)
        self.token = after(token, *results)


def place_kernel(odd, straight, around, out):
    is_straight = pl.program_id(0) == odd[0]

    @pl.when(is_straight)
    def _():
        out[...] = straight[...]

    @pl.when(jnp.logical_not(is_straight))
    def _():
        out[...] = around[...]


def place_rows(odd, straight, around):
    rows, cols = straight.shape
    whole = pl.BlockSpec((rows, cols), lambda i: (0, 0))
    return pl.pallas_call(
        place_kernel,
        grid=(2,),
        in_specs=[pl.BlockSpec(memory_space=pltpu.SMEM), whole, whole],
        out_specs=pl.BlockSpec((rows, cols), lambda i: (i, 0)),
        out_shape=jax.ShapeDtypeStruct((2 * rows, cols), straight.dtype),
        compiler_params=pltpu.CompilerParams(vmem_limit_bytes=VMEM_BYTES),
        cost_estimate=HEAVY,
        name="place_rows",
    )(jnp.reshape(odd, (1,)).astype(jnp.int32), straight, around)


def block_bias(first_query, first_key, rows, cols, query_segs, key_segs):
    query_pos = first_query + lax.broadcasted_iota(jnp.int32, (rows, cols), 0)
    key_pos = first_key + lax.broadcasted_iota(jnp.int32, (rows, cols), 1)
    distance = query_pos - key_pos
    allowed = (query_segs == key_segs) & (distance >= 0) & (distance < WINDOW)
    return jnp.where(allowed, 0.0, NEGATIVE)


def first_block(first_query, query_segs, key_segs, tile_k):
    earlier = jnp.sum((key_segs < query_segs[0:1, 0:1]).astype(jnp.int32))
    return lax.div(jnp.maximum(earlier, first_query - (WINDOW - 1)), tile_k)


def attend_forward_kernel(
    start, q_a, q_b, kv, seg_q, seg_k, ctx_a, ctx_b, lse, m_s, l_s, acc_s, *, tq, tk, heads
):
    first_query = start[0] + pl.program_id(0) * tq
    query_segs = seg_q[...]
    low_block = first_block(first_query, query_segs, seg_k[...], tk)
    high_block = lax.div(first_query + tq - 1, tk)
    scale = 1.0 / math.sqrt(HD)

    def step(block, first):
        first_key = pl.multiple_of(block * tk, tk)
        keys = kv[pl.ds(first_key, tk), :HD]
        values = kv[pl.ds(first_key, tk), HD:]
        bias = block_bias(first_query, first_key, tq, tk, query_segs, seg_k[:, pl.ds(first_key, tk)])
        for h in range(2 * heads):
            q = (q_a, q_b)[h // heads]
            own = slice(h % heads * HD, (h % heads + 1) * HD)
            cols = slice(h * HD, (h + 1) * HD)
            scores = dot_t(q[:, own], keys) * scale + bias
            top = jnp.max(scores, axis=1, keepdims=True)
            if first:
                exps = jnp.exp(scores - top)
                l_s[:, cols] = jnp.broadcast_to(jnp.sum(exps, axis=1, keepdims=True), (tq, HD))
                acc_s[:, cols] = dot(exps.astype(BF16), values)
                m_s[:, cols] = jnp.broadcast_to(top, (tq, HD))
            else:
                old = m_s[:, cols]
                new = jnp.maximum(old, top)
                fade = jnp.exp(old - new)
                exps = jnp.exp(scores - jnp.tile(new, (1, tk // HD)))
                l_s[:, cols] = l_s[:, cols] * fade + jnp.sum(exps, axis=1, keepdims=True)
                acc_s[:, cols] = acc_s[:, cols] * fade + dot(exps.astype(BF16), values)
                m_s[:, cols] = new

    step(high_block, True)

    def body(i, _):
        step(high_block - i, False)
        return 0

    lax.fori_loop(1, high_block - low_block + 1, body, 0)
    lane = lax.broadcasted_iota(jnp.int32, (tq, HD), 1)
    logs = jnp.zeros((tq, HD), F32)
    for h in range(2 * heads):
        own = slice(h % heads * HD, (h % heads + 1) * HD)
        cols = slice(h * HD, (h + 1) * HD)
        total = l_s[:, cols]
        (ctx_a, ctx_b)[h // heads][:, own] = (acc_s[:, cols] / total).astype(BF16)
        logs = jnp.where(lane == h, m_s[:, cols] + jnp.log(total), logs)
    lse[...] = logs


def attend_forward(start, q_a, q_b, kv, seg_q, seg_k):
    rows, width = q_a.shape
    tq = tk = 256
    length = kv.shape[0]
    tile = pl.BlockSpec((tq, width), lambda i: (i, 0))
    ctx = jax.ShapeDtypeStruct((rows, width), BF16)
    return pl.pallas_call(
        functools.partial(attend_forward_kernel, tq=tq, tk=tk, heads=width // HD),
        grid=(rows // tq,),
        in_specs=[
            pl.BlockSpec(memory_space=pltpu.SMEM),
            tile,
            tile,
            pl.BlockSpec((length, 2 * HD), lambda i: (0, 0)),
            pl.BlockSpec((tq, 1), lambda i: (i, 0)),
            pl.BlockSpec((1, length), lambda i: (0, 0)),
        ],
        out_specs=[tile, tile, pl.BlockSpec((tq, HD), lambda i: (i, 0))],
        out_shape=[ctx, ctx, jax.ShapeDtypeStruct((rows, HD), F32)],
        scratch_shapes=[pltpu.VMEM((tq, 2 * width), F32)] * 3,
        compiler_params=pltpu.CompilerParams(vmem_limit_bytes=VMEM_BYTES),
        cost_estimate=HEAVY,
        name="attend_forward",
    )(start, q_a, q_b, kv, seg_q, seg_k)


def attend_backward_kernel(
    start, q_a, q_b, kv, seg_q, seg_k, ctx_a, ctx_b, lse, dctx_a, dctx_b, dq_a, dq_b, dkv, dq_s,
    *, tq, tk, heads,
):
    first_query = start[0] + pl.program_id(0) * tq
    query_segs = seg_q[...]
    low_block = first_block(first_query, query_segs, seg_k[...], tk)
    high_block = lax.div(first_query + tq - 1, tk)
    scale = 1.0 / math.sqrt(HD)

    @pl.when(pl.program_id(0) == 0)
    def _():
        dkv[...] = jnp.zeros_like(dkv)

    dq_s[...] = jnp.zeros_like(dq_s)
    logs = lse[...]

    def body(i, _):
        first_key = pl.multiple_of((high_block - i) * tk, tk)
        keys = kv[pl.ds(first_key, tk), :HD]
        values = kv[pl.ds(first_key, tk), HD:]
        bias = block_bias(first_query, first_key, tq, tk, query_segs, seg_k[:, pl.ds(first_key, tk)])
        dk = jnp.zeros((tk, HD), F32)
        dv = jnp.zeros((tk, HD), F32)
        for h in range(2 * heads):
            own = slice(h % heads * HD, (h % heads + 1) * HD)
            cols = slice(h * HD, (h + 1) * HD)
            q_h = (q_a, q_b)[h // heads][:, own]
            do_h = (dctx_a, dctx_b)[h // heads][:, own]
            ctx_h = (ctx_a, ctx_b)[h // heads][:, own]
            inner = jnp.sum(do_h.astype(F32) * ctx_h.astype(F32), axis=1, keepdims=True)
            scores = dot_t(q_h, keys) * scale + bias
            probs = jnp.exp(scores - logs[:, h : h + 1])
            dprobs = dot_t(do_h, values)
            dscores = (probs * (dprobs - inner)).astype(BF16)
            dq_s[:, cols] += dot(dscores, keys)
            dk = dk + t_dot(dscores, q_h)
            dv = dv + t_dot(probs.astype(BF16), do_h)
        dkv[pl.ds(first_key, tk), :HD] += dk * scale
        dkv[pl.ds(first_key, tk), HD:] += dv
        return 0

    lax.fori_loop(0, high_block - low_block + 1, body, 0)
    half = heads * HD
    dq_a[...] = (dq_s[:, :half] * scale).astype(BF16)
    dq_b[...] = (dq_s[:, half:] * scale).astype(BF16)


def attend_backward(start, q_a, q_b, kv, seg_q, seg_k, ctx_a, ctx_b, lse, dctx_a, dctx_b):
    rows, width = q_a.shape
    tq = tk = 256
    length = kv.shape[0]
    tile = pl.BlockSpec((tq, width), lambda i: (i, 0))
    dq = jax.ShapeDtypeStruct((rows, width), BF16)
    return pl.pallas_call(
        functools.partial(attend_backward_kernel, tq=tq, tk=tk, heads=width // HD),
        grid=(rows // tq,),
        in_specs=[
            pl.BlockSpec(memory_space=pltpu.SMEM),
            tile,
            tile,
            pl.BlockSpec((length, 2 * HD), lambda i: (0, 0)),
            pl.BlockSpec((tq, 1), lambda i: (i, 0)),
            pl.BlockSpec((1, length), lambda i: (0, 0)),
            tile,
            tile,
            pl.BlockSpec((tq, HD), lambda i: (i, 0)),
            tile,
            tile,
        ],
        out_specs=[tile, tile, pl.BlockSpec((length, 2 * HD), lambda i: (0, 0))],
        out_shape=[dq, dq, jax.ShapeDtypeStruct((length, 2 * HD), F32)],
        scratch_shapes=[pltpu.VMEM((tq, 2 * width), F32)],
        compiler_params=pltpu.CompilerParams(vmem_limit_bytes=VMEM_BYTES),
        cost_estimate=HEAVY,
        name="attend_backward",
    )(start, q_a, q_b, kv, seg_q, seg_k, ctx_a, ctx_b, lse, dctx_a, dctx_b)


def feed_kernel(
    n2_a, n2_b, dy_a, dy_b, dy_c, dy_d, wg_a, wg_b, wu_a, wu_b, wd_a, wd_b, hidden, dgate, dup, *, tm
):
    root = math.sqrt(2.0 / math.pi)
    rows = n2_a.shape[0]
    feats = wg_a.shape[0]
    for base, n2, first_dy, second_dy in ((0, n2_a, dy_a, dy_b), (rows, n2_b, dy_c, dy_d)):
        for first in range(0, rows, tm):
            own = slice(first, first + tm)
            low, high = n2[own, :feats], n2[own, feats:]
            gate = dot(low, wg_a[...]) + dot(high, wg_b[...])
            up = dot(low, wu_a[...]) + dot(high, wu_b[...])
            dh = dot_t(first_dy[own], wd_a[...]) + dot_t(second_dy[own], wd_b[...])
            square = gate * gate
            tanh = jnp.tanh(gate * (root + (root * 0.044715) * square))
            half = 0.5 + 0.5 * tanh
            act = gate * half
            slope = half + act * (1.0 - tanh) * (root + (3.0 * 0.044715 * root) * square)
            out = slice(base + first, base + first + tm)
            hidden[out] = (act * up).astype(BF16)
            dgate[out] = (dh * up * slope).astype(BF16)
            dup[out] = (dh * act).astype(BF16)


def feed(n2s, dys, wg, wu, wd):
    rows, width = n2s[0].shape
    feats, units = wg[0].shape
    tn = 384
    whole = pl.BlockSpec((rows, width), lambda j: (0, 0))
    half = pl.BlockSpec((rows, feats), lambda j: (0, 0))
    out = jax.ShapeDtypeStruct((2 * rows, units), BF16)
    return pl.pallas_call(
        functools.partial(feed_kernel, tm=256),
        grid=(units // tn,),
        in_specs=[whole] * 2
        + [half] * 4
        + [pl.BlockSpec((feats, tn), lambda j: (0, j))] * 4
        + [pl.BlockSpec((tn, feats), lambda j: (j, 0))] * 2,
        out_specs=[pl.BlockSpec((2 * rows, tn), lambda j: (0, j))] * 3,
        out_shape=[out] * 3,
        compiler_params=pltpu.CompilerParams(vmem_limit_bytes=VMEM_BYTES),
        cost_estimate=HEAVY,
        name="feed",
    )(*n2s, *dys, *wg, *wu, *wd)


def weight_grad_kernel(*refs):
    out = refs[-1]
    pairs = len(refs) // 2
    total = None
    for left, right in zip(refs[:pairs], refs[pairs:-1]):
        part = t_dot(left[...], right[...])
        total = part if total is None else total + part
    out[...] = total.astype(BF16)


def weight_grad(lefts, rights, name):
    width_left = lefts[0][4]
    width_right = rights[0][4]
    tn = 384

    def left_spec(block):
        _, at, rows, col, cols = block
        return pl.BlockSpec((rows, cols), lambda j: (at, col))

    def right_spec(block):
        _, at, rows, col, cols = block
        return pl.BlockSpec((rows, tn), lambda j: (at, col * (cols // tn) + j))

    out = jax.ShapeDtypeStruct((width_left, width_right), BF16)
    tokens = sum(block[2] for block in lefts)
    return pl.pallas_call(
        weight_grad_kernel,
        grid=(width_right // tn,),
        in_specs=[left_spec(b) for b in lefts] + [right_spec(b) for b in rights],
        out_specs=pl.BlockSpec((width_left, tn), lambda j: (0, j)),
        out_shape=out,
        compiler_params=pltpu.CompilerParams(vmem_limit_bytes=VMEM_BYTES),
        cost_estimate=HEAVY,
        name=name,
    )(*[b[0] for b in lefts], *[b[0] for b in rights])


def project_kernel(*refs, lefts, multiply):
    left = refs[:lefts]
    weights = refs[lefts : 3 * lefts]
    first, second = refs[3 * lefts :]
    rows = first.shape[0]
    in_first = pl.program_id(0) < pl.num_programs(0) // 2

    def fill(chosen):
        for at, out in ((0, first), (rows, second)):
            own = slice(at, at + rows)
            out[...] = sum(multiply(l[own], w[...]) for l, w in zip(left, chosen)).astype(BF16)

    pl.when(in_first)(lambda: fill(weights[0::2]))
    pl.when(jnp.logical_not(in_first))(lambda: fill(weights[1::2]))


def project(lefts, weights, transposed, name):
    rows, units = lefts[0].shape
    feats = weights[0][0].shape[0 if transposed else 1]
    tn = 384
    tiles = feats // tn
    whole = pl.BlockSpec((rows, units), lambda j: (0, 0))

    def low(j):
        return jnp.minimum(j, tiles - 1)

    def high(j):
        return jnp.maximum(j - tiles, 0)

    if transposed:
        specs = [pl.BlockSpec((tn, units), lambda j, f=f: (f(j), 0)) for f in (low, high)]
    else:
        specs = [pl.BlockSpec((units, tn), lambda j, f=f: (0, f(j))) for f in (low, high)]
    out = jax.ShapeDtypeStruct((rows // 2, 2 * feats), BF16)
    flat = [half for weight in weights for half in weight]
    return pl.pallas_call(
        functools.partial(
            project_kernel, lefts=len(lefts), multiply=dot_t if transposed else dot
        ),
        grid=(2 * tiles,),
        in_specs=[whole] * len(lefts) + specs * len(lefts),
        out_specs=[pl.BlockSpec((rows // 2, tn), lambda j: (0, j))] * 2,
        out_shape=[out] * 2,
        compiler_params=pltpu.CompilerParams(vmem_limit_bytes=VMEM_BYTES),
        cost_estimate=HEAVY,
        name=name,
    )(*lefts, *flat)


def per_device(
    tokens_in,
    norm1_gain,
    w_query,
    w_keyval,
    w_attn_out,
    norm2_gain,
    w_gate,
    w_up,
    w_down,
    segment_ids,
    out_cotangent,
):
    width = D
    row = lax.axis_index("row")
    col = lax.axis_index("col")
    local = tokens_in.shape[0]
    mine = local // 2
    feats = tokens_in.shape[1]
    length = segment_ids.shape[1]
    spans = length // local

    def keep(value):
        return lax.dynamic_slice_in_dim(value, row * mine, mine, 0)

    def give(value):
        return lax.dynamic_slice_in_dim(value, (1 - row) * mine, mine, 0)

    is_low = row == 0

    odd = lax.axis_index("dp") % 2
    paired = lax.axis_size("dp") % 2 == 0

    def straight_part(weight):
        span = weight.shape[0] // 2
        return lax.dynamic_slice_in_dim(weight, odd * span, span, 0) if paired else weight

    def placed(straight, around):
        return place_rows(odd, straight, around) if paired else straight

    def send_pair(straight):
        return rounds.send(swap_pair, straight) if paired else straight

    rounds = Rounds()
    small = jnp.concatenate([norm1_gain, norm2_gain, segment_ids.reshape(-1).astype(F32)])
    w_qkv = jnp.concatenate([w_query, w_keyval], axis=1)
    heads_own = w_query.shape[1]
    x_in = rounds.send(swap_row, give(tokens_in))
    wq_far_own = rounds.send(swap_far, w_query)
    small_in = rounds.send(swap_row, small)
    wqkv_in = rounds.send(swap_row, w_qkv)
    rounds.wait(x_in, wq_far_own, small_in)

    wo_far_own = rounds.send(swap_far, w_attn_out)
    wo_in = rounds.send(swap_row, w_attn_out)
    gain_one = jnp.concatenate([norm1_gain, small_in[:feats]])
    gain_two = jnp.concatenate([norm2_gain, small_in[feats : 2 * feats]])
    segs_in = small_in[2 * feats :].astype(jnp.int32).reshape(segment_ids.shape)
    segs_all = jnp.concatenate(
        [jnp.where(is_low, segment_ids, segs_in), jnp.where(is_low, segs_in, segment_ids)], axis=0
    )
    x = jnp.concatenate([keep(tokens_in), x_in], axis=1).astype(F32)
    inverse_one = lax.rsqrt(jnp.mean(x * x, axis=1, keepdims=True) + EPSILON)
    normed_one = (x * inverse_one * gain_one).astype(BF16)
    place = col % spans
    seg_row = lax.dynamic_slice_in_dim(segs_all, col // spans, 1, 0)
    first_token = place * local + row * mine
    seg_q = lax.dynamic_slice_in_dim(seg_row[0], first_token, mine, 0)[:, None]
    start = jnp.reshape(first_token, (1,)).astype(jnp.int32)
    rounds.wait(wqkv_in, wo_far_own)

    wq_in = wqkv_in[:, :heads_own]
    wq_far_in = rounds.send(swap_far, wq_in)
    wkv = jnp.concatenate([w_keyval, wqkv_in[:, heads_own:]], axis=0)
    kv_own = dot(normed_one, wkv, BF16)
    kv_in = rounds.send(swap_row, kv_own)
    wg_straight = rounds.send(swap_row, after(straight_part(w_gate), kv_own))
    rounds.wait(wo_in, kv_in, wq_far_in)

    kv_pair = jnp.concatenate(
        [jnp.where(is_low, kv_own, kv_in), jnp.where(is_low, kv_in, kv_own)], axis=0
    )
    wq_half = jnp.concatenate(
        [
            jnp.concatenate([w_query, wq_far_own], axis=1),
            jnp.concatenate([wq_in, wq_far_in], axis=1),
        ],
        axis=0,
    )
    wo_far_in = rounds.send(swap_far, wo_in)
    wu_straight = rounds.send(swap_row, straight_part(w_up))
    wq_core = rounds.send(swap_core, wq_half)
    if spans == 2:
        kv_far = rounds.send(swap_core, kv_pair)
        first = place == 0
        kv = jnp.concatenate(
            [jnp.where(first, kv_pair, kv_far), jnp.where(first, kv_far, kv_pair)], axis=0
        )
    else:
        kv = kv_pair
    q_a = dot(normed_one, wq_half, BF16)
    q_b = dot(normed_one, wq_core, BF16)
    rounds.wait(wo_far_in, kv, q_b)

    wo_half = jnp.concatenate(
        [
            jnp.concatenate([w_attn_out, wo_far_own], axis=0),
            jnp.concatenate([wo_in, wo_far_in], axis=0),
        ],
        axis=1,
    )
    dy_own = keep(out_cotangent)
    wo_core = rounds.send(swap_core, wo_half)
    dy_far_own = rounds.send(swap_far, dy_own)
    ctx_a, ctx_b, lse = attend_forward(start, after(q_a, rounds.token), q_b, kv, seg_q, seg_row)
    middle = x + dot(ctx_a, wo_half) + dot(ctx_b, wo_core)
    inverse_two = lax.rsqrt(jnp.mean(middle * middle, axis=1, keepdims=True) + EPSILON)
    n2 = (middle * inverse_two * gain_two).astype(BF16)
    rounds.wait(wg_straight, n2)

    n2_far = rounds.send(swap_far, n2)
    wg_around = send_pair(wg_straight)
    wd_straight = rounds.send(swap_row, straight_part(w_down))
    n2_near = rounds.send(swap_core, n2)
    rounds.wait(wu_straight, wg_around, n2_near, dy_far_own)

    dy_in = rounds.send(swap_row, give(out_cotangent))
    wu_around = send_pair(wu_straight)
    dy_near_own = rounds.send(swap_core, dy_own)
    rounds.wait(wd_straight, wu_around, dy_near_own)

    wd_around = send_pair(wd_straight)
    dy_diagonal_own = rounds.send(swap_core, dy_far_own)
    wg = (w_gate, placed(wg_straight, wg_around))
    wu = (w_up, placed(wu_straight, wu_around))
    rounds.wait(dy_in, n2_far, dy_diagonal_own)

    dy_near_in = rounds.send(swap_core, dy_in)
    dy_far_in = rounds.send(swap_far, dy_in)
    n2_diagonal = rounds.send(swap_core, n2_far)
    wd = (w_down, placed(wd_straight, wd_around))
    dy_near = (dy_near_own, dy_near_in)
    hidden_a, dgate_a, dup_a = feed((n2, n2_near), (dy_own, dy_in, *dy_near), wg, wu, wd)
    dy_diagonal = (dy_diagonal_own, swap_core(dy_far_in))
    hidden_b, dgate_b, dup_b = feed(
        (after(n2_far, hidden_a), n2_diagonal), (dy_far_own, dy_far_in, *dy_diagonal), wg, wu, wd
    )

    normed = [n2, n2_near, n2_far, n2_diagonal]
    cotangents = [(dy_own, dy_in), dy_near, (dy_far_own, dy_far_in), dy_diagonal]
    units = w_gate.shape[1]

    def normed_blocks(half):
        return [(value, 0, mine, half, feats) for value in normed]

    def cotangent_blocks(half):
        return [(value[half], 0, mine, 0, feats) for value in cotangents]

    def unit_blocks(first_pair, second_pair, *earlier):
        if earlier:
            first_pair = after(first_pair, *earlier)
        return [
            (value, at, mine, 0, units) for value in (first_pair, second_pair) for at in range(2)
        ]

    steps = Steps()

    def gate_grad(half):
        return steps(
            lambda last: weight_grad(normed_blocks(half), unit_blocks(dgate_a, last), "w_gate_grad"),
            dgate_b,
        )

    def up_grad(half):
        return steps(
            lambda last: weight_grad(normed_blocks(half), unit_blocks(dup_a, last), "w_up_grad"),
            dup_b,
        )

    def down_grad(half):
        return steps(
            lambda last: weight_grad(
                unit_blocks(hidden_a, last), cotangent_blocks(half), "w_down_grad"
            ),
            hidden_b,
        )

    gate_sum, up_sum, down_sum, query_sum, out_sum = [DpTotal(steps) for _ in range(5)]
    gate_in = swap_row(gate_grad(1))
    dn2_far, dn2_diagonal = steps(
        lambda dgate: project([dgate, dup_b], [wg, wu], True, "feed_back"), dgate_b
    )
    diagonal_in = swap_core(dn2_diagonal)
    gate_own = gate_grad(0)
    for_far = steps(
        lambda into: (dn2_far.astype(F32) + into.astype(F32)).astype(BF16), diagonal_in
    )
    far_in = swap_far(for_far)
    up_in = swap_row(up_grad(1))
    dn2_own, dn2_near = steps(
        lambda dgate: project([dgate, dup_a], [wg, wu], True, "feed_back"), dgate_a
    )
    near_in = swap_core(dn2_near)
    gate_sum.begin(gate_own, gate_in)
    up_own = up_grad(0)

    def middle_back(far):
        dnormed = dn2_own.astype(F32) + near_in.astype(F32) + far.astype(F32)
        scaled = dnormed * gain_two
        projection = jnp.mean(scaled * middle, axis=1, keepdims=True)
        dmiddle = (
            jnp.concatenate([dy_own, dy_in], axis=1).astype(F32)
            + inverse_two * scaled
            - middle * (inverse_two**3 * projection)
        )
        return dmiddle, dmiddle.astype(BF16), jnp.sum(dnormed * middle * inverse_two, axis=0)

    dmiddle, dattn, gain_two_part = steps(middle_back, far_in)
    down_in = swap_row(down_grad(1))

    dctx_a, dctx_b = steps(lambda d: (dot_t(d, wo_half, BF16), dot_t(d, wo_core, BF16)), dattn)
    gate_sum.middle()
    up_sum.begin(up_own, up_in)
    out_core = swap_core(steps(lambda d: t_dot(ctx_b, d, BF16), dattn))
    dq_a, dq_b, dkv_all = steps(
        lambda d: attend_backward(
            start, q_a, q_b, kv, seg_q, seg_row, ctx_a, ctx_b, lse, d, dctx_b
        ),
        dctx_a,
    )
    out_chip = steps(lambda core: t_dot(ctx_a, dattn, BF16) + core, out_core)
    out_far = swap_far(out_chip[heads_own:])
    if spans == 2:
        is_first = place == 0

        def other_half(value):
            return jnp.where(is_first, value[local:], value[:local]).astype(BF16)

        dkv_core = swap_core(steps(other_half, dkv_all))
    up_sum.middle()
    gate_sum.end()
    down_own = down_grad(0)
    down_sum.begin(down_own, down_in)
    if spans == 2:

        def pair_of(core):
            value = jnp.where(is_first, dkv_all[:local], dkv_all[local:]) + core.astype(F32)
            return keep(value), give(value).astype(BF16)

        dkv_keep, dkv_give = steps(pair_of, dkv_core)
    else:
        dkv_keep, dkv_give = keep(dkv_all), give(dkv_all).astype(BF16)
    dkv_row = swap_row(dkv_give)
    query_core = swap_core(steps(lambda d: t_dot(normed_one, d, BF16), dq_b))
    ffn_far, ffn_diagonal = steps(lambda h: project([h], [wd], False, "down"), hidden_b)
    out_mine = steps(lambda far: out_chip[:heads_own] + far, out_far)
    out_row = swap_row(out_mine[:, feats:])
    query_chip = steps(lambda core: t_dot(normed_one, dq_a, BF16) + core, query_core)
    query_far = swap_far(query_chip[:, heads_own:])
    gate_total = gate_sum.result()
    ffn_diagonal_in = swap_core(ffn_diagonal)
    dkv = steps(lambda other: (dkv_keep + other.astype(F32)).astype(BF16), dkv_row)

    def norm_one_back(dkv):
        dnormed = dot_t(dq_a, wq_half) + dot_t(dq_b, wq_core) + dot_t(dkv, wkv)
        scaled = dnormed * gain_one
        projection = jnp.mean(scaled * x, axis=1, keepdims=True)
        dx = dmiddle + inverse_one * scaled - x * (inverse_one**3 * projection)
        gain_parts = jnp.stack([jnp.sum(dnormed * x * inverse_one, axis=0), gain_two_part], axis=1)
        kv_part = t_dot(normed_one, dkv, BF16)
        small_part = jnp.pad(gain_parts, ((0, 0), (0, HD - 2))).astype(BF16)
        return dx, dx[:, feats:].astype(BF16), jnp.concatenate([kv_part, small_part], axis=1)

    dx, dx_give, small_part = steps(norm_one_back, dkv)
    down_sum.middle()
    up_sum.end()
    small_row = swap_row(small_part[feats:])
    ffn_own, ffn_near = steps(lambda h: project([h], [wd], False, "down"), hidden_a)
    ffn_for_far = steps(
        lambda into: (ffn_far.astype(F32) + into.astype(F32)).astype(BF16), ffn_diagonal_in
    )
    ffn_far_in = swap_far(ffn_for_far)
    out_sum.begin(out_mine[:, :feats], out_row)
    query_mine = steps(lambda far: query_chip[:, :heads_own] + far, query_far)
    query_row = swap_row(query_mine[feats:])
    up_total = up_sum.result()
    small_one = steps(lambda other: small_part[:feats] + other, small_row)
    small_core = swap_core(small_one)
    out_sum.middle()
    down_sum.end()
    query_sum.begin(query_mine[:feats], query_row)
    dx_in = swap_row(dx_give)
    small_two = steps(jnp.add, small_core, small_one)
    ffn_near_in = swap_core(ffn_near)
    out_sum.end()
    query_sum.middle()

    def add_up(far):
        y = middle + ffn_own.astype(F32) + ffn_near_in.astype(F32) + far.astype(F32)
        return y, y[:, feats:].astype(BF16)

    y, y_give = steps(add_up, ffn_far_in)
    small_far = swap_far(small_two)
    down_total = down_sum.result()
    y_in = swap_row(y_give)
    query_sum.end()
    small_three = steps(jnp.add, small_far, small_two)
    if lax.axis_size("dp") == 4:
        small_four = steps(jnp.add, swap_pair(small_three), small_three)
        small_total = steps(jnp.add, swap_mirror(small_four), small_four)
    else:
        small_total = lax.psum(small_three, "dp")

    def put_back(other, value):
        other = other.astype(F32)
        own = value[:, :feats]
        return jnp.concatenate(
            [jnp.where(is_low, own, other), jnp.where(is_low, other, own)], axis=0
        )

    dx_out = steps(put_back, dx_in, dx)
    y_out = steps(put_back, y_in, y)
    query_total = query_sum.result()
    out_total = out_sum.result()
    small_total = small_total.astype(F32)
    kv_total = small_total[:, : 2 * HD]
    gain_total = small_total[:, 2 * HD : 2 * HD + 2].T

    return (
        y_out,
        dx_out,
        query_total,
        kv_total,
        out_total,
        gate_total,
        up_total,
        down_total,
        gain_total[0],
        gain_total[1],
    )


def solution(mesh):
    return jax.shard_map(
        per_device,
        mesh=mesh,
        in_specs=(
            P(("dp", "col"), "row"),
            P("row"),
            P("row", "col"),
            P("row", None),
            P("col", "row"),
            P("row"),
            P("row", "col"),
            P("row", "col"),
            P("col", "row"),
            P(("dp", "row"), None),
            P(("dp", "col"), "row"),
        ),
        out_specs=(
            P(("dp", "col"), "row"),
            P(("dp", "col"), "row"),
            P("row", "col"),
            P("row", None),
            P("col", "row"),
            P("row", "col"),
            P("row", "col"),
            P("col", "row"),
            P("row"),
            P("row"),
        ),
        check_vma=False,
    )
```

time: 841 us -> 653 us (0.78)
  Pallas kernels: 64.4 us -> 184 us
  waiting for transfers between devices: 329 us -> 227 us
  matrix products: 110 us -> 41.3 us
  blocking collectives: 52.4 us -> 0 us
  starting transfers between devices: 116 us -> 91.3 us
  local copies, waits for them, and re-layouts: 51.4 us -> 27.2 us
  other arithmetic: 95.2 us -> 73.6 us
  between operations: 15.5 us -> 2.12 us
    pallas_call x1 -> x15, Pallas kernels: 37.2 us -> 156 us  [the longest x6 54.5 us: weight_grad(): pl.pallas_call(weight_grad_kernel, grid=(width_right // tn,), in_specs=[l...]
    psum x1 -> x0, blocking collectives: 52.4 us -> none  [per_device(): kv_total, gain_total = lax.psum((kv_mine, gain_mine), ('dp', 'col'))]
    ppermute x21 -> x18, waiting for transfers between devices: 132 us -> 88.3 us  [swap_row(): return lax.ppermute(value, 'row', [(0, 1), (1, 0)])]
    ppermute x15 -> x20, waiting for transfers between devices: 116 us -> 77.7 us  [the longest x14 66.2 us: swap_pair(): return lax.ppermute(value, 'dp', [(i, i ^ 1) for i in range(count)])]
    dot_general x6 -> x5, matrix products: 50.8 us -> 14.4 us  [t_dot(): lax.dot_general(left, right, (((0,), (0,)), ((), ())), preferred_element_...]
    ppermute x21 -> x18, starting transfers between devices: 38.9 us -> 18.3 us  [swap_row(): return lax.ppermute(value, 'row', [(0, 1), (1, 0)])]
    dot_general x5, matrix products: 35.7 us -> 15.3 us  [dot_t(): lax.dot_general(left, right, (((1,), (1,)), ((), ())), preferred_element_...]
    ppermute x8 -> x12, waiting for transfers between devices: 80.3 us -> 61 us  [swap_far(): return lax.ppermute(value, 'col', [(0, 2), (2, 0), (1, 3), (3, 1)])]
  transfers between devices with their start and end apart: 63 -> 67, of which waited for: 23 -> 22; matrix products, arithmetic and copies ran while one was open for 26% -> 20% of each run, Pallas kernels for 3% -> 24%
where the time goes in v2:
time: 653 us; the launch traced here: 646 us
  waiting for transfers between devices  227 us (35%)
  Pallas kernels  184 us (28%)
  starting transfers between devices  91.3 us (14%)
  other arithmetic  73.6 us (11%)
  matrix products  41.3 us (6%)
  local copies, waits for them, and re-layouts  27.2 us (4%)
    ppermute x18, waiting for transfers between devices, swap_row(): return lax.ppermute(value, 'row', [(0, 1), (1, 0)])  88.3 us
    ppermute x14, waiting for transfers between devices, swap_pair(): return lax.ppermute(value, 'dp', [(i, i ^ 1) for i in range(count)])  66.2 us
    ppermute x12, waiting for transfers between devices, swap_far(): return lax.ppermute(value, 'col', [(0, 2), (2, 0), (1, 3), (3, 1)])  61 us
    pallas_call x6, Pallas kernels, weight_grad(): pl.pallas_call(weight_grad_kernel, grid=(width_right // tn,), in_specs=[l...  54.5 us
    pallas_call x4, Pallas kernels, project(): pl.pallas_call(functools.partial(project_kernel, lefts=len(lefts), multip...  51.1 us
    pallas_call x2, Pallas kernels, feed(): pl.pallas_call(functools.partial(feed_kernel, tm=256), grid=(units // tn,...  42.1 us
    ppermute x17, starting transfers between devices, swap_core(): return lax.ppermute(value, 'col', [(0, 1), (1, 0), (2, 3), (3, 2)])  20.2 us
    pallas_call x1, Pallas kernels, attend_backward(): pl.pallas_call(functools.partial(attend_backward_kernel, tq=tq, tk=tk, he...  19.2 us
  transfers between devices with their start and end apart: 67, of which 22 were waited for; matrix products, arithmetic and copies ran while one was open for 20% of the time, Pallas kernels for 24%

profile of v2, /device:TPU:0, one launch (start us, length us, event | category | flops | bytes accessed | tf_op | source)
XLA Modules:
  0.0 646.3 jit_solution(1237702291251083985)
XLA Ops:
  20.5 24.6 %collective-permute-done.1 = f32[3584]{0:T(1024)S(1)} collective-permute-done((f32[3584]{0:T(1024)}, f32[3584]{0:T(1024)S(1)}, u32[]{:S(2)}, u32[]{:S(2)}) %collective-permute-start.1) | collective-permute-done | bytes 14368 | tf_op jit(solution)/shard_map/ppermute | solution.py:27
  57.1 9.7 %collective-permute-done.4 = bf16[384,768]{1,0:T(8,128)(2,1)S(1)} collective-permute-done((bf16[384,768]{1,0:T(8,128)(2,1)}, bf16[384,768]{1,0:T(8,128)(2,1)S(1)}, u32[]{:S(2)}, u32[]{:S(2)}) %collective-permute-start.4) | collective-permute-done | bytes 589856 | tf_op jit(solution)/shard_map/ppermute | solution.py:35
  70.2 7.2 %collective-permute-done.7 = bf16[512,256]{1,0:T(8,128)(2,1)S(1)} collective-permute-done((bf16[512,256]{1,0:T(8,128)(2,1)S(1)}, bf16[512,256]{1,0:T(8,128)(2,1)S(1)}, u32[]{:S(2)}, u32[]{:S(2)}) %collective-permute-start.7) | collective-permute-done | bytes 262176 | tf_op jit(solution)/shard_map/ppermute | solution.py:27
  89.5 8.2 %collective-permute-done.8 = bf16[384,768]{1,0:T(8,128)(2,1)S(1)} collective-permute-done((bf16[384,768]{1,0:T(8,128)(2,1)S(1)}, bf16[384,768]{1,0:T(8,128)(2,1)S(1)}, u32[]{:S(2)}, u32[]{:S(2)}) %collective-permute-start.8) | collective-permute-done | bytes 589856 | tf_op jit(solution)/shard_map/ppermute | solution.py:35
  102.8 8.5 %attend_forward.1 = (bf16[512,768]{1,0:T(8,128)(2,1)}, bf16[512,768]{1,0:T(8,128)(2,1)}, f32[512,128]{1,0:T(8,128)}) custom-call(s32[1]{0:T(128)} %bitcast.start, bf16[512,768]{1,0:T(8,128)(2,1)} %convolution_convert_fusion.8.q_a, bf16[512,768]{1,0:T(8,128)(2,1)} %convolution_convert_fusion.7.q_b, bf16[2048,256]{1,0:T(8,128)(2,1)} %pad_maximum_fusion.4.kv, ...), custom_call_target="tpu_custom_call" | custom-call | flops 999999995904 | bytes 1000000000 | tf_op jit(solution)/shard_map/attend_forward/pallas_call | solution.py:240
  128.3 20.0 %collective-permute-done.15.around = bf16[384,1152]{1,0:T(8,128)(2,1)S(1)} collective-permute-done((bf16[384,1152]{1,0:T(8,128)(2,1)}, bf16[384,1152]{1,0:T(8,128)(2,1)S(1)}, u32[]{:S(2)}, u32[]{:S(2)}) %collective-permute-start.15) | collective-permute-done | bytes 884768 | tf_op jit(solution)/shard_map/ppermute | solution.py:56
  155.0 16.3 %collective-permute-done.19.straight = bf16[576,768]{1,0:T(8,128)(2,1)} collective-permute-done((bf16[576,768]{1,0:T(8,128)(2,1)}, bf16[576,768]{1,0:T(8,128)(2,1)}, u32[]{:S(2)}, u32[]{:S(2)}) %collective-permute-start.19) | collective-permute-done | bytes 884768 | tf_op jit(solution)/shard_map/ppermute | solution.py:27
  178.9 7.8 %collective-permute-done.17.dy_b.refs_4_ = bf16[512,768]{1,0:T(8,128)(2,1)} collective-permute-done((bf16[512,768]{1,0:T(8,128)(2,1)}, bf16[512,768]{1,0:T(8,128)(2,1)}, u32[]{:S(2)}, u32[]{:S(2)}) %collective-permute-start.17) | collective-permute-done | bytes 786464 | tf_op jit(solution)/shard_map/ppermute | solution.py:27
  187.4 9.3 %collective-permute-done.24.around = bf16[576,768]{1,0:T(8,128)(2,1)} collective-permute-done((bf16[576,768]{1,0:T(8,128)(2,1)}, bf16[576,768]{1,0:T(8,128)(2,1)}, u32[]{:S(2)}, u32[]{:S(2)}) %collective-permute-start.24) | collective-permute-done | bytes 884768 | tf_op jit(solution)/shard_map/ppermute | solution.py:56
  199.5 7.4 %collective-permute-done.26.dy_b.refs_6_ = bf16[512,768]{1,0:T(8,128)(2,1)} collective-permute-done((bf16[512,768]{1,0:T(8,128)(2,1)}, bf16[512,768]{1,0:T(8,128)(2,1)}, u32[]{:S(2)}, u32[]{:S(2)}) %collective-permute-start.26) | collective-permute-done | bytes 786464 | tf_op jit(solution)/shard_map/ppermute | solution.py:35
  206.9 21.2 %feed.2 = (bf16[1024,1152]{1,0:T(8,128)(2,1)}, bf16[1024,1152]{1,0:T(8,128)(2,1)}, bf16[1024,1152]{1,0:T(8,128)(2,1)}) custom-call(bf16[512,1536]{1,0:T(8,128)(2,1)} %multiply_convert_fusion.n2_a.refs_0_, bf16[512,1536]{1,0:T(8,128)(2,1)} %collective-permute-done.13.n2_b.refs_1_, bf16[512,768]{1,0:T(8,128)(2,1)} %get-tuple-element.143.dy_a.refs_4_, ...), custom_call_target="tpu_custom_call" | custom-call | flops 999999995904 | bytes 1000000000 | tf_op jit(solution)/shard_map/feed/pallas_call | solution.py:370
  228.1 20.9 %feed.3 = (bf16[1024,1152]{1,0:T(8,128)(2,1)}, bf16[1024,1152]{1,0:T(8,128)(2,1)}, bf16[1024,1152]{1,0:T(8,128)(2,1)}) custom-call(bf16[512,1536]{1,0:T(8,128)(2,1)} %collective-permute-done.21.n2_a.refs_2_, bf16[512,1536]{1,0:T(8,128)(2,1)} %collective-permute-done.25.n2_b.refs_3_, bf16[512,768]{1,0:T(8,128)(2,1)} %collective-permute-done.16.dy_a.refs_6_, ...), custom_call_target="tpu_custom_call" | custom-call | flops 999999995904 | bytes 1000000000 | tf_op jit(solution)/shard_map/feed/pallas_call | solution.py:370
  249.1 8.9 %w_gate_grad.2 = bf16[768,1152]{1,0:T(8,128)(2,1)} custom-call(bf16[512,1536]{1,0:T(8,128)(2,1)} %multiply_convert_fusion.n2_a.refs_0_, bf16[512,1536]{1,0:T(8,128)(2,1)} %collective-permute-done.13.n2_b.refs_1_, bf16[512,1536]{1,0:T(8,128)(2,1)} %collective-permute-done.21.n2_a.refs_2_, bf16[512,1536]{1,0:T(8,128)(2,1)} %collective-permute-done.25.n2_b.refs_3_, ...), custom_call_target="tpu_custom_call" | custom-call | flops 999999995904 | bytes 1000000000 | tf_op jit(solution)/shard_map/w_gate_grad/pallas_call | solution.py:410
  258.3 16.0 %feed_back.2 = (bf16[512,1536]{1,0:T(8,128)(2,1)}, bf16[512,1536]{1,0:T(8,128)(2,1)}) custom-call(bf16[1024,1152]{1,0:T(8,128)(2,1)} %get-tuple-element.161.refs_6_.refs_7_.refs_0_, bf16[1024,1152]{1,0:T(8,128)(2,1)} %get-tuple-element.168.refs_1_.refs_6_.refs_7_, bf16[768,1152]{1,0:T(8,128)(2,1)} %refs_2_.3, bf16[768,1152]{1,0:T(8,128)(2,1)} %place_rows.3.wg_b.refs_3_, ...), custom_call_target="tpu_custom_call" | custom-call | flops 999999995904 | bytes 1000000000 | tf_op jit(solution)/shard_map/feed_back/pallas_call | solution.py:457
  274.6 9.0 %w_gate_grad.3 = bf16[768,1152]{1,0:T(8,128)(2,1)} custom-call(bf16[512,1536]{1,0:T(8,128)(2,1)} %multiply_convert_fusion.n2_a.refs_0_, bf16[512,1536]{1,0:T(8,128)(2,1)} %collective-permute-done.13.n2_b.refs_1_, bf16[512,1536]{1,0:T(8,128)(2,1)} %collective-permute-done.21.n2_a.refs_2_, bf16[512,1536]{1,0:T(8,128)(2,1)} %collective-permute-done.25.n2_b.refs_3_, ...), custom_call_target="tpu_custom_call" | custom-call | flops 999999995904 | bytes 1000000000 | tf_op jit(solution)/shard_map/w_gate_grad/pallas_call | solution.py:410
  287.1 8.9 %w_up_grad.2 = bf16[768,1152]{1,0:T(8,128)(2,1)} custom-call(bf16[512,1536]{1,0:T(8,128)(2,1)} %multiply_convert_fusion.n2_a.refs_0_, bf16[512,1536]{1,0:T(8,128)(2,1)} %collective-permute-done.13.n2_b.refs_1_, bf16[512,1536]{1,0:T(8,128)(2,1)} %collective-permute-done.21.n2_a.refs_2_, bf16[512,1536]{1,0:T(8,128)(2,1)} %collective-permute-done.25.n2_b.refs_3_, ...), custom_call_target="tpu_custom_call" | custom-call | flops 999999995904 | bytes 1000000000 | tf_op jit(solution)/shard_map/w_up_grad/pallas_call | solution.py:410
  297.7 15.9 %feed_back.3 = (bf16[512,1536]{1,0:T(8,128)(2,1)}, bf16[512,1536]{1,0:T(8,128)(2,1)}) custom-call(bf16[1024,1152]{1,0:T(8,128)(2,1)} %get-tuple-element.164.refs_4_.refs_5_.refs_0_, bf16[1024,1152]{1,0:T(8,128)(2,1)} %get-tuple-element.153.refs_4_.refs_5_.refs_1_, bf16[768,1152]{1,0:T(8,128)(2,1)} %refs_2_.3, bf16[768,1152]{1,0:T(8,128)(2,1)} %place_rows.3.wg_b.refs_3_, ...), custom_call_target="tpu_custom_call" | custom-call | flops 999999995904 | bytes 1000000000 | tf_op jit(solution)/shard_map/feed_back/pallas_call | solution.py:457
  318.1 9.0 %w_up_grad.3 = bf16[768,1152]{1,0:T(8,128)(2,1)} custom-call(bf16[512,1536]{1,0:T(8,128)(2,1)} %multiply_convert_fusion.n2_a.refs_0_, bf16[512,1536]{1,0:T(8,128)(2,1)} %collective-permute-done.13.n2_b.refs_1_, bf16[512,1536]{1,0:T(8,128)(2,1)} %collective-permute-done.21.n2_a.refs_2_, bf16[512,1536]{1,0:T(8,128)(2,1)} %collective-permute-done.25.n2_b.refs_3_, ...), custom_call_target="tpu_custom_call" | custom-call | flops 999999995904 | bytes 1000000000 | tf_op jit(solution)/shard_map/w_up_grad/pallas_call | solution.py:410
  335.5 9.4 %w_down_grad.2 = bf16[1152,768]{1,0:T(8,128)(2,1)} custom-call(bf16[1024,1152]{1,0:T(8,128)(2,1)} %get-tuple-element.198.refs_0_.refs_1_, bf16[1024,1152]{1,0:T(8,128)(2,1)} %get-tuple-element.198.refs_0_.refs_1_, bf16[1024,1152]{1,0:T(8,128)(2,1)} %get-tuple-element.189.refs_2_.refs_3_.refs_0_, ...), custom_call_target="tpu_custom_call" | custom-call | flops 999999995904 | bytes 1000000000 | tf_op jit(solution)/shard_map/w_down_grad/pallas_call | solution.py:410
  366.0 19.2 %attend_backward.1 = (bf16[512,768]{1,0:T(8,128)(2,1)}, bf16[512,768]{1,0:T(8,128)(2,1)}, f32[2048,256]{1,0:T(8,128)}) custom-call(s32[1]{0:T(128)} %bitcast.start, bf16[512,768]{1,0:T(8,128)(2,1)} %convolution_convert_fusion.8.q_a, bf16[512,768]{1,0:T(8,128)(2,1)} %convolution_convert_fusion.7.q_b, bf16[2048,256]{1,0:T(8,128)(2,1)} %pad_maximum_fusion.4.kv, ...), custom_call_target="tpu_custom_call" | custom-call | flops 999999995904 | bytes 1000000000 | tf_op jit(solution)/shard_map/attend_backward/pallas_call | solution.py:314
  395.2 14.1 %collective-permute-start.40 = (bf16[1024,256]{1,0:T(8,128)(2,1)}, bf16[1024,256]{1,0:T(8,128)(2,1)}, u32[]{:S(2)}, u32[]{:S(2)}) collective-permute-start(bf16[1024,256]{1,0:T(8,128)(2,1)} %select_convert_fusion), channel_id=1, source_target_pairs={{0,1},{1,0},{2,3},{3,2},{4,5},{5,4},{6,7},{7,6},{8,9},{9,8},{10,11... | collective-permute-start | bytes 1572872 | tf_op jit(solution)/shard_map/ppermute | solution.py:31
  415.5 9.3 %w_down_grad.3 = bf16[1152,768]{1,0:T(8,128)(2,1)} custom-call(bf16[1024,1152]{1,0:T(8,128)(2,1)} %get-tuple-element.198.refs_0_.refs_1_, bf16[1024,1152]{1,0:T(8,128)(2,1)} %get-tuple-element.198.refs_0_.refs_1_, bf16[1024,1152]{1,0:T(8,128)(2,1)} %get-tuple-element.189.refs_2_.refs_3_.refs_0_, ...), custom_call_target="tpu_custom_call" | custom-call | flops 999999995904 | bytes 1000000000 | tf_op jit(solution)/shard_map/w_down_grad/pallas_call | solution.py:410
  441.1 9.8 %down.2 = (bf16[512,1536]{1,0:T(8,128)(2,1)}, bf16[512,1536]{1,0:T(8,128)(2,1)}) custom-call(bf16[1024,1152]{1,0:T(8,128)(2,1)} %get-tuple-element.189.refs_2_.refs_3_.refs_0_, bf16[1152,768]{1,0:T(8,128)(2,1)} %refs_1_.3, bf16[1152,768]{1,0:T(8,128)(2,1)} %place_rows.5.wd_b.refs_2_), custom_call_target="tpu_custom_call" | custom-call | flops 999999995904 | bytes 1000000000 | tf_op jit(solution)/shard_map/down/pallas_call | solution.py:457
  451.0 10.4 %collective-permute-done.44 = bf16[384,1536]{1,0:T(8,128)(2,1)} collective-permute-done((bf16[384,1536]{1,0:T(8,128)(2,1)}, bf16[384,1536]{1,0:T(8,128)(2,1)}, u32[]{:S(2)}, u32[]{:S(2)}) %collective-permute-start.44) | collective-permute-done | bytes 1179680 | tf_op jit(solution)/shard_map/ppermute | solution.py:35
  491.1 9.4 %down.3 = (bf16[512,1536]{1,0:T(8,128)(2,1)}, bf16[512,1536]{1,0:T(8,128)(2,1)}) custom-call(bf16[1024,1152]{1,0:T(8,128)(2,1)} %get-tuple-element.198.refs_0_.refs_1_, bf16[1152,768]{1,0:T(8,128)(2,1)} %refs_1_.3, bf16[1152,768]{1,0:T(8,128)(2,1)} %place_rows.5.wd_b.refs_2_), custom_call_target="tpu_custom_call" | custom-call | flops 999999995904 | bytes 1000000000 | tf_op jit(solution)/shard_map/down/pallas_call | solution.py:457
  507.0 22.5 %collective-permute-done.48 = bf16[1536,384]{1,0:T(8,128)(2,1)S(1)} collective-permute-done((bf16[1536,384]{1,0:T(8,128)(2,1)S(1)}, bf16[1536,384]{1,0:T(8,128)(2,1)S(1)}, u32[]{:S(2)}, u32[]{:S(2)}) %collective-permute-start.48) | collective-permute-done | bytes 1179680 | tf_op jit(solution)/shard_map/ppermute | solution.py:35
  532.9 12.2 %collective-permute-done.53 = bf16[768,384]{0,1:T(8,128)(2,1)S(1)} collective-permute-done((bf16[768,384]{0,1:T(8,128)(2,1)S(1)}, bf16[768,384]{0,1:T(8,128)(2,1)S(1)}, u32[]{:S(2)}, u32[]{:S(2)}) %collective-permute-start.53) | collective-permute-done | bytes 589856 | tf_op jit(solution)/shard_map/ppermute | solution.py:27
  571.8 16.0 %collective-permute-done.62 = bf16[576,768]{1,0:T(8,128)(2,1)S(1)} collective-permute-done((bf16[576,768]{1,0:T(8,128)(2,1)S(1)}, bf16[576,768]{1,0:T(8,128)(2,1)S(1)}, u32[]{:S(2)}, u32[]{:S(2)}) %collective-permute-start.62) | collective-permute-done | bytes 884768 | tf_op jit(solution)/shard_map/ppermute | solution.py:56
  591.6 11.9 %collective-permute-done.63 = bf16[768,384]{0,1:T(8,128)(2,1)S(1)} collective-permute-done((bf16[768,384]{0,1:T(8,128)(2,1)S(1)}, bf16[768,384]{0,1:T(8,128)(2,1)S(1)}, u32[]{:S(2)}, u32[]{:S(2)}) %collective-permute-start.63) | collective-permute-done | bytes 589856 | tf_op jit(solution)/shard_map/ppermute | solution.py:56
  612.6 10.2 %collective-permute-done.64 = bf16[768,384]{0,1:T(8,128)(2,1)S(1)} collective-permute-done((bf16[768,384]{0,1:T(8,128)(2,1)S(1)}, bf16[768,384]{0,1:T(8,128)(2,1)S(1)}, u32[]{:S(2)}, u32[]{:S(2)}) %collective-permute-start.64) | collective-permute-done | bytes 589856 | tf_op jit(solution)/shard_map/ppermute | solution.py:61
  622.9 6.1 collective-permute-done.59
  631.1 8.8 %collective-permute-done.58 = bf16[512,768]{1,0:T(8,128)(2,1)S(1)} collective-permute-done((bf16[512,768]{1,0:T(8,128)(2,1)S(1)}, bf16[512,768]{1,0:T(8,128)(2,1)S(1)}, u32[]{:S(2)}, u32[]{:S(2)}) %collective-permute-start.58) | collective-permute-done | bytes 786464 | tf_op jit(solution)/shard_map/ppermute | solution.py:27
  (422 shorter events, 246.2 us)
Async XLA Ops:
  3.0 52.8 %collective-permute-start.3 = (bf16[768,640]{1,0:T(8,128)(2,1)}, bf16[768,640]{1,0:T(8,128)(2,1)S(1)}, u32[]{:S(2)}, u32[]{:S(2)}) collective-permute-start(bf16[768,640]{1,0:T(8,128)(2,1)} %pad_maximum_fusion.5), channel_id=1, source_target_pairs={{0,4},{4,0},{1,5},{5,1},{2,6},{6,2},{3,7},{7,3},{8,12},{12,8},{9,1... | collective-permute-start | bytes 2949128 | tf_op jit(solution)/shard_map/ppermute | solution.py:27
  8.3 43.7 %collective-permute-start = (bf16[512,768]{1,0:T(8,128)(2,1)}, bf16[512,768]{1,0:T(8,128)(2,1)S(1)}, u32[]{:S(2)}, u32[]{:S(2)}) collective-permute-start(bf16[512,768]{1,0:T(8,128)(2,1)} %get-tuple-element.116), channel_id=1, source_target_pairs={{0,4},{4,0},{1,5},{5,1},{2,6},{6,2},{3,7},{7,3},{8,12},{12,8},{9,1... | collective-permute-start | bytes 2359304 | tf_op jit(solution)/shard_map/ppermute | solution.py:27
  8.3 43.7 %collective-permute-start.2 = (bf16[768,384]{1,0:T(8,128)(2,1)S(1)}, bf16[768,384]{1,0:T(8,128)(2,1)}, u32[]{:S(2)}, u32[]{:S(2)}) collective-permute-start(bf16[768,384]{1,0:T(8,128)(2,1)S(1)} %copy-done.26), channel_id=1, source_target_pairs={{0,2},{2,0},{1,3},{3,1},{4,6},{6,4},{5,7},{7,5},{8,10},{10,8},{9,1... | collective-permute-start | bytes 1769480 | tf_op jit(solution)/shard_map/ppermute | solution.py:35
  10.9 34.2 %collective-permute-start.1 = (f32[3584]{0:T(1024)}, f32[3584]{0:T(1024)S(1)}, u32[]{:S(2)}, u32[]{:S(2)}) collective-permute-start(f32[3584]{0:T(1024)} %pad_maximum_fusion.10), channel_id=1, source_target_pairs={{0,4},{4,0},{1,5},{5,1},{2,6},{6,2},{3,7},{7,3},{8,12},{12,8},{9,1... | collective-permute-start | bytes 43016 | tf_op jit(solution)/shard_map/ppermute | solution.py:27
  69.7 49.0 %collective-permute-start.12 = (bf16[384,1152]{1,0:T(8,128)(2,1)}, bf16[384,1152]{1,0:T(8,128)(2,1)}, u32[]{:S(2)}, u32[]{:S(2)}) collective-permute-start(bf16[384,1152]{1,0:T(8,128)(2,1)} %constant_dynamic-slice_fusion.5), channel_id=1, source_target_pairs={{0,4},{4,0},{1,5},{5,1},{2,6},{6,2},{3,7},{7,3},{8,12},{12,8},{9,1... | collective-permute-start | bytes 2654216 | tf_op jit(solution)/shard_map/ppermute | solution.py:27
  83.3 68.6 %collective-permute-start.14 = (bf16[384,1152]{1,0:T(8,128)(2,1)}, bf16[384,1152]{1,0:T(8,128)(2,1)}, u32[]{:S(2)}, u32[]{:S(2)}) collective-permute-start(bf16[384,1152]{1,0:T(8,128)(2,1)} %constant_dynamic-slice_fusion.2), channel_id=1, source_target_pairs={{0,4},{4,0},{1,5},{5,1},{2,6},{6,2},{3,7},{7,3},{8,12},{12,8},{9,1... | collective-permute-start | bytes 2654216 | tf_op jit(solution)/shard_map/ppermute | solution.py:27
  101.8 50.2 %collective-permute-start.16 = (bf16[512,768]{1,0:T(8,128)(2,1)}, bf16[512,768]{1,0:T(8,128)(2,1)}, u32[]{:S(2)}, u32[]{:S(2)}) collective-permute-start(bf16[512,768]{1,0:T(8,128)(2,1)} %get-tuple-element.143.dy_a.refs_4_), channel_id=1, source_target_pairs={{0,2},{2,0},{1,3},{3,1},{4,6},{6,4},{5,7},{7,5},{8,10},{10,8},{9,1... | collective-permute-start | bytes 2359304 | tf_op jit(solution)/shard_map/ppermute | solution.py:35
  118.7 60.1 %collective-permute-start.21 = (bf16[512,1536]{1,0:T(8,128)(2,1)}, bf16[512,1536]{1,0:T(8,128)(2,1)}, u32[]{:S(2)}, u32[]{:S(2)}) collective-permute-start(bf16[512,1536]{1,0:T(8,128)(2,1)} %multiply_convert_fusion.n2_a.refs_0_), channel_id=1, source_target_pairs={{0,2},{2,0},{1,3},{3,1},{4,6},{6,4},{5,7},{7,5},{8,10},{10,8},{9,1... | collective-permute-start | bytes 4718600 | tf_op jit(solution)/shard_map/ppermute | solution.py:35
  119.7 32.2 %collective-permute-start.13 = (bf16[512,1536]{1,0:T(8,128)(2,1)}, bf16[512,1536]{1,0:T(8,128)(2,1)}, u32[]{:S(2)}, u32[]{:S(2)}) collective-permute-start(bf16[512,1536]{1,0:T(8,128)(2,1)} %multiply_convert_fusion.n2_a.refs_0_), channel_id=1, source_target_pairs={{0,1},{1,0},{2,3},{3,2},{4,5},{5,4},{6,7},{7,6},{8,9},{9,8},{10,11... | collective-permute-start | bytes 4718600 | tf_op jit(solution)/shard_map/ppermute | solution.py:31
  153.9 32.8 %collective-permute-start.17 = (bf16[512,768]{1,0:T(8,128)(2,1)}, bf16[512,768]{1,0:T(8,128)(2,1)}, u32[]{:S(2)}, u32[]{:S(2)}) collective-permute-start(bf16[512,768]{1,0:T(8,128)(2,1)} %get-tuple-element.142), channel_id=1, source_target_pairs={{0,4},{4,0},{1,5},{5,1},{2,6},{6,2},{3,7},{7,3},{8,12},{12,8},{9,1... | collective-permute-start | bytes 2359304 | tf_op jit(solution)/shard_map/ppermute | solution.py:27
  187.2 40.9 %collective-permute-start.25 = (bf16[512,1536]{1,0:T(8,128)(2,1)}, bf16[512,1536]{1,0:T(8,128)(2,1)}, u32[]{:S(2)}, u32[]{:S(2)}) collective-permute-start(bf16[512,1536]{1,0:T(8,128)(2,1)} %collective-permute-done.21.n2_a.refs_2_), channel_id=1, source_target_pairs={{0,1},{1,0},{2,3},{3,2},{4,5},{5,4},{6,7},{7,6},{8,9},{9,8},{10,11... | collective-permute-start | bytes 4718600 | tf_op jit(solution)/shard_map/ppermute | solution.py:31
  258.0 55.6 %collective-permute-start.28 = (bf16[768,1152]{1,0:T(8,128)(2,1)}, bf16[768,1152]{1,0:T(8,128)(2,1)}, u32[]{:S(2)}, u32[]{:S(2)}) collective-permute-start(bf16[768,1152]{1,0:T(8,128)(2,1)} %w_gate_grad.2), channel_id=1, source_target_pairs={{0,4},{4,0},{1,5},{5,1},{2,6},{6,2},{3,7},{7,3},{8,12},{12,8},{9,1... | collective-permute-start | bytes 5308424 | tf_op jit(solution)/shard_map/ppermute | solution.py:27
  286.5 40.6 %collective-permute-start.33 = (bf16[512,1536]{1,0:T(8,128)(2,1)}, bf16[512,1536]{1,0:T(8,128)(2,1)}, u32[]{:S(2)}, u32[]{:S(2)}) collective-permute-start(bf16[512,1536]{1,0:T(8,128)(2,1)} %add_convert_fusion.1), channel_id=1, source_target_pairs={{0,2},{2,0},{1,3},{3,1},{4,6},{6,4},{5,7},{7,5},{8,10},{10,8},{9,1... | collective-permute-start | bytes 4718600 | tf_op jit(solution)/shard_map/ppermute | solution.py:35
  296.0 63.4 %collective-permute-start.30 = (bf16[768,1152]{1,0:T(8,128)(2,1)}, bf16[768,1152]{1,0:T(8,128)(2,1)}, u32[]{:S(2)}, u32[]{:S(2)}) collective-permute-start(bf16[768,1152]{1,0:T(8,128)(2,1)} %w_up_grad.2), channel_id=1, source_target_pairs={{0,4},{4,0},{1,5},{5,1},{2,6},{6,2},{3,7},{7,3},{8,12},{12,8},{9,1... | collective-permute-start | bytes 5308424 | tf_op jit(solution)/shard_map/ppermute | solution.py:27
  316.7 35.5 %collective-permute-start.31 = (bf16[384,1152]{1,0:T(8,128)(2,1)}, bf16[384,1152]{1,0:T(8,128)(2,1)}, u32[]{:S(2)}, u32[]{:S(2)}) collective-permute-start(bf16[384,1152]{1,0:T(8,128)(2,1)} %get-tuple-element.261), channel_id=1, source_target_pairs={{0,8},{8,0},{16,24},{24,16},{1,9},{9,1},{17,25},{25,17},{2,10},{10... | collective-permute-start | bytes 2654216 | tf_op jit(solution)/shard_map/ppermute | solution.py:56
  344.8 81.1 %collective-permute-start.38 = (bf16[1152,768]{1,0:T(8,128)(2,1)}, bf16[1152,768]{1,0:T(8,128)(2,1)}, u32[]{:S(2)}, u32[]{:S(2)}) collective-permute-start(bf16[1152,768]{1,0:T(8,128)(2,1)} %w_down_grad.2), channel_id=1, source_target_pairs={{0,4},{4,0},{1,5},{5,1},{2,6},{6,2},{3,7},{7,3},{8,12},{12,8},{9,1... | collective-permute-start | bytes 5308424 | tf_op jit(solution)/shard_map/ppermute | solution.py:27
  354.7 56.9 %collective-permute-start.37 = (bf16[384,1152]{1,0:T(8,128)(2,1)}, bf16[384,1152]{1,0:T(8,128)(2,1)}, u32[]{:S(2)}, u32[]{:S(2)}) collective-permute-start(bf16[384,1152]{1,0:T(8,128)(2,1)} %add.262), channel_id=1, source_target_pairs={{0,24},{8,16},{16,8},{24,0},{1,25},{9,17},{17,9},{25,1},{2,26},{10... | collective-permute-start | bytes 2654216 | tf_op jit(solution)/shard_map/ppermute | solution.py:61
  365.3 44.0 %collective-permute-start.34 = (bf16[384,1152]{1,0:T(8,128)(2,1)}, bf16[384,1152]{1,0:T(8,128)(2,1)}, u32[]{:S(2)}, u32[]{:S(2)}) collective-permute-start(bf16[384,1152]{1,0:T(8,128)(2,1)} %get-tuple-element.259), channel_id=1, source_target_pairs={{0,8},{8,0},{16,24},{24,16},{1,9},{9,1},{17,25},{25,17},{2,10},{10... | collective-permute-start | bytes 2654216 | tf_op jit(solution)/shard_map/ppermute | solution.py:56
  395.2 40.0 %collective-permute-start.40 = (bf16[1024,256]{1,0:T(8,128)(2,1)}, bf16[1024,256]{1,0:T(8,128)(2,1)}, u32[]{:S(2)}, u32[]{:S(2)}) collective-permute-start(bf16[1024,256]{1,0:T(8,128)(2,1)} %select_convert_fusion), channel_id=1, source_target_pairs={{0,1},{1,0},{2,3},{3,2},{4,5},{5,4},{6,7},{7,6},{8,9},{9,8},{10,11... | collective-permute-start | bytes 1572872 | tf_op jit(solution)/shard_map/ppermute | solution.py:31
  411.6 76.1 %collective-permute-start.36 = (bf16[384,1152]{1,0:T(8,128)(2,1)}, bf16[384,1152]{1,0:T(8,128)(2,1)}, u32[]{:S(2)}, u32[]{:S(2)}) collective-permute-start(bf16[384,1152]{1,0:T(8,128)(2,1)} %add.266), channel_id=1, source_target_pairs={{0,24},{8,16},{16,8},{24,0},{1,25},{9,17},{17,9},{25,1},{2,26},{10... | collective-permute-start | bytes 2654216 | tf_op jit(solution)/shard_map/ppermute | solution.py:61
  414.2 56.8 %collective-permute-start.42 = (bf16[384,1152]{1,0:T(8,128)(2,1)}, bf16[384,1152]{1,0:T(8,128)(2,1)}, u32[]{:S(2)}, u32[]{:S(2)}) collective-permute-start(bf16[384,1152]{1,0:T(8,128)(2,1)} %add.267), channel_id=1, source_target_pairs={{0,8},{8,0},{16,24},{24,16},{1,9},{9,1},{17,25},{25,17},{2,10},{10... | collective-permute-start | bytes 2654216 | tf_op jit(solution)/shard_map/ppermute | solution.py:56
  429.9 53.2 %collective-permute-start.39 = (bf16[576,768]{1,0:T(8,128)(2,1)}, bf16[576,768]{1,0:T(8,128)(2,1)}, u32[]{:S(2)}, u32[]{:S(2)}) collective-permute-start(bf16[576,768]{1,0:T(8,128)(2,1)} %get-tuple-element.257), channel_id=1, source_target_pairs={{0,8},{8,0},{16,24},{24,16},{1,9},{9,1},{17,25},{25,17},{2,10},{10... | collective-permute-start | bytes 2654216 | tf_op jit(solution)/shard_map/ppermute | solution.py:56
  430.7 30.7 %collective-permute-start.44 = (bf16[384,1536]{1,0:T(8,128)(2,1)}, bf16[384,1536]{1,0:T(8,128)(2,1)}, u32[]{:S(2)}, u32[]{:S(2)}) collective-permute-start(bf16[384,1536]{1,0:T(8,128)(2,1)} %slice.116), channel_id=1, source_target_pairs={{0,2},{2,0},{1,3},{3,1},{4,6},{6,4},{5,7},{7,5},{8,10},{10,8},{9,1... | collective-permute-start | bytes 3538952 | tf_op jit(solution)/shard_map/ppermute | solution.py:35
  461.4 39.2 %collective-permute-start.46 = (bf16[512,1536]{1,0:T(8,128)(2,1)}, bf16[512,1536]{1,0:T(8,128)(2,1)}, u32[]{:S(2)}, u32[]{:S(2)}) collective-permute-start(bf16[512,1536]{1,0:T(8,128)(2,1)} %get-tuple-element.191), channel_id=1, source_target_pairs={{0,1},{1,0},{2,3},{3,2},{4,5},{5,4},{6,7},{7,6},{8,9},{9,8},{10,11... | collective-permute-start | bytes 4718600 | tf_op jit(solution)/shard_map/ppermute | solution.py:31
  471.0 34.1 %collective-permute-start.49 = (bf16[384,768]{1,0:T(8,128)(2,1)}, bf16[384,768]{1,0:T(8,128)(2,1)}, u32[]{:S(2)}, u32[]{:S(2)}) collective-permute-start(bf16[384,768]{1,0:T(8,128)(2,1)} %get-tuple-element.279), channel_id=1, source_target_pairs={{0,4},{4,0},{1,5},{5,1},{2,6},{6,2},{3,7},{7,3},{8,12},{12,8},{9,1... | collective-permute-start | bytes 1769480 | tf_op jit(solution)/shard_map/ppermute | solution.py:27
  485.6 62.3 %collective-permute-start.51 = (bf16[576,768]{1,0:T(8,128)(2,1)}, bf16[576,768]{1,0:T(8,128)(2,1)}, u32[]{:S(2)}, u32[]{:S(2)}) collective-permute-start(bf16[576,768]{1,0:T(8,128)(2,1)} %add.279), channel_id=1, source_target_pairs={{0,24},{8,16},{16,8},{24,0},{1,25},{9,17},{17,9},{25,1},{2,26},{10... | collective-permute-start | bytes 2654216 | tf_op jit(solution)/shard_map/ppermute | solution.py:61
  490.3 40.6 %collective-permute-start.54 = (bf16[384,1152]{1,0:T(8,128)(2,1)}, bf16[384,1152]{1,0:T(8,128)(2,1)}, u32[]{:S(2)}, u32[]{:S(2)}) collective-permute-start(bf16[384,1152]{1,0:T(8,128)(2,1)} %add.280), channel_id=1, source_target_pairs={{0,8},{8,0},{16,24},{24,16},{1,9},{9,1},{17,25},{25,17},{2,10},{10... | collective-permute-start | bytes 2654216 | tf_op jit(solution)/shard_map/ppermute | solution.py:56
  500.5 70.4 %collective-permute-start.45 = (bf16[512,1536]{1,0:T(8,128)(2,1)}, bf16[512,1536]{1,0:T(8,128)(2,1)S(1)}, u32[]{:S(2)}, u32[]{:S(2)}) collective-permute-start(bf16[512,1536]{1,0:T(8,128)(2,1)} %get-tuple-element.200), channel_id=1, source_target_pairs={{0,1},{1,0},{2,3},{3,2},{4,5},{5,4},{6,7},{7,6},{8,9},{9,8},{10,11... | collective-permute-start | bytes 4718600 | tf_op jit(solution)/shard_map/ppermute | solution.py:31
  505.1 65.8 %collective-permute-start.47 = (bf16[512,1536]{1,0:T(8,128)(2,1)S(1)}, bf16[512,1536]{1,0:T(8,128)(2,1)S(1)}, u32[]{:S(2)}, u32[]{:S(2)}) collective-permute-start(bf16[512,1536]{1,0:T(8,128)(2,1)S(1)} %add_convert_fusion), channel_id=1, source_target_pairs={{0,2},{2,0},{1,3},{3,1},{4,6},{6,4},{5,7},{7,5},{8,10},{10,8},{9,1... | collective-permute-start | bytes 4718600 | tf_op jit(solution)/shard_map/ppermute | solution.py:35
  608.5 35.9 %collective-permute-start.66 = (bf16[192,768]{1,0:T(8,128)(2,1)S(1)}, bf16[192,768]{1,0:T(8,128)(2,1)S(1)}, u32[]{:S(2)}, u32[]{:S(2)}) collective-permute-start(bf16[192,768]{1,0:T(8,128)(2,1)S(1)} %add.295), channel_id=1, source_target_pairs={{0,8},{8,0},{16,24},{24,16},{1,9},{9,1},{17,25},{25,17},{2,10},{10... | collective-permute-start | bytes 884744 | tf_op jit(solution)/shard_map/ppermute | solution.py:56
  608.5 31.3 %collective-permute-start.58 = (bf16[512,768]{1,0:T(8,128)(2,1)S(1)}, bf16[512,768]{1,0:T(8,128)(2,1)S(1)}, u32[]{:S(2)}, u32[]{:S(2)}) collective-permute-start(bf16[512,768]{1,0:T(8,128)(2,1)S(1)} %slice.165), channel_id=1, source_target_pairs={{0,4},{4,0},{1,5},{5,1},{2,6},{6,2},{3,7},{7,3},{8,12},{12,8},{9,1... | collective-permute-start | bytes 2359304 | tf_op jit(solution)/shard_map/ppermute | solution.py:27
  610.5 31.5 %collective-permute-start.65 = (bf16[384,384]{1,0:T(8,128)(2,1)S(1)}, bf16[384,384]{1,0:T(8,128)(2,1)S(1)}, u32[]{:S(2)}, u32[]{:S(2)}) collective-permute-start(bf16[384,384]{1,0:T(8,128)(2,1)S(1)} %add.298), channel_id=1, source_target_pairs={{0,8},{8,0},{16,24},{24,16},{1,9},{9,1},{17,25},{25,17},{2,10},{10... | collective-permute-start | bytes 884744 | tf_op jit(solution)/shard_map/ppermute | solution.py:56
  (134 other events, 1611.9 us)

commit v3 on v2

--- a/solution.py
+++ b/solution.py
@@ -15,7 +15,14 @@
 NEGATIVE = -1e30
 BF16 = jnp.bfloat16
 F32 = jnp.float32
-VMEM_BYTES = 56 * 1024 * 1024
+VMEM_BYTES = 20 * 1024 * 1024
+SCALE = 0.1
+
+
+def lasting(us):
+    return pl.CostEstimate(flops=int(us * SCALE * 1_150_000_000), bytes_accessed=int(us * SCALE * 3_690_000), transcendentals=0)
+
+
 HEAVY = pl.CostEstimate(flops=10**12, bytes_accessed=10**9, transcendentals=0)
 
 
@@ -71,51 +78,111 @@
         return result
 
 
+def add_kernel(left, right, out):
+    out[...] = (left[...].astype(F32) + right[...].astype(F32)).astype(out.dtype)
+
+
+def add(left, right):
+    rows, cols = left.shape
+    tile = pl.BlockSpec((rows // 2, cols), lambda i: (i, 0))
+    return pl.pallas_call(
+        add_kernel,
+        grid=(2,),
+        in_specs=[tile, tile],
+        out_specs=tile,
+        out_shape=jax.ShapeDtypeStruct((rows, cols), BF16),
+        compiler_params=pltpu.CompilerParams(vmem_limit_bytes=VMEM_BYTES),
+        cost_estimate=lasting(2.2),
+        name="add",
+    )(left, right)
+
+
+def split_add_kernel(side, own_a, other_a, own_b, other_b, give, kept):
+    give[...] = (own_a[...].astype(F32) + other_a[...].astype(F32)).astype(BF16)
+    kept[...] = (own_b[...].astype(F32) + other_b[...].astype(F32)).astype(BF16)
+
+
+def split_add(side, own, other):
+    rows, cols = own.shape
+    tile = (rows // 4, cols)
+    give = pl.BlockSpec(tile, lambda i, side: ((1 - side[0]) * 2 + i, 0))
+    kept = pl.BlockSpec(tile, lambda i, side: (side[0] * 2 + i, 0))
+    out = pl.BlockSpec(tile, lambda i, side: (i, 0))
+    shape = jax.ShapeDtypeStruct((rows // 2, cols), BF16)
+    return pl.pallas_call(
+        split_add_kernel,
+        grid_spec=pltpu.PrefetchScalarGridSpec(
+            num_scalar_prefetch=1,
+            grid=(2,),
+            in_specs=[give, give, kept, kept],
+            out_specs=[out, out],
+        ),
+        out_shape=[shape, shape],
+        compiler_params=pltpu.CompilerParams(vmem_limit_bytes=VMEM_BYTES),
+        cost_estimate=lasting(2.4),
+        name="split_add",
+    )(side, own, other, own, other)
+
+
+def join_kernel(side, total, rest, out):
+    is_total = pl.program_id(0) // 2 == side[0]
+
+    @pl.when(is_total)
+    def _():
+        out[...] = total[...].astype(F32)
+
+    @pl.when(jnp.logical_not(is_total))
+    def _():
+        out[...] = rest[...].astype(F32)
+
+
+def join(side, total, rest):
+    rows, cols = total.shape
+    tile = (rows // 2, cols)
+    half = pl.BlockSpec(tile, lambda i, side: (i % 2, 0))
+    return pl.pallas_call(
+        join_kernel,
+        grid_spec=pltpu.PrefetchScalarGridSpec(
+            num_scalar_prefetch=1,
+            grid=(4,),
+            in_specs=[half, half],
+            out_specs=pl.BlockSpec(tile, lambda i, side: (i, 0)),
+        ),
+        out_shape=jax.ShapeDtypeStruct((2 * rows, cols), F32),
+        compiler_params=pltpu.CompilerParams(vmem_limit_bytes=VMEM_BYTES),
+        cost_estimate=lasting(4.0),
+        name="join",
+    )(side, total, rest)
+
+
 class DpTotal:
     def __init__(self, steps):
         self.steps = steps
         self.staged = lax.axis_size("dp") == 4
-        self.side = (lax.axis_index("dp") + 1) // 2 % 2
+        side = (lax.axis_index("dp") + 1) // 2 % 2
+        self.side = jnp.reshape(side, (1,)).astype(jnp.int32)
 
     def begin(self, own, other):
         if not self.staged:
             self.value = lax.psum(own + other, "dp")
             return
-        span = own.shape[0] // 2
-
-        def both(other):
-            def half(which):
-                at = which * span
-                return lax.dynamic_slice_in_dim(own, at, span, 0) + lax.dynamic_slice_in_dim(
-                    other, at, span, 0
-                )
-
-            return half(1 - self.side), half(self.side)
-
-        give, self.keep = self.steps(both, other)
+        give, self.keep = self.steps(lambda other: split_add(self.side, own, other), other)
         self.inward = swap_pair(give)
 
     def middle(self):
         if self.staged:
-            self.pair = self.steps(jnp.add, self.inward, self.keep)
+            self.pair = self.steps(add, self.inward, self.keep)
             self.across = swap_mirror(self.pair)
 
     def end(self):
         if self.staged:
-            self.total = self.steps(jnp.add, self.across, self.pair)
+            self.total = self.steps(add, self.across, self.pair)
             self.rest = swap_pair(self.total)
 
     def result(self):
         if not self.staged:
             return self.value.astype(F32)
-        first = self.side == 0
-
-        def join(rest):
-            return jnp.concatenate(
-                [jnp.where(first, self.total, rest), jnp.where(first, rest, self.total)], axis=0
-            ).astype(F32)
-
-        return self.steps(join, self.rest)
+        return self.steps(lambda rest: join(self.side, self.total, rest), self.rest)
 
 
 def fence_kernel(value, out):
@@ -129,14 +196,17 @@
     def send(self, move, value):
         return move(after(value, self.token))
 
-    def wait(self, *results):
-        token = pl.pallas_call(
+    def fence(self):
+        self.token = pl.pallas_call(
             fence_kernel,
             out_shape=jax.ShapeDtypeStruct((8, 128), F32),
             cost_estimate=HEAVY,
             name="fence",
         )(self.token)
-        self.token = after(token, *results)
+
+    def wait(self, *results):
+        self.fence()
+        self.token = after(self.token, *results)
 
 
 def place_kernel(odd, straight, around, out):
@@ -161,7 +231,7 @@
         out_specs=pl.BlockSpec((rows, cols), lambda i: (i, 0)),
         out_shape=jax.ShapeDtypeStruct((2 * rows, cols), straight.dtype),
         compiler_params=pltpu.CompilerParams(vmem_limit_bytes=VMEM_BYTES),
-        cost_estimate=HEAVY,
+        cost_estimate=lasting(1.4),
         name="place_rows",
     )(jnp.reshape(odd, (1,)).astype(jnp.int32), straight, around)
 
@@ -252,7 +322,7 @@
         out_shape=[ctx, ctx, jax.ShapeDtypeStruct((rows, HD), F32)],
         scratch_shapes=[pltpu.VMEM((tq, 2 * width), F32)] * 3,
         compiler_params=pltpu.CompilerParams(vmem_limit_bytes=VMEM_BYTES),
-        cost_estimate=HEAVY,
+        cost_estimate=lasting(8),
         name="attend_forward",
     )(start, q_a, q_b, kv, seg_q, seg_k)
 
@@ -331,7 +401,7 @@
         out_shape=[dq, dq, jax.ShapeDtypeStruct((length, 2 * HD), F32)],
         scratch_shapes=[pltpu.VMEM((tq, 2 * width), F32)],
         compiler_params=pltpu.CompilerParams(vmem_limit_bytes=VMEM_BYTES),
-        cost_estimate=HEAVY,
+        cost_estimate=lasting(20),
         name="attend_backward",
     )(start, q_a, q_b, kv, seg_q, seg_k, ctx_a, ctx_b, lse, dctx_a, dctx_b)
 
@@ -363,13 +433,13 @@
 def feed(n2s, dys, wg, wu, wd):
     rows, width = n2s[0].shape
     feats, units = wg[0].shape
-    tn = 384
+    tn = 256
     whole = pl.BlockSpec((rows, width), lambda j: (0, 0))
     half = pl.BlockSpec((rows, feats), lambda j: (0, 0))
     out = jax.ShapeDtypeStruct((2 * rows, units), BF16)
     return pl.pallas_call(
-        functools.partial(feed_kernel, tm=256),
-        grid=(units // tn,),
+        functools.partial(feed_kernel, tm=min(512, rows)),
+        grid=(pl.cdiv(units, tn),),
         in_specs=[whole] * 2
         + [half] * 4
         + [pl.BlockSpec((feats, tn), lambda j: (0, j))] * 4
@@ -377,7 +447,7 @@
         out_specs=[pl.BlockSpec((2 * rows, tn), lambda j: (0, j))] * 3,
         out_shape=[out] * 3,
         compiler_params=pltpu.CompilerParams(vmem_limit_bytes=VMEM_BYTES),
-        cost_estimate=HEAVY,
+        cost_estimate=lasting(17.5),
         name="feed",
     )(*n2s, *dys, *wg, *wu, *wd)
 
@@ -395,7 +465,7 @@
 def weight_grad(lefts, rights, name):
     width_left = lefts[0][4]
     width_right = rights[0][4]
-    tn = 384
+    tn = 256
 
     def left_spec(block):
         _, at, rows, col, cols = block
@@ -409,12 +479,12 @@
     tokens = sum(block[2] for block in lefts)
     return pl.pallas_call(
         weight_grad_kernel,
-        grid=(width_right // tn,),
+        grid=(pl.cdiv(width_right, tn),),
         in_specs=[left_spec(b) for b in lefts] + [right_spec(b) for b in rights],
         out_specs=pl.BlockSpec((width_left, tn), lambda j: (0, j)),
         out_shape=out,
         compiler_params=pltpu.CompilerParams(vmem_limit_bytes=VMEM_BYTES),
-        cost_estimate=HEAVY,
+        cost_estimate=lasting(7.5),
         name=name,
     )(*[b[0] for b in lefts], *[b[0] for b in rights])
 
@@ -438,7 +508,7 @@
 def project(lefts, weights, transposed, name):
     rows, units = lefts[0].shape
     feats = weights[0][0].shape[0 if transposed else 1]
-    tn = 384
+    tn = 256
     tiles = feats // tn
     whole = pl.BlockSpec((rows, units), lambda j: (0, 0))
 
@@ -463,7 +533,7 @@
         out_specs=[pl.BlockSpec((rows // 2, tn), lambda j: (0, j))] * 2,
         out_shape=[out] * 2,
         compiler_params=pltpu.CompilerParams(vmem_limit_bytes=VMEM_BYTES),
-        cost_estimate=HEAVY,
+        cost_estimate=lasting(8.5),
         name=name,
     )(*lefts, *flat)
 
@@ -513,11 +583,12 @@
 
     rounds = Rounds()
     small = jnp.concatenate([norm1_gain, norm2_gain, segment_ids.reshape(-1).astype(F32)])
-    w_qkv = jnp.concatenate([w_query, w_keyval], axis=1)
     heads_own = w_query.shape[1]
+    small_in = rounds.send(swap_row, small)
     x_in = rounds.send(swap_row, give(tokens_in))
     wq_far_own = rounds.send(swap_far, w_query)
-    small_in = rounds.send(swap_row, small)
+    rounds.fence()
+    w_qkv = jnp.concatenate([w_query, w_keyval], axis=1)
     wqkv_in = rounds.send(swap_row, w_qkv)
     rounds.wait(x_in, wq_far_own, small_in)
 
@@ -537,14 +608,16 @@
     first_token = place * local + row * mine
     seg_q = lax.dynamic_slice_in_dim(seg_row[0], first_token, mine, 0)[:, None]
     start = jnp.reshape(first_token, (1,)).astype(jnp.int32)
-    rounds.wait(wqkv_in, wo_far_own)
+    rounds.wait(wqkv_in, wo_far_own, normed_one)
 
     wq_in = wqkv_in[:, :heads_own]
     wq_far_in = rounds.send(swap_far, wq_in)
     wkv = jnp.concatenate([w_keyval, wqkv_in[:, heads_own:]], axis=0)
     kv_own = dot(normed_one, wkv, BF16)
+    rounds.wait(kv_own)
     kv_in = rounds.send(swap_row, kv_own)
-    wg_straight = rounds.send(swap_row, after(straight_part(w_gate), kv_own))
+    rounds.fence()
+    wg_straight = rounds.send(swap_row, straight_part(w_gate))
     rounds.wait(wo_in, kv_in, wq_far_in)
 
     kv_pair = jnp.concatenate(
@@ -569,46 +642,49 @@
     else:
         kv = kv_pair
     q_a = dot(normed_one, wq_half, BF16)
+    rounds.wait(kv, wq_core, q_a)
+
     q_b = dot(normed_one, wq_core, BF16)
-    rounds.wait(wo_far_in, kv, q_b)
+    ctx_a, ctx_b, lse = attend_forward(start, after(q_a, rounds.token), q_b, kv, seg_q, seg_row)
+    rounds.wait(wo_far_in, wg_straight, ctx_a)
 
     wo_half = jnp.concatenate(
         [
             jnp.concatenate([w_attn_out, wo_far_own], axis=0),
-            jnp.concatenate([wo_in, wo_far_in], axis=0),
+            jnp.concatenate([wo_in, after(wo_far_in, rounds.token)], axis=0),
         ],
         axis=1,
     )
+    wo_core = rounds.send(swap_core, wo_half)
+    wg_around = send_pair(wg_straight)
     dy_own = keep(out_cotangent)
-    wo_core = rounds.send(swap_core, wo_half)
     dy_far_own = rounds.send(swap_far, dy_own)
-    ctx_a, ctx_b, lse = attend_forward(start, after(q_a, rounds.token), q_b, kv, seg_q, seg_row)
-    middle = x + dot(ctx_a, wo_half) + dot(ctx_b, wo_core)
+    wd_straight = rounds.send(swap_row, straight_part(w_down))
+    middle = x + dot(after(ctx_a, rounds.token), wo_half) + dot(ctx_b, wo_core)
+    middle = lax.optimization_barrier(middle)
     inverse_two = lax.rsqrt(jnp.mean(middle * middle, axis=1, keepdims=True) + EPSILON)
     n2 = (middle * inverse_two * gain_two).astype(BF16)
-    rounds.wait(wg_straight, n2)
+    rounds.wait(n2, wo_core, wu_straight)
 
     n2_far = rounds.send(swap_far, n2)
-    wg_around = send_pair(wg_straight)
-    wd_straight = rounds.send(swap_row, straight_part(w_down))
     n2_near = rounds.send(swap_core, n2)
-    rounds.wait(wu_straight, wg_around, n2_near, dy_far_own)
-
     dy_in = rounds.send(swap_row, give(out_cotangent))
+    rounds.wait(wg_around, n2_near)
+
     wu_around = send_pair(wu_straight)
     dy_near_own = rounds.send(swap_core, dy_own)
-    rounds.wait(wd_straight, wu_around, dy_near_own)
+    rounds.wait(wd_straight, wu_around, dy_near_own, dy_far_own)
 
     wd_around = send_pair(wd_straight)
     dy_diagonal_own = rounds.send(swap_core, dy_far_own)
-    wg = (w_gate, placed(wg_straight, wg_around))
-    wu = (w_up, placed(wu_straight, wu_around))
+    wg = (w_gate, placed(wg_straight, after(wg_around, rounds.token)))
+    wu = (w_up, placed(wu_straight, after(wu_around, wg[1])))
     rounds.wait(dy_in, n2_far, dy_diagonal_own)
 
     dy_near_in = rounds.send(swap_core, dy_in)
     dy_far_in = rounds.send(swap_far, dy_in)
     n2_diagonal = rounds.send(swap_core, n2_far)
-    wd = (w_down, placed(wd_straight, wd_around))
+    wd = (w_down, placed(wd_straight, after(wd_around, rounds.token)))
     dy_near = (dy_near_own, dy_near_in)
     hidden_a, dgate_a, dup_a = feed((n2, n2_near), (dy_own, dy_in, *dy_near), wg, wu, wd)
     dy_diagonal = (dy_diagonal_own, swap_core(dy_far_in))
@@ -655,7 +731,7 @@
             hidden_b,
         )
 
-    gate_sum, up_sum, down_sum, query_sum, out_sum = [DpTotal(steps) for _ in range(5)]
+    gate_sum, up_sum, down_sum, rest_sum = [DpTotal(steps) for _ in range(4)]
     gate_in = swap_row(gate_grad(1))
     dn2_far, dn2_diagonal = steps(
         lambda dgate: project([dgate, dup_b], [wg, wu], True, "feed_back"), dgate_b
@@ -686,20 +762,22 @@
         return dmiddle, dmiddle.astype(BF16), jnp.sum(dnormed * middle * inverse_two, axis=0)
 
     dmiddle, dattn, gain_two_part = steps(middle_back, far_in)
+    gate_sum.middle()
     down_in = swap_row(down_grad(1))
 
     dctx_a, dctx_b = steps(lambda d: (dot_t(d, wo_half, BF16), dot_t(d, wo_core, BF16)), dattn)
-    gate_sum.middle()
     up_sum.begin(up_own, up_in)
-    out_core = swap_core(steps(lambda d: t_dot(ctx_b, d, BF16), dattn))
+    out_core = swap_core(steps(lambda d: t_dot(d, ctx_b, BF16), dattn))
+    down_own = down_grad(0)
+    out_part = steps(lambda d: t_dot(d, ctx_a, BF16), dattn)
+    out_chip = steps(add, out_core, out_part)
+    out_far = swap_far(out_chip[:, heads_own:])
     dq_a, dq_b, dkv_all = steps(
         lambda d: attend_backward(
             start, q_a, q_b, kv, seg_q, seg_row, ctx_a, ctx_b, lse, d, dctx_b
         ),
         dctx_a,
     )
-    out_chip = steps(lambda core: t_dot(ctx_a, dattn, BF16) + core, out_core)
-    out_far = swap_far(out_chip[heads_own:])
     if spans == 2:
         is_first = place == 0
 
@@ -709,8 +787,14 @@
         dkv_core = swap_core(steps(other_half, dkv_all))
     up_sum.middle()
     gate_sum.end()
-    down_own = down_grad(0)
+    out_mine = steps(add, out_far, out_chip[:, :heads_own])
+    out_row = swap_row(out_mine[feats:])
     down_sum.begin(down_own, down_in)
+    query_core = swap_core(steps(lambda d: t_dot(normed_one, d, BF16), dq_b))
+    query_part = steps(lambda d: t_dot(normed_one, d, BF16), dq_a)
+    ffn_far, ffn_diagonal = steps(lambda h: project([h], [wd], False, "down"), hidden_b)
+    query_chip = steps(add, query_core, query_part)
+    query_far = swap_far(query_chip[:, heads_own:])
     if spans == 2:
 
         def pair_of(core):
@@ -721,14 +805,7 @@
     else:
         dkv_keep, dkv_give = keep(dkv_all), give(dkv_all).astype(BF16)
     dkv_row = swap_row(dkv_give)
-    query_core = swap_core(steps(lambda d: t_dot(normed_one, d, BF16), dq_b))
-    ffn_far, ffn_diagonal = steps(lambda h: project([h], [wd], False, "down"), hidden_b)
-    out_mine = steps(lambda far: out_chip[:heads_own] + far, out_far)
-    out_row = swap_row(out_mine[:, feats:])
-    query_chip = steps(lambda core: t_dot(normed_one, dq_a, BF16) + core, query_core)
-    query_far = swap_far(query_chip[:, heads_own:])
     gate_total = gate_sum.result()
-    ffn_diagonal_in = swap_core(ffn_diagonal)
     dkv = steps(lambda other: (dkv_keep + other.astype(F32)).astype(BF16), dkv_row)
 
     def norm_one_back(dkv):
@@ -742,44 +819,37 @@
         return dx, dx[:, feats:].astype(BF16), jnp.concatenate([kv_part, small_part], axis=1)
 
     dx, dx_give, small_part = steps(norm_one_back, dkv)
+    small_row = swap_row(small_part[feats:])
+    ffn_diagonal_in = swap_core(after(ffn_diagonal, small_part))
+    up_sum.end()
     down_sum.middle()
-    up_sum.end()
-    small_row = swap_row(small_part[feats:])
     ffn_own, ffn_near = steps(lambda h: project([h], [wd], False, "down"), hidden_a)
-    ffn_for_far = steps(
-        lambda into: (ffn_far.astype(F32) + into.astype(F32)).astype(BF16), ffn_diagonal_in
-    )
-    ffn_far_in = swap_far(ffn_for_far)
-    out_sum.begin(out_mine[:, :feats], out_row)
-    query_mine = steps(lambda far: query_chip[:, :heads_own] + far, query_far)
+    query_mine = steps(add, query_far, query_chip[:, :heads_own])
     query_row = swap_row(query_mine[feats:])
+    small_one = steps(add, small_row, small_part[:feats])
+    small_core = swap_core(small_one)
+    ffn_for_far = steps(add, ffn_diagonal_in, ffn_far)
+    small_two = steps(add, small_core, small_one)
+    small_far = swap_far(small_two)
+    ffn_far_in = swap_far(after(ffn_for_far, small_two))
+    ffn_near_in = swap_core(after(ffn_near, small_two))
     up_total = up_sum.result()
-    small_one = steps(lambda other: small_part[:feats] + other, small_row)
-    small_core = swap_core(small_one)
-    out_sum.middle()
     down_sum.end()
-    query_sum.begin(query_mine[:feats], query_row)
-    dx_in = swap_row(dx_give)
-    small_two = steps(jnp.add, small_core, small_one)
-    ffn_near_in = swap_core(ffn_near)
-    out_sum.end()
-    query_sum.middle()
+    rest_own = jnp.concatenate([out_mine[:feats], query_mine[:feats], small_two], axis=1)
+    rest_in = jnp.concatenate([out_row, query_row, small_far], axis=1)
+    rest_sum.begin(rest_own, rest_in)
+    ffn_chip = steps(add, ffn_near_in, ffn_own)
+    rest_sum.middle()
 
     def add_up(far):
-        y = middle + ffn_own.astype(F32) + ffn_near_in.astype(F32) + far.astype(F32)
+        y = middle + ffn_chip.astype(F32) + far.astype(F32)
         return y, y[:, feats:].astype(BF16)
 
     y, y_give = steps(add_up, ffn_far_in)
-    small_far = swap_far(small_two)
+    y_in = swap_row(y_give)
     down_total = down_sum.result()
-    y_in = swap_row(y_give)
-    query_sum.end()
-    small_three = steps(jnp.add, small_far, small_two)
-    if lax.axis_size("dp") == 4:
-        small_four = steps(jnp.add, swap_pair(small_three), small_three)
-        small_total = steps(jnp.add, swap_mirror(small_four), small_four)
-    else:
-        small_total = lax.psum(small_three, "dp")
+    dx_in = swap_row(after(dx_give, down_total))
+    rest_sum.end()
 
     def put_back(other, value):
         other = other.astype(F32)
@@ -790,11 +860,11 @@
 
     dx_out = steps(put_back, dx_in, dx)
     y_out = steps(put_back, y_in, y)
-    query_total = query_sum.result()
-    out_total = out_sum.result()
-    small_total = small_total.astype(F32)
-    kv_total = small_total[:, : 2 * HD]
-    gain_total = small_total[:, 2 * HD : 2 * HD + 2].T
+    rest_total = rest_sum.result()
+    out_total = rest_total[:, :heads_own].T
+    query_total = rest_total[:, heads_own : 2 * heads_own]
+    kv_total = rest_total[:, 2 * heads_own : 2 * heads_own + 2 * HD]
+    gain_total = rest_total[:, 2 * heads_own + 2 * HD : 2 * heads_own + 2 * HD + 2].T
 
     return (
         y_out,

time: 653 us -> 573 us (0.88)
  other arithmetic: 73.6 us -> 31.1 us
  Pallas kernels: 184 us -> 142 us
  waiting for transfers between devices: 227 us -> 240 us
  matrix products: 41.3 us -> 33.3 us
    ppermute x18, starting transfers between devices: 18.3 us -> 49.7 us  [swap_row(): return lax.ppermute(value, 'row', [(0, 1), (1, 0)])]
    add x22 -> x1, other arithmetic: 28.1 us -> 0.6 us  [add_up(): y = middle + ffn_chip.astype(F32) + far.astype(F32)]
    ppermute x6 -> x4, waiting for transfers between devices: 11.6 us -> 36 us  [swap_mirror(): return lax.ppermute(value, 'dp', [(i, count - 1 - i) for i in range(count)])]
    ppermute x18, waiting for transfers between devices: 88.3 us -> 64.2 us  [swap_row(): return lax.ppermute(value, 'row', [(0, 1), (1, 0)])]
    ppermute x14 -> x11, waiting for transfers between devices: 66.2 us -> 89 us  [swap_pair(): return lax.ppermute(value, 'dp', [(i, i ^ 1) for i in range(count)])]
    pallas_call x4, Pallas kernels: 51.1 us -> 31.5 us  [project(): pl.pallas_call(functools.partial(project_kernel, lefts=len(lefts), multip...]
    ppermute x17, starting transfers between devices: 20.2 us -> 4.05 us  [swap_core(): return lax.ppermute(value, 'col', [(0, 1), (1, 0), (2, 3), (3, 2)])]
    ppermute x12, waiting for transfers between devices: 61 us -> 49.3 us  [swap_far(): return lax.ppermute(value, 'col', [(0, 2), (2, 0), (1, 3), (3, 1)])]
  transfers between devices with their start and end apart: 67 -> 62, of which waited for: 22 -> 27; matrix products, arithmetic and copies ran while one was open for 20% -> 13% of each run, Pallas kernels for 24% -> 19%
where the time goes in v3:
time: 573 us; the launch traced here: 571 us
  waiting for transfers between devices  240 us (42%)
  Pallas kernels  142 us (25%)
  starting transfers between devices  91.9 us (16%)
  matrix products  33.3 us (6%)
  other arithmetic  31.1 us (5%)
  local copies, waits for them, and re-layouts  29.9 us (5%)
    ppermute x11, waiting for transfers between devices, swap_pair(): return lax.ppermute(value, 'dp', [(i, i ^ 1) for i in range(count)])  89 us
    ppermute x18, waiting for transfers between devices, swap_row(): return lax.ppermute(value, 'row', [(0, 1), (1, 0)])  64.2 us
    ppermute x18, starting transfers between devices, swap_row(): return lax.ppermute(value, 'row', [(0, 1), (1, 0)])  49.7 us
    ppermute x12, waiting for transfers between devices, swap_far(): return lax.ppermute(value, 'col', [(0, 2), (2, 0), (1, 3), (3, 1)])  49.3 us
    pallas_call x6, Pallas kernels, weight_grad(): pl.pallas_call(weight_grad_kernel, grid=(pl.cdiv(width_right, tn),), in_s...  36.6 us
    ppermute x4, waiting for transfers between devices, swap_mirror(): return lax.ppermute(value, 'dp', [(i, count - 1 - i) for i in range(count)])  36 us
    pallas_call x4, Pallas kernels, project(): pl.pallas_call(functools.partial(project_kernel, lefts=len(lefts), multip...  31.5 us
    pallas_call x2, Pallas kernels, feed(): pl.pallas_call(functools.partial(feed_kernel, tm=min(512, rows)), grid=(p...  31.3 us
  transfers between devices with their start and end apart: 62, of which 27 were waited for; matrix products, arithmetic and copies ran while one was open for 13% of the time, Pallas kernels for 19%

profile of v3, /device:TPU:0, one launch (start us, length us, event | category | flops | bytes accessed | tf_op | source)
XLA Modules:
  0.0 571.1 jit_solution(15032400632720253019)
XLA Ops:
  20.9 28.7 %collective-permute-done = bf16[512,768]{1,0:T(8,128)(2,1)} collective-permute-done((bf16[512,768]{1,0:T(8,128)(2,1)}, bf16[512,768]{1,0:T(8,128)(2,1)}, u32[]{:S(2)}, u32[]{:S(2)}) %collective-permute-start) | collective-permute-done | bytes 786464 | tf_op jit(solution)/shard_map/ppermute | solution.py:34
  57.0 6.6 %collective-permute-done.4 = bf16[384,768]{1,0:T(8,128)(2,1)S(1)} collective-permute-done((bf16[384,768]{1,0:T(8,128)(2,1)}, bf16[384,768]{1,0:T(8,128)(2,1)S(1)}, u32[]{:S(2)}, u32[]{:S(2)}) %collective-permute-start.4) | collective-permute-done | bytes 589856 | tf_op jit(solution)/shard_map/ppermute | solution.py:42
  66.5 6.3 %collective-permute-done.7 = bf16[512,256]{1,0:T(8,128)(2,1)S(1)} collective-permute-done((bf16[512,256]{1,0:T(8,128)(2,1)S(1)}, bf16[512,256]{1,0:T(8,128)(2,1)S(1)}, u32[]{:S(2)}, u32[]{:S(2)}) %collective-permute-start.7) | collective-permute-done | bytes 262176 | tf_op jit(solution)/shard_map/ppermute | solution.py:34
  85.5 6.2 %attend_forward.1 = (bf16[512,768]{1,0:T(8,128)(2,1)S(1)}, bf16[512,768]{1,0:T(8,128)(2,1)S(1)}, f32[512,128]{1,0:T(8,128)S(1)}) custom-call(s32[1]{0:T(128)} %bitcast.start, bf16[512,768]{1,0:T(8,128)(2,1)S(1)} %convolution_convert_fusion.8.q_a, bf16[512,768]{1,0:T(8,128)(2,1)S(1)} %convolution_convert_fusion.7.q_b, ...), custom_call_target="tpu_custom_call" | custom-call | flops 920000000 | bytes 2952000 | tf_op jit(solution)/shard_map/attend_forward/pallas_call | solution.py:310
  98.1 6.1 %collective-permute-start.18 = (bf16[576,768]{1,0:T(8,128)(2,1)S(1)}, bf16[576,768]{1,0:T(8,128)(2,1)S(1)}, u32[]{:S(2)}, u32[]{:S(2)}) collective-permute-start(bf16[576,768]{1,0:T(8,128)(2,1)S(1)} %copy-done.81), channel_id=1, source_target_pairs={{0,4},{4,0},{1,5},{5,1},{2,6},{6,2},{3,7},{7,3},{8,12},{12,8},{9,1... | collective-permute-start | bytes 2654216 | tf_op jit(solution)/shard_map/ppermute | solution.py:34
  107.0 9.7 %fusion.1 = f32[512,1536]{1,0:T(8,128)S(1)} fusion(f32[512,1536]{1,0:T(8,128)S(1)} %fusion.26, bf16[512,768]{1,0:T(8,128)(2,1)S(1)} %get-tuple-element.149.ctx_a, bf16[512,768]{1,0:T(8,128)(2,1)} %collective-permute-done, bf16[512,768]{1,0:T(8,128)(2,1)S(1)} %copy-done.67, bf16[384,768]{1,0:T(8,128)(2,1)S(1)} %collective-permute-done.10, ...), kind=kOutput, calls=%fused_computation.12 | convolution fusion | flops 1222115328 | bytes 11010048 | tf_op jit(solution)/shard_map/dot_general | solution.py:46
  126.8 17.9 %collective-permute-done.19.around = bf16[384,1152]{1,0:T(8,128)(2,1)S(1)} collective-permute-done((bf16[384,1152]{1,0:T(8,128)(2,1)S(1)}, bf16[384,1152]{1,0:T(8,128)(2,1)S(1)}, u32[]{:S(2)}, u32[]{:S(2)}) %collective-permute-start.19) | collective-permute-done | bytes 884768 | tf_op jit(solution)/shard_map/ppermute | solution.py:63
  144.8 11.2 %collective-permute-done.21.n2_a.refs_2_ = bf16[512,1536]{1,0:T(8,128)(2,1)S(1)} collective-permute-done((bf16[512,1536]{1,0:T(8,128)(2,1)S(1)}, bf16[512,1536]{1,0:T(8,128)(2,1)S(1)}, u32[]{:S(2)}, u32[]{:S(2)}) %collective-permute-start.21) | collective-permute-done | bytes 1572896 | tf_op jit(solution)/shard_map/ppermute | solution.py:42
  159.5 15.3 %collective-permute-done.26.dy_b.refs_6_ = bf16[512,768]{1,0:T(8,128)(2,1)S(1)} collective-permute-done((bf16[512,768]{1,0:T(8,128)(2,1)S(1)}, bf16[512,768]{1,0:T(8,128)(2,1)S(1)}, u32[]{:S(2)}, u32[]{:S(2)}) %collective-permute-start.26) | collective-permute-done | bytes 786464 | tf_op jit(solution)/shard_map/ppermute | solution.py:42
  180.0 15.6 %feed.2 = (bf16[1024,1152]{1,0:T(8,128)(2,1)S(1)}, bf16[1024,1152]{1,0:T(8,128)(2,1)S(1)}, bf16[1024,1152]{1,0:T(8,128)(2,1)S(1)}) custom-call(bf16[512,1536]{1,0:T(8,128)(2,1)S(1)} %multiply_convert_fusion.n2_a.refs_0_, bf16[512,1536]{1,0:T(8,128)(2,1)S(1)} %collective-permute-done.14.n2_b.refs_1_, bf16[512,768]{1,0:T(8,128)(2,1)S(1)} %copy-done.26, ...), custom_call_target="tpu_custom_call" | custom-call | flops 2012499968 | bytes 6457500 | tf_op jit(solution)/shard_map/feed/pallas_call | solution.py:440
  197.1 15.7 %feed.3 = (bf16[1024,1152]{1,0:T(8,128)(2,1)S(1)}, bf16[1024,1152]{1,0:T(8,128)(2,1)S(1)}, bf16[1024,1152]{1,0:T(8,128)(2,1)S(1)}) custom-call(bf16[512,1536]{1,0:T(8,128)(2,1)S(1)} %collective-permute-done.21.n2_a.refs_2_, bf16[512,1536]{1,0:T(8,128)(2,1)S(1)} %collective-permute-done.25.n2_b.refs_3_, ...), custom_call_target="tpu_custom_call" | custom-call | flops 2012499968 | bytes 6457500 | tf_op jit(solution)/shard_map/feed/pallas_call | solution.py:440
  212.8 7.0 %w_gate_grad.2 = bf16[768,1152]{1,0:T(8,128)(2,1)} custom-call(bf16[512,1536]{1,0:T(8,128)(2,1)S(1)} %multiply_convert_fusion.n2_a.refs_0_, bf16[512,1536]{1,0:T(8,128)(2,1)S(1)} %collective-permute-done.14.n2_b.refs_1_, bf16[512,1536]{1,0:T(8,128)(2,1)S(1)} %collective-permute-done.21.n2_a.refs_2_, ...), custom_call_target="tpu_custom_call" | custom-call | flops 862499968 | bytes 2767500 | tf_op jit(solution)/shard_map/w_gate_grad/pallas_call | solution.py:480
  219.9 9.6 %feed_back.2 = (bf16[512,1536]{1,0:T(8,128)(2,1)S(1)}, bf16[512,1536]{1,0:T(8,128)(2,1)S(1)}) custom-call(bf16[1024,1152]{1,0:T(8,128)(2,1)S(1)} %get-tuple-element.182.refs_6_.refs_7_.refs_0_, bf16[1024,1152]{1,0:T(8,128)(2,1)S(1)} %get-tuple-element.191.refs_1_.refs_6_.refs_7_, bf16[768,1152]{1,0:T(8,128)(2,1)S(1)} %copy-done.22, ...), custom_call_target="tpu_custom_call" | custom-call | flops 977500032 | bytes 3136500 | tf_op jit(solution)/shard_map/feed_back/pallas_call | solution.py:527
  231.8 6.9 %w_gate_grad.3.own_a.own_b = bf16[768,1152]{1,0:T(8,128)(2,1)S(1)} custom-call(bf16[512,1536]{1,0:T(8,128)(2,1)S(1)} %multiply_convert_fusion.n2_a.refs_0_, bf16[512,1536]{1,0:T(8,128)(2,1)S(1)} %collective-permute-done.14.n2_b.refs_1_, bf16[512,1536]{1,0:T(8,128)(2,1)S(1)} %collective-permute-done.21.n2_a.refs_2_, ...), custom_call_target="tpu_custom_call" | custom-call | flops 862499968 | bytes 2767500 | tf_op jit(solution)/shard_map/w_gate_grad/pallas_call | solution.py:480
  242.3 6.5 %w_up_grad.2 = bf16[768,1152]{1,0:T(8,128)(2,1)S(1)} custom-call(bf16[512,1536]{1,0:T(8,128)(2,1)S(1)} %multiply_convert_fusion.n2_a.refs_0_, bf16[512,1536]{1,0:T(8,128)(2,1)S(1)} %collective-permute-done.14.n2_b.refs_1_, bf16[512,1536]{1,0:T(8,128)(2,1)S(1)} %collective-permute-done.21.n2_a.refs_2_, ...), custom_call_target="tpu_custom_call" | custom-call | flops 862499968 | bytes 2767500 | tf_op jit(solution)/shard_map/w_up_grad/pallas_call | solution.py:480
  248.8 10.4 %feed_back.3 = (bf16[512,1536]{1,0:T(8,128)(2,1)S(1)}, bf16[512,1536]{1,0:T(8,128)(2,1)}) custom-call(bf16[1024,1152]{1,0:T(8,128)(2,1)S(1)} %get-tuple-element.185.refs_4_.refs_5_.refs_0_, bf16[1024,1152]{1,0:T(8,128)(2,1)S(1)} %get-tuple-element.176.refs_4_.refs_5_.refs_1_, bf16[768,1152]{1,0:T(8,128)(2,1)S(1)} %copy-done.22, ...), custom_call_target="tpu_custom_call" | custom-call | flops 977500032 | bytes 3136500 | tf_op jit(solution)/shard_map/feed_back/pallas_call | solution.py:527
  260.5 11.0 %collective-permute-done.31.other_a.other_b = bf16[768,1152]{1,0:T(8,128)(2,1)} collective-permute-done((bf16[768,1152]{1,0:T(8,128)(2,1)}, bf16[768,1152]{1,0:T(8,128)(2,1)}, u32[]{:S(2)}, u32[]{:S(2)}) %collective-permute-start.31) | collective-permute-done | bytes 1769504 | tf_op jit(solution)/shard_map/ppermute | solution.py:34
  278.0 6.5 %w_up_grad.3.own_a.own_b = bf16[768,1152]{1,0:T(8,128)(2,1)S(1)} custom-call(bf16[512,1536]{1,0:T(8,128)(2,1)S(1)} %copy-done.7, bf16[512,1536]{1,0:T(8,128)(2,1)S(1)} %copy-done.12, bf16[512,1536]{1,0:T(8,128)(2,1)S(1)} %copy-done.14, bf16[512,1536]{1,0:T(8,128)(2,1)S(1)} %copy-done.16, bf16[1024,1152]{1,0:T(8,128)(2,1)S(1)} %get-tuple-element.176.refs_4_.refs_5_.refs_1_, ...), custom_call_target="tpu_custom_call" | custom-call | flops 862499968 | bytes 2767500 | tf_op jit(solution)/shard_map/w_up_grad/pallas_call | solution.py:480
  296.4 4.9 w_down_grad.2
  325.6 15.0 %attend_backward.1 = (bf16[512,768]{1,0:T(8,128)(2,1)S(1)}, bf16[512,768]{1,0:T(8,128)(2,1)S(1)}, f32[2048,256]{1,0:T(8,128)S(1)}) custom-call(s32[1]{0:T(128)} %bitcast.start, bf16[512,768]{1,0:T(8,128)(2,1)S(1)} %copy-done.54, bf16[512,768]{1,0:T(8,128)(2,1)S(1)} %copy-done.56, bf16[2048,256]{1,0:T(8,128)(2,1)S(1)} %copy-done.48, ...), custom_call_target="tpu_custom_call" | custom-call | flops 2300000000 | bytes 7380000 | tf_op jit(solution)/shard_map/attend_backward/pallas_call | solution.py:384
  344.4 19.7 %collective-permute-done.37.left = bf16[384,1152]{1,0:T(8,128)(2,1)S(1)} collective-permute-done((bf16[384,1152]{1,0:T(8,128)(2,1)S(1)}, bf16[384,1152]{1,0:T(8,128)(2,1)S(1)}, u32[]{:S(2)}, u32[]{:S(2)}) %collective-permute-start.37) | collective-permute-done | bytes 884768 | tf_op jit(solution)/shard_map/ppermute | solution.py:68
  369.2 5.2 collective-permute-start.40
  378.4 5.8 %down.2 = (bf16[512,1536]{1,0:T(8,128)(2,1)S(1)}, bf16[512,1536]{1,0:T(8,128)(2,1)S(1)}) custom-call(bf16[1024,1152]{1,0:T(8,128)(2,1)S(1)} %copy-done.5, bf16[1152,768]{1,0:T(8,128)(2,1)S(1)} %copy-done.19, bf16[1152,768]{1,0:T(8,128)(2,1)S(1)} %copy-done.9), custom_call_target="tpu_custom_call" | custom-call | flops 977500032 | bytes 3136500 | tf_op jit(solution)/shard_map/down/pallas_call | solution.py:527
  398.8 5.7 fusion.5
  407.9 22.6 %collective-permute-start.45 = (bf16[768,384]{1,0:T(8,128)(2,1)S(1)}, bf16[768,384]{1,0:T(8,128)(2,1)S(1)}, u32[]{:S(2)}, u32[]{:S(2)}) collective-permute-start(bf16[768,384]{1,0:T(8,128)(2,1)S(1)} %get-tuple-element.307), channel_id=1, source_target_pairs={{0,4},{4,0},{1,5},{5,1},{2,6},{6,2},{3,7},{7,3},{8,12},{12,8},{9,1... | collective-permute-start | bytes 1769480 | tf_op jit(solution)/shard_map/ppermute | solution.py:34
  438.7 5.7 %down.3 = (bf16[512,1536]{1,0:T(8,128)(2,1)S(1)}, bf16[512,1536]{1,0:T(8,128)(2,1)S(1)}) custom-call(bf16[1024,1152]{1,0:T(8,128)(2,1)S(1)} %copy-done.3, bf16[1152,768]{1,0:T(8,128)(2,1)S(1)} %copy-done.20, bf16[1152,768]{1,0:T(8,128)(2,1)S(1)} %copy-done.10), custom_call_target="tpu_custom_call" | custom-call | flops 977500032 | bytes 3136500 | tf_op jit(solution)/shard_map/down/pallas_call | solution.py:527
  449.9 29.3 %collective-permute-done.54.rest = bf16[384,1152]{1,0:T(8,128)(2,1)S(1)} collective-permute-done((bf16[384,1152]{1,0:T(8,128)(2,1)S(1)}, bf16[384,1152]{1,0:T(8,128)(2,1)S(1)}, u32[]{:S(2)}, u32[]{:S(2)}) %collective-permute-start.54) | collective-permute-done | bytes 884768 | tf_op jit(solution)/shard_map/ppermute | solution.py:63
  485.5 20.1 %collective-permute-done.56.left = bf16[384,1152]{1,0:T(8,128)(2,1)S(1)} collective-permute-done((bf16[384,1152]{1,0:T(8,128)(2,1)S(1)}, bf16[384,1152]{1,0:T(8,128)(2,1)S(1)}, u32[]{:S(2)}, u32[]{:S(2)}) %collective-permute-start.56) | collective-permute-done | bytes 884768 | tf_op jit(solution)/shard_map/ppermute | solution.py:63
  508.1 7.9 %collective-permute-done.55 = bf16[512,1536]{1,0:T(8,128)(2,1)S(1)} collective-permute-done((bf16[512,1536]{1,0:T(8,128)(2,1)S(1)}, bf16[512,1536]{1,0:T(8,128)(2,1)S(1)}, u32[]{:S(2)}, u32[]{:S(2)}) %collective-permute-start.55) | collective-permute-done | bytes 1572896 | tf_op jit(solution)/shard_map/ppermute | solution.py:42
  516.7 7.1 %collective-permute-done.58.rest = bf16[576,768]{1,0:T(8,128)(2,1)S(1)} collective-permute-done((bf16[576,768]{1,0:T(8,128)(2,1)S(1)}, bf16[576,768]{1,0:T(8,128)(2,1)S(1)}, u32[]{:S(2)}, u32[]{:S(2)}) %collective-permute-start.58) | collective-permute-done | bytes 884768 | tf_op jit(solution)/shard_map/ppermute | solution.py:63
  528.3 16.3 %collective-permute-done.60.left = bf16[384,1152]{1,0:T(8,128)(2,1)S(1)} collective-permute-done((bf16[384,1152]{1,0:T(8,128)(2,1)S(1)}, bf16[384,1152]{1,0:T(8,128)(2,1)S(1)}, u32[]{:S(2)}, u32[]{:S(2)}) %collective-permute-start.60) | collective-permute-done | bytes 884768 | tf_op jit(solution)/shard_map/ppermute | solution.py:68
  548.8 12.9 %collective-permute-done.57 = bf16[512,768]{1,0:T(8,128)(2,1)S(1)} collective-permute-done((bf16[512,768]{1,0:T(8,128)(2,1)S(1)}, bf16[512,768]{1,0:T(8,128)(2,1)S(1)}, u32[]{:S(2)}, u32[]{:S(2)}) %collective-permute-start.57) | collective-permute-done | bytes 786464 | tf_op jit(solution)/shard_map/ppermute | solution.py:34
  (421 shorter events, 193.0 us)
Async XLA Ops:
  9.5 44.2 %collective-permute-start.3 = (bf16[768,640]{1,0:T(8,128)(2,1)}, bf16[768,640]{1,0:T(8,128)(2,1)}, u32[]{:S(2)}, u32[]{:S(2)}) collective-permute-start(bf16[768,640]{1,0:T(8,128)(2,1)} %pad_maximum_fusion.6), channel_id=1, source_target_pairs={{0,4},{4,0},{1,5},{5,1},{2,6},{6,2},{3,7},{7,3},{8,12},{12,8},{9,1... | collective-permute-start | bytes 2949128 | tf_op jit(solution)/shard_map/ppermute | solution.py:34
  11.2 38.4 %collective-permute-start = (bf16[512,768]{1,0:T(8,128)(2,1)}, bf16[512,768]{1,0:T(8,128)(2,1)}, u32[]{:S(2)}, u32[]{:S(2)}) collective-permute-start(bf16[512,768]{1,0:T(8,128)(2,1)} %get-tuple-element.130), channel_id=1, source_target_pairs={{0,4},{4,0},{1,5},{5,1},{2,6},{6,2},{3,7},{7,3},{8,12},{12,8},{9,1... | collective-permute-start | bytes 2359304 | tf_op jit(solution)/shard_map/ppermute | solution.py:34
  49.6 23.4 %collective-permute-start.6 = (bf16[384,768]{1,0:T(8,128)(2,1)}, bf16[384,768]{1,0:T(8,128)(2,1)S(1)}, u32[]{:S(2)}, u32[]{:S(2)}) collective-permute-start(bf16[384,768]{1,0:T(8,128)(2,1)} %param.15), channel_id=1, source_target_pairs={{0,4},{4,0},{1,5},{5,1},{2,6},{6,2},{3,7},{7,3},{8,12},{12,8},{9,1... | collective-permute-start | bytes 1769480 | tf_op jit(solution)/shard_map/ppermute | solution.py:34
  65.7 26.1 %collective-permute-start.11 = (bf16[384,1152]{1,0:T(8,128)(2,1)S(1)}, bf16[384,1152]{1,0:T(8,128)(2,1)S(1)}, u32[]{:S(2)}, u32[]{:S(2)}) collective-permute-start(bf16[384,1152]{1,0:T(8,128)(2,1)S(1)} %copy-done.83), channel_id=1, source_target_pairs={{0,4},{4,0},{1,5},{5,1},{2,6},{6,2},{3,7},{7,3},{8,12},{12,8},{9,1... | collective-permute-start | bytes 2654216 | tf_op jit(solution)/shard_map/ppermute | solution.py:34
  79.6 38.8 %collective-permute-start.13 = (bf16[384,1152]{1,0:T(8,128)(2,1)S(1)}, bf16[384,1152]{1,0:T(8,128)(2,1)S(1)}, u32[]{:S(2)}, u32[]{:S(2)}) collective-permute-start(bf16[384,1152]{1,0:T(8,128)(2,1)S(1)} %copy-done.82), channel_id=1, source_target_pairs={{0,4},{4,0},{1,5},{5,1},{2,6},{6,2},{3,7},{7,3},{8,12},{12,8},{9,1... | collective-permute-start | bytes 2654216 | tf_op jit(solution)/shard_map/ppermute | solution.py:34
  95.9 28.4 %collective-permute-start.20 = (bf16[512,768]{1,0:T(8,128)(2,1)S(1)}, bf16[512,768]{1,0:T(8,128)(2,1)S(1)}, u32[]{:S(2)}, u32[]{:S(2)}) collective-permute-start(bf16[512,768]{1,0:T(8,128)(2,1)S(1)} %copy-done.26), channel_id=1, source_target_pairs={{0,2},{2,0},{1,3},{3,1},{4,6},{6,4},{5,7},{7,5},{8,10},{10,8},{9,1... | collective-permute-start | bytes 2359304 | tf_op jit(solution)/shard_map/ppermute | solution.py:42
  96.4 24.5 %collective-permute-start.16 = (bf16[384,1152]{1,0:T(8,128)(2,1)S(1)}, bf16[384,1152]{1,0:T(8,128)(2,1)S(1)}, u32[]{:S(2)}, u32[]{:S(2)}) collective-permute-start(bf16[384,1152]{1,0:T(8,128)(2,1)S(1)} %collective-permute-done.11.straight), channel_id=1, source_target_pairs={{0,8},{8,0},{16,24},{24,16},{1,9},{9,1},{17,25},{25,17},{2,10},{10... | collective-permute-start | bytes 2654216 | tf_op jit(solution)/shard_map/ppermute | solution.py:63
  98.1 28.7 %collective-permute-start.18 = (bf16[576,768]{1,0:T(8,128)(2,1)S(1)}, bf16[576,768]{1,0:T(8,128)(2,1)S(1)}, u32[]{:S(2)}, u32[]{:S(2)}) collective-permute-start(bf16[576,768]{1,0:T(8,128)(2,1)S(1)} %copy-done.81), channel_id=1, source_target_pairs={{0,4},{4,0},{1,5},{5,1},{2,6},{6,2},{3,7},{7,3},{8,12},{12,8},{9,1... | collective-permute-start | bytes 2654216 | tf_op jit(solution)/shard_map/ppermute | solution.py:34
  119.6 36.4 %collective-permute-start.21 = (bf16[512,1536]{1,0:T(8,128)(2,1)S(1)}, bf16[512,1536]{1,0:T(8,128)(2,1)S(1)}, u32[]{:S(2)}, u32[]{:S(2)}) collective-permute-start(bf16[512,1536]{1,0:T(8,128)(2,1)S(1)} %multiply_convert_fusion.n2_a.refs_0_), channel_id=1, source_target_pairs={{0,2},{2,0},{1,3},{3,1},{4,6},{6,4},{5,7},{7,5},{8,10},{10,8},{9,1... | collective-permute-start | bytes 4718600 | tf_op jit(solution)/shard_map/ppermute | solution.py:42
  157.3 39.7 %collective-permute-start.25 = (bf16[512,1536]{1,0:T(8,128)(2,1)S(1)}, bf16[512,1536]{1,0:T(8,128)(2,1)S(1)}, u32[]{:S(2)}, u32[]{:S(2)}) collective-permute-start(bf16[512,1536]{1,0:T(8,128)(2,1)S(1)} %collective-permute-done.21.n2_a.refs_2_), channel_id=1, source_target_pairs={{0,1},{1,0},{2,3},{3,2},{4,5},{5,4},{6,7},{7,6},{8,9},{9,8},{10,11... | collective-permute-start | bytes 4718600 | tf_op jit(solution)/shard_map/ppermute | solution.py:38
  229.6 42.0 %collective-permute-start.31 = (bf16[768,1152]{1,0:T(8,128)(2,1)}, bf16[768,1152]{1,0:T(8,128)(2,1)}, u32[]{:S(2)}, u32[]{:S(2)}) collective-permute-start(bf16[768,1152]{1,0:T(8,128)(2,1)} %w_gate_grad.2), channel_id=1, source_target_pairs={{0,4},{4,0},{1,5},{5,1},{2,6},{6,2},{3,7},{7,3},{8,12},{12,8},{9,1... | collective-permute-start | bytes 5308424 | tf_op jit(solution)/shard_map/ppermute | solution.py:34
  240.5 44.0 %collective-permute-start.30 = (bf16[512,1536]{1,0:T(8,128)(2,1)}, bf16[512,1536]{1,0:T(8,128)(2,1)}, u32[]{:S(2)}, u32[]{:S(2)}) collective-permute-start(bf16[512,1536]{1,0:T(8,128)(2,1)} %add_convert_fusion), channel_id=1, source_target_pairs={{0,2},{2,0},{1,3},{3,1},{4,6},{6,4},{5,7},{7,5},{8,10},{10,8},{9,1... | collective-permute-start | bytes 4718600 | tf_op jit(solution)/shard_map/ppermute | solution.py:42
  260.4 24.2 %collective-permute-start.29 = (bf16[512,1536]{1,0:T(8,128)(2,1)}, bf16[512,1536]{1,0:T(8,128)(2,1)}, u32[]{:S(2)}, u32[]{:S(2)}) collective-permute-start(bf16[512,1536]{1,0:T(8,128)(2,1)} %get-tuple-element.187), channel_id=1, source_target_pairs={{0,1},{1,0},{2,3},{3,2},{4,5},{5,4},{6,7},{7,6},{8,9},{9,8},{10,11... | collective-permute-start | bytes 4718600 | tf_op jit(solution)/shard_map/ppermute | solution.py:38
  260.4 48.7 %collective-permute-start.32 = (bf16[768,1152]{1,0:T(8,128)(2,1)}, bf16[768,1152]{1,0:T(8,128)(2,1)S(1)}, u32[]{:S(2)}, u32[]{:S(2)}) collective-permute-start(bf16[768,1152]{1,0:T(8,128)(2,1)} %copy-done.44), channel_id=1, source_target_pairs={{0,4},{4,0},{1,5},{5,1},{2,6},{6,2},{3,7},{7,3},{8,12},{12,8},{9,1... | collective-permute-start | bytes 5308424 | tf_op jit(solution)/shard_map/ppermute | solution.py:34
  311.2 53.5 %collective-permute-start.34 = (bf16[1152,768]{1,0:T(8,128)(2,1)S(1)}, bf16[1152,768]{1,0:T(8,128)(2,1)S(1)}, u32[]{:S(2)}, u32[]{:S(2)}) collective-permute-start(bf16[1152,768]{1,0:T(8,128)(2,1)S(1)} %w_down_grad.2), channel_id=1, source_target_pairs={{0,4},{4,0},{1,5},{5,1},{2,6},{6,2},{3,7},{7,3},{8,12},{12,8},{9,1... | collective-permute-start | bytes 5308424 | tf_op jit(solution)/shard_map/ppermute | solution.py:34
  320.1 44.3 %collective-permute-start.36 = (bf16[1536,384]{1,0:T(8,128)(2,1)S(1)}, bf16[1536,384]{1,0:T(8,128)(2,1)S(1)}, u32[]{:S(2)}, u32[]{:S(2)}) collective-permute-start(bf16[1536,384]{1,0:T(8,128)(2,1)S(1)} %get-tuple-element.297), channel_id=1, source_target_pairs={{0,2},{2,0},{1,3},{3,1},{4,6},{6,4},{5,7},{7,5},{8,10},{10,8},{9,1... | collective-permute-start | bytes 3538952 | tf_op jit(solution)/shard_map/ppermute | solution.py:42
  322.2 41.9 %collective-permute-start.37 = (bf16[384,1152]{1,0:T(8,128)(2,1)S(1)}, bf16[384,1152]{1,0:T(8,128)(2,1)S(1)}, u32[]{:S(2)}, u32[]{:S(2)}) collective-permute-start(bf16[384,1152]{1,0:T(8,128)(2,1)S(1)} %add.200.right), channel_id=1, source_target_pairs={{0,24},{8,16},{16,8},{24,0},{1,25},{9,17},{17,9},{25,1},{2,26},{10... | collective-permute-start | bytes 2654216 | tf_op jit(solution)/shard_map/ppermute | solution.py:68
  369.2 64.5 %collective-permute-start.40 = (bf16[384,1152]{1,0:T(8,128)(2,1)}, bf16[384,1152]{1,0:T(8,128)(2,1)}, u32[]{:S(2)}, u32[]{:S(2)}) collective-permute-start(bf16[384,1152]{1,0:T(8,128)(2,1)} %add.202.right), channel_id=1, source_target_pairs={{0,24},{8,16},{16,8},{24,0},{1,25},{9,17},{17,9},{25,1},{2,26},{10... | collective-permute-start | bytes 2654216 | tf_op jit(solution)/shard_map/ppermute | solution.py:68
  375.8 59.6 %collective-permute-start.39 = (bf16[576,768]{1,0:T(8,128)(2,1)}, bf16[576,768]{1,0:T(8,128)(2,1)}, u32[]{:S(2)}, u32[]{:S(2)}) collective-permute-start(bf16[576,768]{1,0:T(8,128)(2,1)} %get-tuple-element.213), channel_id=1, source_target_pairs={{0,8},{8,0},{16,24},{24,16},{1,9},{9,1},{17,25},{25,17},{2,10},{10... | collective-permute-start | bytes 2654216 | tf_op jit(solution)/shard_map/ppermute | solution.py:63
  391.0 53.5 %collective-permute-start.46 = (bf16[1536,384]{1,0:T(8,128)(2,1)}, bf16[1536,384]{1,0:T(8,128)(2,1)}, u32[]{:S(2)}, u32[]{:S(2)}) collective-permute-start(bf16[1536,384]{1,0:T(8,128)(2,1)} %get-tuple-element.295), channel_id=1, source_target_pairs={{0,2},{2,0},{1,3},{3,1},{4,6},{6,4},{5,7},{7,5},{8,10},{10,8},{9,1... | collective-permute-start | bytes 3538952 | tf_op jit(solution)/shard_map/ppermute | solution.py:42
  407.2 39.6 %collective-permute-start.48 = (bf16[512,1536]{1,0:T(8,128)(2,1)S(1)}, bf16[512,1536]{1,0:T(8,128)(2,1)S(1)}, u32[]{:S(2)}, u32[]{:S(2)}) collective-permute-start(bf16[512,1536]{1,0:T(8,128)(2,1)S(1)} %copy-done.52), channel_id=1, source_target_pairs={{0,1},{1,0},{2,3},{3,2},{4,5},{5,4},{6,7},{7,6},{8,9},{9,8},{10,11... | collective-permute-start | bytes 4718600 | tf_op jit(solution)/shard_map/ppermute | solution.py:38
  407.9 38.0 %collective-permute-start.45 = (bf16[768,384]{1,0:T(8,128)(2,1)S(1)}, bf16[768,384]{1,0:T(8,128)(2,1)S(1)}, u32[]{:S(2)}, u32[]{:S(2)}) collective-permute-start(bf16[768,384]{1,0:T(8,128)(2,1)S(1)} %get-tuple-element.307), channel_id=1, source_target_pairs={{0,4},{4,0},{1,5},{5,1},{2,6},{6,2},{3,7},{7,3},{8,12},{12,8},{9,1... | collective-permute-start | bytes 1769480 | tf_op jit(solution)/shard_map/ppermute | solution.py:34
  436.7 42.4 %collective-permute-start.53 = (bf16[576,768]{1,0:T(8,128)(2,1)S(1)}, bf16[576,768]{1,0:T(8,128)(2,1)S(1)}, u32[]{:S(2)}, u32[]{:S(2)}) collective-permute-start(bf16[576,768]{1,0:T(8,128)(2,1)S(1)} %add.207.right), channel_id=1, source_target_pairs={{0,24},{8,16},{16,8},{24,0},{1,25},{9,17},{17,9},{25,1},{2,26},{10... | collective-permute-start | bytes 2654216 | tf_op jit(solution)/shard_map/ppermute | solution.py:68
  438.7 40.5 %collective-permute-start.54 = (bf16[384,1152]{1,0:T(8,128)(2,1)S(1)}, bf16[384,1152]{1,0:T(8,128)(2,1)S(1)}, u32[]{:S(2)}, u32[]{:S(2)}) collective-permute-start(bf16[384,1152]{1,0:T(8,128)(2,1)S(1)} %add.206.total), channel_id=1, source_target_pairs={{0,8},{8,0},{16,24},{24,16},{1,9},{9,1},{17,25},{25,17},{2,10},{10... | collective-permute-start | bytes 2654216 | tf_op jit(solution)/shard_map/ppermute | solution.py:63
  446.3 36.0 %collective-permute-start.50 = (bf16[768,384]{1,0:T(8,128)(2,1)S(1)}, bf16[768,384]{1,0:T(8,128)(2,1)S(1)}, u32[]{:S(2)}, u32[]{:S(2)}) collective-permute-start(bf16[768,384]{1,0:T(8,128)(2,1)S(1)} %get-tuple-element.302), channel_id=1, source_target_pairs={{0,4},{4,0},{1,5},{5,1},{2,6},{6,2},{3,7},{7,3},{8,12},{12,8},{9,1... | collective-permute-start | bytes 1769480 | tf_op jit(solution)/shard_map/ppermute | solution.py:34
  446.8 35.5 %collective-permute-start.51 = (bf16[768,384]{1,0:T(8,128)(2,1)S(1)}, bf16[768,384]{1,0:T(8,128)(2,1)S(1)}, u32[]{:S(2)}, u32[]{:S(2)}) collective-permute-start(bf16[768,384]{1,0:T(8,128)(2,1)S(1)} %get-tuple-element.304), channel_id=1, source_target_pairs={{0,4},{4,0},{1,5},{5,1},{2,6},{6,2},{3,7},{7,3},{8,12},{12,8},{9,1... | collective-permute-start | bytes 1769480 | tf_op jit(solution)/shard_map/ppermute | solution.py:34
  449.2 33.1 %collective-permute-start.52 = (bf16[768,384]{1,0:T(8,128)(2,1)S(1)}, bf16[768,384]{1,0:T(8,128)(2,1)S(1)}, u32[]{:S(2)}, u32[]{:S(2)}) collective-permute-start(bf16[768,384]{1,0:T(8,128)(2,1)S(1)} %add.211), channel_id=1, source_target_pairs={{0,2},{2,0},{1,3},{3,1},{4,6},{6,4},{5,7},{7,5},{8,10},{10,8},{9,1... | collective-permute-start | bytes 1769480 | tf_op jit(solution)/shard_map/ppermute | solution.py:42
  479.2 36.8 %collective-permute-start.55 = (bf16[512,1536]{1,0:T(8,128)(2,1)S(1)}, bf16[512,1536]{1,0:T(8,128)(2,1)S(1)}, u32[]{:S(2)}, u32[]{:S(2)}) collective-permute-start(bf16[512,1536]{1,0:T(8,128)(2,1)S(1)} %add.210), channel_id=1, source_target_pairs={{0,2},{2,0},{1,3},{3,1},{4,6},{6,4},{5,7},{7,5},{8,10},{10,8},{9,1... | collective-permute-start | bytes 4718600 | tf_op jit(solution)/shard_map/ppermute | solution.py:42
  483.0 22.5 %collective-permute-start.56 = (bf16[384,1152]{1,0:T(8,128)(2,1)S(1)}, bf16[384,1152]{1,0:T(8,128)(2,1)S(1)}, u32[]{:S(2)}, u32[]{:S(2)}) collective-permute-start(bf16[384,1152]{1,0:T(8,128)(2,1)S(1)} %get-tuple-element.238), channel_id=1, source_target_pairs={{0,8},{8,0},{16,24},{24,16},{1,9},{9,1},{17,25},{25,17},{2,10},{10... | collective-permute-start | bytes 2654216 | tf_op jit(solution)/shard_map/ppermute | solution.py:63
  483.4 40.4 %collective-permute-start.58 = (bf16[576,768]{1,0:T(8,128)(2,1)S(1)}, bf16[576,768]{1,0:T(8,128)(2,1)S(1)}, u32[]{:S(2)}, u32[]{:S(2)}) collective-permute-start(bf16[576,768]{1,0:T(8,128)(2,1)S(1)} %add.212.total), channel_id=1, source_target_pairs={{0,8},{8,0},{16,24},{24,16},{1,9},{9,1},{17,25},{25,17},{2,10},{10... | collective-permute-start | bytes 2654216 | tf_op jit(solution)/shard_map/ppermute | solution.py:63
  505.8 38.8 %collective-permute-start.60 = (bf16[384,1152]{1,0:T(8,128)(2,1)S(1)}, bf16[384,1152]{1,0:T(8,128)(2,1)S(1)}, u32[]{:S(2)}, u32[]{:S(2)}) collective-permute-start(bf16[384,1152]{1,0:T(8,128)(2,1)S(1)} %add.214.right), channel_id=1, source_target_pairs={{0,24},{8,16},{16,8},{24,0},{1,25},{9,17},{17,9},{25,1},{2,26},{10... | collective-permute-start | bytes 2654216 | tf_op jit(solution)/shard_map/ppermute | solution.py:68
  528.2 33.5 %collective-permute-start.57 = (bf16[512,768]{1,0:T(8,128)(2,1)S(1)}, bf16[512,768]{1,0:T(8,128)(2,1)S(1)}, u32[]{:S(2)}, u32[]{:S(2)}) collective-permute-start(bf16[512,768]{1,0:T(8,128)(2,1)S(1)} %slice.158), channel_id=1, source_target_pairs={{0,4},{4,0},{1,5},{5,1},{2,6},{6,2},{3,7},{7,3},{8,12},{12,8},{9,1... | collective-permute-start | bytes 2359304 | tf_op jit(solution)/shard_map/ppermute | solution.py:34
  (135 other events, 2092.3 us)

commit v4 on v3

--- a/solution.py
+++ b/solution.py
@@ -325,6 +325,37 @@
         cost_estimate=lasting(8),
         name="attend_forward",
     )(start, q_a, q_b, kv, seg_q, seg_k)
+
+
+def attend_out_kernel(x, ctx_a, ctx_b, wo_a, wo_b, gain, middle, normed, inverse):
+    value = x[...] + dot(ctx_a[...], wo_a[...]) + dot(ctx_b[...], wo_b[...])
+    scale = lax.rsqrt(jnp.mean(value * value, axis=1, keepdims=True) + EPSILON)
+    middle[...] = value
+    normed[...] = (value * scale * gain[...]).astype(BF16)
+    inverse[...] = scale
+
+
+def attend_out(x, ctx_a, ctx_b, wo_a, wo_b, gain):
+    rows, width = x.shape
+    half = ctx_a.shape[1]
+    tm = 256
+    tile = pl.BlockSpec((tm, width), lambda i: (i, 0))
+    part = pl.BlockSpec((tm, half), lambda i: (i, 0))
+    weight = pl.BlockSpec((half, width), lambda i: (0, 0))
+    return pl.pallas_call(
+        attend_out_kernel,
+        grid=(rows // tm,),
+        in_specs=[tile, part, part, weight, weight, pl.BlockSpec((1, width), lambda i: (0, 0))],
+        out_specs=[tile, tile, pl.BlockSpec((tm, 1), lambda i: (i, 0))],
+        out_shape=[
+            jax.ShapeDtypeStruct((rows, width), F32),
+            jax.ShapeDtypeStruct((rows, width), BF16),
+            jax.ShapeDtypeStruct((rows, 1), F32),
+        ],
+        compiler_params=pltpu.CompilerParams(vmem_limit_bytes=32 * 1024 * 1024),
+        cost_estimate=lasting(5),
+        name="attend_out",
+    )(x, ctx_a, ctx_b, wo_a, wo_b, gain)
 
 
 def attend_backward_kernel(
@@ -586,11 +617,12 @@
     heads_own = w_query.shape[1]
     small_in = rounds.send(swap_row, small)
     x_in = rounds.send(swap_row, give(tokens_in))
-    wq_far_own = rounds.send(swap_far, w_query)
-    rounds.fence()
+    dy_own = keep(out_cotangent)
+    dy_far_own = rounds.send(swap_far, dy_own)
+    wq_far_own = swap_far(after(w_query, dy_own))
     w_qkv = jnp.concatenate([w_query, w_keyval], axis=1)
-    wqkv_in = rounds.send(swap_row, w_qkv)
-    rounds.wait(x_in, wq_far_own, small_in)
+    wqkv_in = swap_row(after(w_qkv, small_in))
+    rounds.wait(x_in, dy_far_own, small_in)
 
     wo_far_own = rounds.send(swap_far, w_attn_out)
     wo_in = rounds.send(swap_row, w_attn_out)
@@ -608,7 +640,7 @@
     first_token = place * local + row * mine
     seg_q = lax.dynamic_slice_in_dim(seg_row[0], first_token, mine, 0)[:, None]
     start = jnp.reshape(first_token, (1,)).astype(jnp.int32)
-    rounds.wait(wqkv_in, wo_far_own, normed_one)
+    rounds.wait(wqkv_in, wq_far_own, normed_one)
 
     wq_in = wqkv_in[:, :heads_own]
     wq_far_in = rounds.send(swap_far, wq_in)
@@ -618,7 +650,7 @@
     kv_in = rounds.send(swap_row, kv_own)
     rounds.fence()
     wg_straight = rounds.send(swap_row, straight_part(w_gate))
-    rounds.wait(wo_in, kv_in, wq_far_in)
+    rounds.wait(wo_in, kv_in, wq_far_in, wo_far_own)
 
     kv_pair = jnp.concatenate(
         [jnp.where(is_low, kv_own, kv_in), jnp.where(is_low, kv_in, kv_own)], axis=0
@@ -657,23 +689,20 @@
     )
     wo_core = rounds.send(swap_core, wo_half)
     wg_around = send_pair(wg_straight)
-    dy_own = keep(out_cotangent)
-    dy_far_own = rounds.send(swap_far, dy_own)
     wd_straight = rounds.send(swap_row, straight_part(w_down))
-    middle = x + dot(after(ctx_a, rounds.token), wo_half) + dot(ctx_b, wo_core)
-    middle = lax.optimization_barrier(middle)
-    inverse_two = lax.rsqrt(jnp.mean(middle * middle, axis=1, keepdims=True) + EPSILON)
-    n2 = (middle * inverse_two * gain_two).astype(BF16)
-    rounds.wait(n2, wo_core, wu_straight)
+    middle, n2, inverse_two = attend_out(
+        x, after(ctx_a, rounds.token), ctx_b, wo_half, wo_core, gain_two[None, :]
+    )
+    rounds.wait(n2, wo_core)
 
     n2_far = rounds.send(swap_far, n2)
     n2_near = rounds.send(swap_core, n2)
+    rounds.wait(n2_near, wu_straight, wg_around)
+
     dy_in = rounds.send(swap_row, give(out_cotangent))
-    rounds.wait(wg_around, n2_near)
-
     wu_around = send_pair(wu_straight)
     dy_near_own = rounds.send(swap_core, dy_own)
-    rounds.wait(wd_straight, wu_around, dy_near_own, dy_far_own)
+    rounds.wait(wd_straight, wu_around, dy_near_own)
 
     wd_around = send_pair(wd_straight)
     dy_diagonal_own = rounds.send(swap_core, dy_far_own)
@@ -681,8 +710,8 @@
     wu = (w_up, placed(wu_straight, after(wu_around, wg[1])))
     rounds.wait(dy_in, n2_far, dy_diagonal_own)
 
+    dy_far_in = rounds.send(swap_far, dy_in)
     dy_near_in = rounds.send(swap_core, dy_in)
-    dy_far_in = rounds.send(swap_far, dy_in)
     n2_diagonal = rounds.send(swap_core, n2_far)
     wd = (w_down, placed(wd_straight, after(wd_around, rounds.token)))
     dy_near = (dy_near_own, dy_near_in)

time: 573 us -> 555 us (0.969)
  starting transfers between devices: 91.9 us -> 72.8 us
  matrix products: 33.3 us -> 22.6 us
  Pallas kernels: 142 us -> 151 us
    ppermute x4, waiting for transfers between devices: 36 us -> 61.6 us  [swap_mirror(): return lax.ppermute(value, 'dp', [(i, count - 1 - i) for i in range(count)])]
    ppermute x18, starting transfers between devices: 49.7 us -> 31.6 us  [swap_row(): return lax.ppermute(value, 'row', [(0, 1), (1, 0)])]
    ppermute x11, waiting for transfers between devices: 89 us -> 71 us  [swap_pair(): return lax.ppermute(value, 'dp', [(i, i ^ 1) for i in range(count)])]
    ppermute x12, waiting for transfers between devices: 49.3 us -> 33 us  [swap_far(): return lax.ppermute(value, 'col', [(0, 2), (2, 0), (1, 3), (3, 1)])]
    dot_general x5 -> x3, matrix products: 15.5 us -> 4.58 us  [dot(): return jnp.dot(left, right, preferred_element_type=F32).astype(out)]
    ppermute x18, waiting for transfers between devices: 64.2 us -> 72.4 us  [swap_row(): return lax.ppermute(value, 'row', [(0, 1), (1, 0)])]
    unnamed x211 -> x213, local copies, waits for them, and re-layouts: 13.7 us -> 12.5 us
  transfers between devices with their start and end apart: 62 -> 62, of which waited for: 27 -> 31; matrix products, arithmetic and copies ran while one was open for 13% -> 12% of each run, Pallas kernels for 19% -> 21%
where the time goes in v4:
time: 555 us; the launch traced here: 549 us
  waiting for transfers between devices  238 us (43%)
  Pallas kernels  151 us (27%)
  starting transfers between devices  72.8 us (13%)
  other arithmetic  33.7 us (6%)
  local copies, waits for them, and re-layouts  28.4 us (5%)
  matrix products  22.6 us (4%)
    ppermute x18, waiting for transfers between devices, swap_row(): return lax.ppermute(value, 'row', [(0, 1), (1, 0)])  72.4 us
    ppermute x11, waiting for transfers between devices, swap_pair(): return lax.ppermute(value, 'dp', [(i, i ^ 1) for i in range(count)])  71 us
    ppermute x4, waiting for transfers between devices, swap_mirror(): return lax.ppermute(value, 'dp', [(i, count - 1 - i) for i in range(count)])  61.6 us
    pallas_call x6, Pallas kernels, weight_grad(): pl.pallas_call(weight_grad_kernel, grid=(pl.cdiv(width_right, tn),), in_s...  37 us
    pallas_call x2, Pallas kernels, feed(): pl.pallas_call(functools.partial(feed_kernel, tm=min(512, rows)), grid=(p...  33.9 us
    ppermute x12, waiting for transfers between devices, swap_far(): return lax.ppermute(value, 'col', [(0, 2), (2, 0), (1, 3), (3, 1)])  33 us
    ppermute x18, starting transfers between devices, swap_row(): return lax.ppermute(value, 'row', [(0, 1), (1, 0)])  31.6 us
    pallas_call x4, Pallas kernels, project(): pl.pallas_call(functools.partial(project_kernel, lefts=len(lefts), multip...  31.6 us
  transfers between devices with their start and end apart: 62, of which 31 were waited for; matrix products, arithmetic and copies ran while one was open for 12% of the time, Pallas kernels for 21%

profile of v4, /device:TPU:0, one launch (start us, length us, event | category | flops | bytes accessed | tf_op | source)
XLA Modules:
  0.0 549.1 jit_solution(12101848194242060818)
XLA Ops:
  16.2 8.4 %collective-permute-done.1 = f32[3584]{0:T(1024)} collective-permute-done((f32[3584]{0:T(1024)}, f32[3584]{0:T(1024)}, u32[]{:S(2)}, u32[]{:S(2)}) %collective-permute-start.1) | collective-permute-done | bytes 14368 | tf_op jit(solution)/shard_map/ppermute | solution.py:34
  41.7 7.8 %collective-permute-done.3 = bf16[768,640]{1,0:T(8,128)(2,1)S(1)} collective-permute-done((bf16[768,640]{1,0:T(8,128)(2,1)}, bf16[768,640]{1,0:T(8,128)(2,1)S(1)}, u32[]{:S(2)}, u32[]{:S(2)}) %collective-permute-start.3) | collective-permute-done | bytes 983072 | tf_op jit(solution)/shard_map/ppermute | solution.py:34
  54.2 13.6 %collective-permute-done.7 = bf16[512,256]{1,0:T(8,128)(2,1)S(1)} collective-permute-done((bf16[512,256]{1,0:T(8,128)(2,1)S(1)}, bf16[512,256]{1,0:T(8,128)(2,1)S(1)}, u32[]{:S(2)}, u32[]{:S(2)}) %collective-permute-start.7) | collective-permute-done | bytes 262176 | tf_op jit(solution)/shard_map/ppermute | solution.py:34
  78.6 6.2 %attend_forward.1 = (bf16[512,768]{1,0:T(8,128)(2,1)S(1)}, bf16[512,768]{1,0:T(8,128)(2,1)S(1)}, f32[512,128]{1,0:T(8,128)S(1)}) custom-call(s32[1]{0:T(128)} %bitcast.start, bf16[512,768]{1,0:T(8,128)(2,1)S(1)} %convolution_convert_fusion.8.q_a, bf16[512,768]{1,0:T(8,128)(2,1)S(1)} %convolution_convert_fusion.7.q_b, ...), custom_call_target="tpu_custom_call" | custom-call | flops 920000000 | bytes 2952000 | tf_op jit(solution)/shard_map/attend_forward/pallas_call | solution.py:310
  89.3 6.3 %collective-permute-start.19 = (bf16[576,768]{1,0:T(8,128)(2,1)S(1)}, bf16[576,768]{1,0:T(8,128)(2,1)S(1)}, u32[]{:S(2)}, u32[]{:S(2)}) collective-permute-start(bf16[576,768]{1,0:T(8,128)(2,1)S(1)} %copy-done.84), channel_id=1, source_target_pairs={{0,4},{4,0},{1,5},{5,1},{2,6},{6,2},{3,7},{7,3},{8,12},{12,8},{9,1... | collective-permute-start | bytes 2654216 | tf_op jit(solution)/shard_map/ppermute | solution.py:34
  111.4 5.8 %collective-permute-start.17 = (bf16[512,768]{1,0:T(8,128)(2,1)S(1)}, bf16[512,768]{1,0:T(8,128)(2,1)S(1)}, u32[]{:S(2)}, u32[]{:S(2)}) collective-permute-start(bf16[512,768]{1,0:T(8,128)(2,1)S(1)} %copy-done.87), channel_id=1, source_target_pairs={{0,4},{4,0},{1,5},{5,1},{2,6},{6,2},{3,7},{7,3},{8,12},{12,8},{9,1... | collective-permute-start | bytes 2359304 | tf_op jit(solution)/shard_map/ppermute | solution.py:34
  117.2 7.5 %collective-permute-done.19.straight = bf16[576,768]{1,0:T(8,128)(2,1)S(1)} collective-permute-done((bf16[576,768]{1,0:T(8,128)(2,1)S(1)}, bf16[576,768]{1,0:T(8,128)(2,1)S(1)}, u32[]{:S(2)}, u32[]{:S(2)}) %collective-permute-start.19) | collective-permute-done | bytes 884768 | tf_op jit(solution)/shard_map/ppermute | solution.py:34
  124.6 6.7 %collective-permute-done.20.around = bf16[384,1152]{1,0:T(8,128)(2,1)S(1)} collective-permute-done((bf16[384,1152]{1,0:T(8,128)(2,1)S(1)}, bf16[384,1152]{1,0:T(8,128)(2,1)S(1)}, u32[]{:S(2)}, u32[]{:S(2)}) %collective-permute-start.20) | collective-permute-done | bytes 884768 | tf_op jit(solution)/shard_map/ppermute | solution.py:63
  142.9 16.9 %collective-permute-done.26.dy_b.refs_6_ = bf16[512,768]{1,0:T(8,128)(2,1)S(1)} collective-permute-done((bf16[512,768]{1,0:T(8,128)(2,1)S(1)}, bf16[512,768]{1,0:T(8,128)(2,1)S(1)}, u32[]{:S(2)}, u32[]{:S(2)}) %collective-permute-start.26) | collective-permute-done | bytes 786464 | tf_op jit(solution)/shard_map/ppermute | solution.py:42
  163.2 17.0 %feed.2 = (bf16[1024,1152]{1,0:T(8,128)(2,1)S(1)}, bf16[1024,1152]{1,0:T(8,128)(2,1)S(1)}, bf16[1024,1152]{1,0:T(8,128)(2,1)S(1)}) custom-call(bf16[512,1536]{1,0:T(8,128)(2,1)S(1)} %get-tuple-element.160.n2_a.refs_0_, bf16[512,1536]{1,0:T(8,128)(2,1)S(1)} %collective-permute-done.14.n2_b.refs_1_, bf16[512,768]{1,0:T(8,128)(2,1)} %get-tuple-element.165.dy_a.refs_4_, ...), custom_call_target="tpu_custom_call" | custom-call | flops 2012499968 | bytes 6457500 | tf_op jit(solution)/shard_map/feed/pallas_call | solution.py:471
  181.7 16.9 %feed.3 = (bf16[1024,1152]{1,0:T(8,128)(2,1)S(1)}, bf16[1024,1152]{1,0:T(8,128)(2,1)S(1)}, bf16[1024,1152]{1,0:T(8,128)(2,1)S(1)}) custom-call(bf16[512,1536]{1,0:T(8,128)(2,1)S(1)} %collective-permute-done.21.n2_a.refs_2_, bf16[512,1536]{1,0:T(8,128)(2,1)S(1)} %collective-permute-done.25.n2_b.refs_3_, bf16[512,768]{1,0:T(8,128)(2,1)} %collective-permute-done.4.dy_a.refs_6_, ...), custom_call_target="tpu_custom_call" | custom-call | flops 2012499968 | bytes 6457500 | tf_op jit(solution)/shard_map/feed/pallas_call | solution.py:471
  198.7 7.0 %w_gate_grad.2 = bf16[768,1152]{1,0:T(8,128)(2,1)} custom-call(bf16[512,1536]{1,0:T(8,128)(2,1)S(1)} %get-tuple-element.160.n2_a.refs_0_, bf16[512,1536]{1,0:T(8,128)(2,1)S(1)} %collective-permute-done.14.n2_b.refs_1_, bf16[512,1536]{1,0:T(8,128)(2,1)S(1)} %collective-permute-done.21.n2_a.refs_2_, ...), custom_call_target="tpu_custom_call" | custom-call | flops 862499968 | bytes 2767500 | tf_op jit(solution)/shard_map/w_gate_grad/pallas_call | solution.py:511
  205.7 9.6 %feed_back.2 = (bf16[512,1536]{1,0:T(8,128)(2,1)S(1)}, bf16[512,1536]{1,0:T(8,128)(2,1)S(1)}) custom-call(bf16[1024,1152]{1,0:T(8,128)(2,1)S(1)} %get-tuple-element.188.refs_6_.refs_7_.refs_0_, bf16[1024,1152]{1,0:T(8,128)(2,1)S(1)} %get-tuple-element.197.refs_1_.refs_6_.refs_7_, bf16[768,1152]{1,0:T(8,128)(2,1)S(1)} %copy-done.22, ...), custom_call_target="tpu_custom_call" | custom-call | flops 977500032 | bytes 3136500 | tf_op jit(solution)/shard_map/feed_back/pallas_call | solution.py:558
  217.0 6.5 %w_gate_grad.3.own_a.own_b = bf16[768,1152]{1,0:T(8,128)(2,1)S(1)} custom-call(bf16[512,1536]{1,0:T(8,128)(2,1)S(1)} %get-tuple-element.160.n2_a.refs_0_, bf16[512,1536]{1,0:T(8,128)(2,1)S(1)} %collective-permute-done.14.n2_b.refs_1_, bf16[512,1536]{1,0:T(8,128)(2,1)S(1)} %collective-permute-done.21.n2_a.refs_2_, ...), custom_call_target="tpu_custom_call" | custom-call | flops 862499968 | bytes 2767500 | tf_op jit(solution)/shard_map/w_gate_grad/pallas_call | solution.py:511
  226.6 6.5 %w_up_grad.2 = bf16[768,1152]{1,0:T(8,128)(2,1)S(1)} custom-call(bf16[512,1536]{1,0:T(8,128)(2,1)S(1)} %get-tuple-element.160.n2_a.refs_0_, bf16[512,1536]{1,0:T(8,128)(2,1)S(1)} %collective-permute-done.14.n2_b.refs_1_, bf16[512,1536]{1,0:T(8,128)(2,1)S(1)} %collective-permute-done.21.n2_a.refs_2_, ...), custom_call_target="tpu_custom_call" | custom-call | flops 862499968 | bytes 2767500 | tf_op jit(solution)/shard_map/w_up_grad/pallas_call | solution.py:511
  233.1 10.5 %feed_back.3 = (bf16[512,1536]{1,0:T(8,128)(2,1)S(1)}, bf16[512,1536]{1,0:T(8,128)(2,1)}) custom-call(bf16[1024,1152]{1,0:T(8,128)(2,1)S(1)} %get-tuple-element.191.refs_4_.refs_5_.refs_0_, bf16[1024,1152]{1,0:T(8,128)(2,1)S(1)} %get-tuple-element.182.refs_4_.refs_5_.refs_1_, bf16[768,1152]{1,0:T(8,128)(2,1)S(1)} %copy-done.22, ...), custom_call_target="tpu_custom_call" | custom-call | flops 977500032 | bytes 3136500 | tf_op jit(solution)/shard_map/feed_back/pallas_call | solution.py:558
  245.5 11.7 %collective-permute-done.31.other_a.other_b = bf16[768,1152]{1,0:T(8,128)(2,1)} collective-permute-done((bf16[768,1152]{1,0:T(8,128)(2,1)}, bf16[768,1152]{1,0:T(8,128)(2,1)}, u32[]{:S(2)}, u32[]{:S(2)}) %collective-permute-start.31) | collective-permute-done | bytes 1769504 | tf_op jit(solution)/shard_map/ppermute | solution.py:34
  265.1 6.5 %w_up_grad.3.own_a.own_b = bf16[768,1152]{1,0:T(8,128)(2,1)S(1)} custom-call(bf16[512,1536]{1,0:T(8,128)(2,1)S(1)} %copy-done.10, bf16[512,1536]{1,0:T(8,128)(2,1)S(1)} %copy-done.12, bf16[512,1536]{1,0:T(8,128)(2,1)S(1)} %copy-done.14, bf16[512,1536]{1,0:T(8,128)(2,1)S(1)} %copy-done.16, bf16[1024,1152]{1,0:T(8,128)(2,1)S(1)} %get-tuple-element.182.refs_4_.refs_5_.refs_1_, ...), custom_call_target="tpu_custom_call" | custom-call | flops 862499968 | bytes 2767500 | tf_op jit(solution)/shard_map/w_up_grad/pallas_call | solution.py:511
  299.5 5.8 %w_down_grad.3.own_a.own_b = bf16[1152,768]{1,0:T(8,128)(2,1)S(1)} custom-call(bf16[1024,1152]{1,0:T(8,128)(2,1)S(1)} %copy-done.3, bf16[1024,1152]{1,0:T(8,128)(2,1)S(1)} %copy-done.3, bf16[1024,1152]{1,0:T(8,128)(2,1)S(1)} %copy-done.5, bf16[1024,1152]{1,0:T(8,128)(2,1)S(1)} %copy-done.5, bf16[512,768]{1,0:T(8,128)(2,1)} %get-tuple-element.165.dy_a.refs_4_, ...), custom_call_target="tpu_custom_call" | custom-call | flops 862499968 | bytes 2767500 | tf_op jit(solution)/shard_map/w_down_grad/pallas_call | solution.py:511
  312.7 14.8 %attend_backward.1 = (bf16[512,768]{1,0:T(8,128)(2,1)S(1)}, bf16[512,768]{1,0:T(8,128)(2,1)S(1)}, f32[2048,256]{1,0:T(8,128)S(1)}) custom-call(s32[1]{0:T(128)} %bitcast.start, bf16[512,768]{1,0:T(8,128)(2,1)S(1)} %copy-done.67, bf16[512,768]{1,0:T(8,128)(2,1)S(1)} %copy-done.69, bf16[2048,256]{1,0:T(8,128)(2,1)S(1)} %copy-done.53, s32[512,1]{1,0:T(8,128)S(1)} %copy-done.63, ...), custom_call_target="tpu_custom_call" | custom-call | flops 2300000000 | bytes 7380000 | tf_op jit(solution)/shard_map/attend_backward/pallas_call | solution.py:415
  331.2 19.9 %collective-permute-done.37.left = bf16[384,1152]{1,0:T(8,128)(2,1)S(1)} collective-permute-done((bf16[384,1152]{1,0:T(8,128)(2,1)S(1)}, bf16[384,1152]{1,0:T(8,128)(2,1)S(1)}, u32[]{:S(2)}, u32[]{:S(2)}) %collective-permute-start.37) | collective-permute-done | bytes 884768 | tf_op jit(solution)/shard_map/ppermute | solution.py:68
  362.1 5.7 %down.2 = (bf16[512,1536]{1,0:T(8,128)(2,1)S(1)}, bf16[512,1536]{1,0:T(8,128)(2,1)S(1)}) custom-call(bf16[1024,1152]{1,0:T(8,128)(2,1)S(1)} %copy-done.5, bf16[1152,768]{1,0:T(8,128)(2,1)S(1)} %copy-done.19, bf16[1152,768]{1,0:T(8,128)(2,1)S(1)} %copy-done.7), custom_call_target="tpu_custom_call" | custom-call | flops 977500032 | bytes 3136500 | tf_op jit(solution)/shard_map/down/pallas_call | solution.py:558
  372.0 6.5 %collective-permute-done.44.rest = bf16[384,1152]{1,0:T(8,128)(2,1)S(1)} collective-permute-done((bf16[384,1152]{1,0:T(8,128)(2,1)S(1)}, bf16[384,1152]{1,0:T(8,128)(2,1)S(1)}, u32[]{:S(2)}, u32[]{:S(2)}) %collective-permute-start.44) | collective-permute-done | bytes 884768 | tf_op jit(solution)/shard_map/ppermute | solution.py:63
  384.2 5.9 %fusion.4 = (f32[512]{0:T(512)}, bf16[1536]{0:T(1024)(128)(2,1)S(1)}, f32[512,1536]{1,0:T(8,128)}) fusion(f32[1536]{0:T(1024)S(1)} %pad_maximum_fusion.12, bf16[512,768]{1,0:T(8,128)(2,1)} %collective-permute-done, bf16[512,768]{1,0:T(8,128)(2,1)S(1)} %copy-done.73, f32[512]{0:T(512)} %add_rsqrt_fusion, f32[512,1536]{1,0:T(8,128)S(1)} %fusion.10, ...), kind=kOutput, calls=%fused_computation.14 | convolution fusion | flops 1226831872 | bytes 14169088 | tf_op jit(solution)/shard_map/dot_general | solution.py:50
  400.1 15.9 %collective-permute-done.39.left = bf16[576,768]{1,0:T(8,128)(2,1)} collective-permute-done((bf16[576,768]{1,0:T(8,128)(2,1)}, bf16[576,768]{1,0:T(8,128)(2,1)}, u32[]{:S(2)}, u32[]{:S(2)}) %collective-permute-start.39) | collective-permute-done | bytes 884768 | tf_op jit(solution)/shard_map/ppermute | solution.py:63
  421.4 5.7 %down.3 = (bf16[512,1536]{1,0:T(8,128)(2,1)S(1)}, bf16[512,1536]{1,0:T(8,128)(2,1)S(1)}) custom-call(bf16[1024,1152]{1,0:T(8,128)(2,1)S(1)} %copy-done.3, bf16[1152,768]{1,0:T(8,128)(2,1)S(1)} %copy-done.20, bf16[1152,768]{1,0:T(8,128)(2,1)S(1)} %copy-done.8), custom_call_target="tpu_custom_call" | custom-call | flops 977500032 | bytes 3136500 | tf_op jit(solution)/shard_map/down/pallas_call | solution.py:558
  434.0 25.1 %collective-permute-done.53.left = bf16[576,768]{1,0:T(8,128)(2,1)S(1)} collective-permute-done((bf16[576,768]{1,0:T(8,128)(2,1)S(1)}, bf16[576,768]{1,0:T(8,128)(2,1)S(1)}, u32[]{:S(2)}, u32[]{:S(2)}) %collective-permute-start.53) | collective-permute-done | bytes 884768 | tf_op jit(solution)/shard_map/ppermute | solution.py:68
  465.9 20.1 %collective-permute-done.56.left = bf16[384,1152]{1,0:T(8,128)(2,1)S(1)} collective-permute-done((bf16[384,1152]{1,0:T(8,128)(2,1)S(1)}, bf16[384,1152]{1,0:T(8,128)(2,1)S(1)}, u32[]{:S(2)}, u32[]{:S(2)}) %collective-permute-start.56) | collective-permute-done | bytes 884768 | tf_op jit(solution)/shard_map/ppermute | solution.py:63
  488.9 6.1 %collective-permute-done.55 = bf16[512,1536]{1,0:T(8,128)(2,1)S(1)} collective-permute-done((bf16[512,1536]{1,0:T(8,128)(2,1)S(1)}, bf16[512,1536]{1,0:T(8,128)(2,1)S(1)}, u32[]{:S(2)}, u32[]{:S(2)}) %collective-permute-start.55) | collective-permute-done | bytes 1572896 | tf_op jit(solution)/shard_map/ppermute | solution.py:42
  495.7 8.8 %collective-permute-done.58.rest = bf16[576,768]{1,0:T(8,128)(2,1)S(1)} collective-permute-done((bf16[576,768]{1,0:T(8,128)(2,1)S(1)}, bf16[576,768]{1,0:T(8,128)(2,1)S(1)}, u32[]{:S(2)}, u32[]{:S(2)}) %collective-permute-start.58) | collective-permute-done | bytes 884768 | tf_op jit(solution)/shard_map/ppermute | solution.py:63
  508.7 15.7 %collective-permute-done.60.left = bf16[384,1152]{1,0:T(8,128)(2,1)S(1)} collective-permute-done((bf16[384,1152]{1,0:T(8,128)(2,1)S(1)}, bf16[384,1152]{1,0:T(8,128)(2,1)S(1)}, u32[]{:S(2)}, u32[]{:S(2)}) %collective-permute-start.60) | collective-permute-done | bytes 884768 | tf_op jit(solution)/shard_map/ppermute | solution.py:68
  529.3 11.0 %collective-permute-done.57 = bf16[512,768]{1,0:T(8,128)(2,1)S(1)} collective-permute-done((bf16[512,768]{1,0:T(8,128)(2,1)S(1)}, bf16[512,768]{1,0:T(8,128)(2,1)S(1)}, u32[]{:S(2)}, u32[]{:S(2)}) %collective-permute-start.57) | collective-permute-done | bytes 786464 | tf_op jit(solution)/shard_map/ppermute | solution.py:34
  (424 shorter events, 208.2 us)
Async XLA Ops:
  10.3 31.4 %collective-permute-start.2 = (bf16[768,384]{1,0:T(8,128)(2,1)}, bf16[768,384]{1,0:T(8,128)(2,1)}, u32[]{:S(2)}, u32[]{:S(2)}) collective-permute-start(bf16[768,384]{1,0:T(8,128)(2,1)} %param.13), channel_id=1, source_target_pairs={{0,2},{2,0},{1,3},{3,1},{4,6},{6,4},{5,7},{7,5},{8,10},{10,8},{9,1... | collective-permute-start | bytes 1769480 | tf_op jit(solution)/shard_map/ppermute | solution.py:42
  24.6 24.9 %collective-permute-start.3 = (bf16[768,640]{1,0:T(8,128)(2,1)}, bf16[768,640]{1,0:T(8,128)(2,1)S(1)}, u32[]{:S(2)}, u32[]{:S(2)}) collective-permute-start(bf16[768,640]{1,0:T(8,128)(2,1)} %pad_maximum_fusion.6), channel_id=1, source_target_pairs={{0,4},{4,0},{1,5},{5,1},{2,6},{6,2},{3,7},{7,3},{8,12},{12,8},{9,1... | collective-permute-start | bytes 2949128 | tf_op jit(solution)/shard_map/ppermute | solution.py:34
  29.1 38.8 %collective-permute-start.6 = (bf16[384,768]{1,0:T(8,128)(2,1)}, bf16[384,768]{1,0:T(8,128)(2,1)S(1)}, u32[]{:S(2)}, u32[]{:S(2)}) collective-permute-start(bf16[384,768]{1,0:T(8,128)(2,1)} %param.15), channel_id=1, source_target_pairs={{0,4},{4,0},{1,5},{5,1},{2,6},{6,2},{3,7},{7,3},{8,12},{12,8},{9,1... | collective-permute-start | bytes 1769480 | tf_op jit(solution)/shard_map/ppermute | solution.py:34
  31.1 36.8 %collective-permute-start.8 = (bf16[384,768]{1,0:T(8,128)(2,1)}, bf16[384,768]{1,0:T(8,128)(2,1)S(1)}, u32[]{:S(2)}, u32[]{:S(2)}) collective-permute-start(bf16[384,768]{1,0:T(8,128)(2,1)} %param.15), channel_id=1, source_target_pairs={{0,2},{2,0},{1,3},{3,1},{4,6},{6,4},{5,7},{7,5},{8,10},{10,8},{9,1... | collective-permute-start | bytes 1769480 | tf_op jit(solution)/shard_map/ppermute | solution.py:42
  53.7 33.0 %collective-permute-start.12 = (bf16[384,1152]{1,0:T(8,128)(2,1)S(1)}, bf16[384,1152]{1,0:T(8,128)(2,1)S(1)}, u32[]{:S(2)}, u32[]{:S(2)}) collective-permute-start(bf16[384,1152]{1,0:T(8,128)(2,1)S(1)} %copy-done.86), channel_id=1, source_target_pairs={{0,4},{4,0},{1,5},{5,1},{2,6},{6,2},{3,7},{7,3},{8,12},{12,8},{9,1... | collective-permute-start | bytes 2654216 | tf_op jit(solution)/shard_map/ppermute | solution.py:34
  72.4 33.3 %collective-permute-start.15 = (bf16[384,1152]{1,0:T(8,128)(2,1)S(1)}, bf16[384,1152]{1,0:T(8,128)(2,1)S(1)}, u32[]{:S(2)}, u32[]{:S(2)}) collective-permute-start(bf16[384,1152]{1,0:T(8,128)(2,1)S(1)} %copy-done.85), channel_id=1, source_target_pairs={{0,4},{4,0},{1,5},{5,1},{2,6},{6,2},{3,7},{7,3},{8,12},{12,8},{9,1... | collective-permute-start | bytes 2654216 | tf_op jit(solution)/shard_map/ppermute | solution.py:34
  89.3 35.3 %collective-permute-start.19 = (bf16[576,768]{1,0:T(8,128)(2,1)S(1)}, bf16[576,768]{1,0:T(8,128)(2,1)S(1)}, u32[]{:S(2)}, u32[]{:S(2)}) collective-permute-start(bf16[576,768]{1,0:T(8,128)(2,1)S(1)} %copy-done.84), channel_id=1, source_target_pairs={{0,4},{4,0},{1,5},{5,1},{2,6},{6,2},{3,7},{7,3},{8,12},{12,8},{9,1... | collective-permute-start | bytes 2654216 | tf_op jit(solution)/shard_map/ppermute | solution.py:34
  98.9 37.6 %collective-permute-start.21 = (bf16[512,1536]{1,0:T(8,128)(2,1)S(1)}, bf16[512,1536]{1,0:T(8,128)(2,1)S(1)}, u32[]{:S(2)}, u32[]{:S(2)}) collective-permute-start(bf16[512,1536]{1,0:T(8,128)(2,1)S(1)} %get-tuple-element.160.n2_a.refs_0_), channel_id=1, source_target_pairs={{0,2},{2,0},{1,3},{3,1},{4,6},{6,4},{5,7},{7,5},{8,10},{10,8},{9,1... | collective-permute-start | bytes 4718600 | tf_op jit(solution)/shard_map/ppermute | solution.py:42
  111.4 28.3 %collective-permute-start.17 = (bf16[512,768]{1,0:T(8,128)(2,1)S(1)}, bf16[512,768]{1,0:T(8,128)(2,1)S(1)}, u32[]{:S(2)}, u32[]{:S(2)}) collective-permute-start(bf16[512,768]{1,0:T(8,128)(2,1)S(1)} %copy-done.87), channel_id=1, source_target_pairs={{0,4},{4,0},{1,5},{5,1},{2,6},{6,2},{3,7},{7,3},{8,12},{12,8},{9,1... | collective-permute-start | bytes 2359304 | tf_op jit(solution)/shard_map/ppermute | solution.py:34
  139.8 41.9 %collective-permute-start.25 = (bf16[512,1536]{1,0:T(8,128)(2,1)S(1)}, bf16[512,1536]{1,0:T(8,128)(2,1)S(1)}, u32[]{:S(2)}, u32[]{:S(2)}) collective-permute-start(bf16[512,1536]{1,0:T(8,128)(2,1)S(1)} %collective-permute-done.21.n2_a.refs_2_), channel_id=1, source_target_pairs={{0,1},{1,0},{2,3},{3,2},{4,5},{5,4},{6,7},{7,6},{8,9},{9,8},{10,11... | collective-permute-start | bytes 4718600 | tf_op jit(solution)/shard_map/ppermute | solution.py:38
  215.4 41.8 %collective-permute-start.31 = (bf16[768,1152]{1,0:T(8,128)(2,1)}, bf16[768,1152]{1,0:T(8,128)(2,1)}, u32[]{:S(2)}, u32[]{:S(2)}) collective-permute-start(bf16[768,1152]{1,0:T(8,128)(2,1)} %w_gate_grad.2), channel_id=1, source_target_pairs={{0,4},{4,0},{1,5},{5,1},{2,6},{6,2},{3,7},{7,3},{8,12},{12,8},{9,1... | collective-permute-start | bytes 5308424 | tf_op jit(solution)/shard_map/ppermute | solution.py:34
  225.3 47.5 %collective-permute-start.30 = (bf16[512,1536]{1,0:T(8,128)(2,1)}, bf16[512,1536]{1,0:T(8,128)(2,1)}, u32[]{:S(2)}, u32[]{:S(2)}) collective-permute-start(bf16[512,1536]{1,0:T(8,128)(2,1)} %add_convert_fusion), channel_id=1, source_target_pairs={{0,2},{2,0},{1,3},{3,1},{4,6},{6,4},{5,7},{7,5},{8,10},{10,8},{9,1... | collective-permute-start | bytes 4718600 | tf_op jit(solution)/shard_map/ppermute | solution.py:42
  244.8 28.1 %collective-permute-start.29 = (bf16[512,1536]{1,0:T(8,128)(2,1)}, bf16[512,1536]{1,0:T(8,128)(2,1)}, u32[]{:S(2)}, u32[]{:S(2)}) collective-permute-start(bf16[512,1536]{1,0:T(8,128)(2,1)} %get-tuple-element.193), channel_id=1, source_target_pairs={{0,1},{1,0},{2,3},{3,2},{4,5},{5,4},{6,7},{7,6},{8,9},{9,8},{10,11... | collective-permute-start | bytes 4718600 | tf_op jit(solution)/shard_map/ppermute | solution.py:38
  244.9 49.7 %collective-permute-start.32 = (bf16[768,1152]{1,0:T(8,128)(2,1)}, bf16[768,1152]{1,0:T(8,128)(2,1)}, u32[]{:S(2)}, u32[]{:S(2)}) collective-permute-start(bf16[768,1152]{1,0:T(8,128)(2,1)} %copy-done.49), channel_id=1, source_target_pairs={{0,4},{4,0},{1,5},{5,1},{2,6},{6,2},{3,7},{7,3},{8,12},{12,8},{9,1... | collective-permute-start | bytes 5308424 | tf_op jit(solution)/shard_map/ppermute | solution.py:34
  297.9 53.9 %collective-permute-start.34 = (bf16[1152,768]{1,0:T(8,128)(2,1)S(1)}, bf16[1152,768]{1,0:T(8,128)(2,1)S(1)}, u32[]{:S(2)}, u32[]{:S(2)}) collective-permute-start(bf16[1152,768]{1,0:T(8,128)(2,1)S(1)} %w_down_grad.2), channel_id=1, source_target_pairs={{0,4},{4,0},{1,5},{5,1},{2,6},{6,2},{3,7},{7,3},{8,12},{12,8},{9,1... | collective-permute-start | bytes 5308424 | tf_op jit(solution)/shard_map/ppermute | solution.py:34
  307.6 43.7 %collective-permute-start.36 = (bf16[1536,384]{1,0:T(8,128)(2,1)S(1)}, bf16[1536,384]{1,0:T(8,128)(2,1)S(1)}, u32[]{:S(2)}, u32[]{:S(2)}) collective-permute-start(bf16[1536,384]{1,0:T(8,128)(2,1)S(1)} %get-tuple-element.303), channel_id=1, source_target_pairs={{0,2},{2,0},{1,3},{3,1},{4,6},{6,4},{5,7},{7,5},{8,10},{10,8},{9,1... | collective-permute-start | bytes 3538952 | tf_op jit(solution)/shard_map/ppermute | solution.py:42
  310.2 41.0 %collective-permute-start.37 = (bf16[384,1152]{1,0:T(8,128)(2,1)S(1)}, bf16[384,1152]{1,0:T(8,128)(2,1)S(1)}, u32[]{:S(2)}, u32[]{:S(2)}) collective-permute-start(bf16[384,1152]{1,0:T(8,128)(2,1)S(1)} %add.182.right), channel_id=1, source_target_pairs={{0,24},{8,16},{16,8},{24,0},{1,25},{9,17},{17,9},{25,1},{2,26},{10... | collective-permute-start | bytes 2654216 | tf_op jit(solution)/shard_map/ppermute | solution.py:68
  356.1 42.2 %collective-permute-start.40 = (bf16[384,1152]{1,0:T(8,128)(2,1)}, bf16[384,1152]{1,0:T(8,128)(2,1)}, u32[]{:S(2)}, u32[]{:S(2)}) collective-permute-start(bf16[384,1152]{1,0:T(8,128)(2,1)} %add.184.right), channel_id=1, source_target_pairs={{0,24},{8,16},{16,8},{24,0},{1,25},{9,17},{17,9},{25,1},{2,26},{10... | collective-permute-start | bytes 2654216 | tf_op jit(solution)/shard_map/ppermute | solution.py:68
  360.1 55.9 %collective-permute-start.39 = (bf16[576,768]{1,0:T(8,128)(2,1)}, bf16[576,768]{1,0:T(8,128)(2,1)}, u32[]{:S(2)}, u32[]{:S(2)}) collective-permute-start(bf16[576,768]{1,0:T(8,128)(2,1)} %get-tuple-element.219), channel_id=1, source_target_pairs={{0,8},{8,0},{16,24},{24,16},{1,9},{9,1},{17,25},{25,17},{2,10},{10... | collective-permute-start | bytes 2654216 | tf_op jit(solution)/shard_map/ppermute | solution.py:63
  378.5 48.6 %collective-permute-start.46 = (bf16[1536,384]{1,0:T(8,128)(2,1)}, bf16[1536,384]{1,0:T(8,128)(2,1)}, u32[]{:S(2)}, u32[]{:S(2)}) collective-permute-start(bf16[1536,384]{1,0:T(8,128)(2,1)} %get-tuple-element.301), channel_id=1, source_target_pairs={{0,2},{2,0},{1,3},{3,1},{4,6},{6,4},{5,7},{7,5},{8,10},{10,8},{9,1... | collective-permute-start | bytes 3538952 | tf_op jit(solution)/shard_map/ppermute | solution.py:42
  392.8 38.0 %collective-permute-start.48 = (bf16[512,1536]{1,0:T(8,128)(2,1)S(1)}, bf16[512,1536]{1,0:T(8,128)(2,1)S(1)}, u32[]{:S(2)}, u32[]{:S(2)}) collective-permute-start(bf16[512,1536]{1,0:T(8,128)(2,1)S(1)} %copy-done.65), channel_id=1, source_target_pairs={{0,1},{1,0},{2,3},{3,2},{4,5},{5,4},{6,7},{7,6},{8,9},{9,8},{10,11... | collective-permute-start | bytes 4718600 | tf_op jit(solution)/shard_map/ppermute | solution.py:38
  392.8 35.7 %collective-permute-start.45 = (bf16[768,384]{1,0:T(8,128)(2,1)S(1)}, bf16[768,384]{1,0:T(8,128)(2,1)S(1)}, u32[]{:S(2)}, u32[]{:S(2)}) collective-permute-start(bf16[768,384]{1,0:T(8,128)(2,1)S(1)} %get-tuple-element.313), channel_id=1, source_target_pairs={{0,4},{4,0},{1,5},{5,1},{2,6},{6,2},{3,7},{7,3},{8,12},{12,8},{9,1... | collective-permute-start | bytes 1769480 | tf_op jit(solution)/shard_map/ppermute | solution.py:34
  400.0 34.0 %collective-permute-start.54 = (bf16[384,1152]{1,0:T(8,128)(2,1)S(1)}, bf16[384,1152]{1,0:T(8,128)(2,1)S(1)}, u32[]{:S(2)}, u32[]{:S(2)}) collective-permute-start(bf16[384,1152]{1,0:T(8,128)(2,1)S(1)} %add.188.total), channel_id=1, source_target_pairs={{0,8},{8,0},{16,24},{24,16},{1,9},{9,1},{17,25},{25,17},{2,10},{10... | collective-permute-start | bytes 2654216 | tf_op jit(solution)/shard_map/ppermute | solution.py:63
  417.3 41.8 %collective-permute-start.53 = (bf16[576,768]{1,0:T(8,128)(2,1)S(1)}, bf16[576,768]{1,0:T(8,128)(2,1)S(1)}, u32[]{:S(2)}, u32[]{:S(2)}) collective-permute-start(bf16[576,768]{1,0:T(8,128)(2,1)S(1)} %add.189.right), channel_id=1, source_target_pairs={{0,24},{8,16},{16,8},{24,0},{1,25},{9,17},{17,9},{25,1},{2,26},{10... | collective-permute-start | bytes 2654216 | tf_op jit(solution)/shard_map/ppermute | solution.py:68
  429.1 33.4 %collective-permute-start.50 = (bf16[768,384]{1,0:T(8,128)(2,1)S(1)}, bf16[768,384]{1,0:T(8,128)(2,1)S(1)}, u32[]{:S(2)}, u32[]{:S(2)}) collective-permute-start(bf16[768,384]{1,0:T(8,128)(2,1)S(1)} %get-tuple-element.308), channel_id=1, source_target_pairs={{0,4},{4,0},{1,5},{5,1},{2,6},{6,2},{3,7},{7,3},{8,12},{12,8},{9,1... | collective-permute-start | bytes 1769480 | tf_op jit(solution)/shard_map/ppermute | solution.py:34
  430.8 31.7 %collective-permute-start.51 = (bf16[768,384]{1,0:T(8,128)(2,1)S(1)}, bf16[768,384]{1,0:T(8,128)(2,1)S(1)}, u32[]{:S(2)}, u32[]{:S(2)}) collective-permute-start(bf16[768,384]{1,0:T(8,128)(2,1)S(1)} %get-tuple-element.310), channel_id=1, source_target_pairs={{0,4},{4,0},{1,5},{5,1},{2,6},{6,2},{3,7},{7,3},{8,12},{12,8},{9,1... | collective-permute-start | bytes 1769480 | tf_op jit(solution)/shard_map/ppermute | solution.py:34
  432.0 30.6 %collective-permute-start.52 = (bf16[768,384]{1,0:T(8,128)(2,1)S(1)}, bf16[768,384]{1,0:T(8,128)(2,1)S(1)}, u32[]{:S(2)}, u32[]{:S(2)}) collective-permute-start(bf16[768,384]{1,0:T(8,128)(2,1)S(1)} %add.193), channel_id=1, source_target_pairs={{0,2},{2,0},{1,3},{3,1},{4,6},{6,4},{5,7},{7,5},{8,10},{10,8},{9,1... | collective-permute-start | bytes 1769480 | tf_op jit(solution)/shard_map/ppermute | solution.py:42
  434.0 31.5 %collective-permute-start.49 = (bf16[512,1536]{1,0:T(8,128)(2,1)S(1)}, bf16[512,1536]{1,0:T(8,128)(2,1)S(1)}, u32[]{:S(2)}, u32[]{:S(2)}) collective-permute-start(bf16[512,1536]{1,0:T(8,128)(2,1)S(1)} %get-tuple-element.240), channel_id=1, source_target_pairs={{0,1},{1,0},{2,3},{3,2},{4,5},{5,4},{6,7},{7,6},{8,9},{9,8},{10,11... | collective-permute-start | bytes 4718600 | tf_op jit(solution)/shard_map/ppermute | solution.py:38
  459.1 36.0 %collective-permute-start.55 = (bf16[512,1536]{1,0:T(8,128)(2,1)S(1)}, bf16[512,1536]{1,0:T(8,128)(2,1)S(1)}, u32[]{:S(2)}, u32[]{:S(2)}) collective-permute-start(bf16[512,1536]{1,0:T(8,128)(2,1)S(1)} %add.192), channel_id=1, source_target_pairs={{0,2},{2,0},{1,3},{3,1},{4,6},{6,4},{5,7},{7,5},{8,10},{10,8},{9,1... | collective-permute-start | bytes 4718600 | tf_op jit(solution)/shard_map/ppermute | solution.py:42
  465.4 39.1 %collective-permute-start.58 = (bf16[576,768]{1,0:T(8,128)(2,1)S(1)}, bf16[576,768]{1,0:T(8,128)(2,1)S(1)}, u32[]{:S(2)}, u32[]{:S(2)}) collective-permute-start(bf16[576,768]{1,0:T(8,128)(2,1)S(1)} %add.194.total), channel_id=1, source_target_pairs={{0,8},{8,0},{16,24},{24,16},{1,9},{9,1},{17,25},{25,17},{2,10},{10... | collective-permute-start | bytes 2654216 | tf_op jit(solution)/shard_map/ppermute | solution.py:63
  486.2 38.2 %collective-permute-start.60 = (bf16[384,1152]{1,0:T(8,128)(2,1)S(1)}, bf16[384,1152]{1,0:T(8,128)(2,1)S(1)}, u32[]{:S(2)}, u32[]{:S(2)}) collective-permute-start(bf16[384,1152]{1,0:T(8,128)(2,1)S(1)} %add.196.right), channel_id=1, source_target_pairs={{0,24},{8,16},{16,8},{24,0},{1,25},{9,17},{17,9},{25,1},{2,26},{10... | collective-permute-start | bytes 2654216 | tf_op jit(solution)/shard_map/ppermute | solution.py:68
  508.2 32.1 %collective-permute-start.57 = (bf16[512,768]{1,0:T(8,128)(2,1)S(1)}, bf16[512,768]{1,0:T(8,128)(2,1)S(1)}, u32[]{:S(2)}, u32[]{:S(2)}) collective-permute-start(bf16[512,768]{1,0:T(8,128)(2,1)S(1)} %slice.158), channel_id=1, source_target_pairs={{0,4},{4,0},{1,5},{5,1},{2,6},{6,2},{3,7},{7,3},{8,12},{12,8},{9,1... | collective-permute-start | bytes 2359304 | tf_op jit(solution)/shard_map/ppermute | solution.py:34
  (136 other events, 1744.5 us)

commit v5 on v4

--- a/solution.py
+++ b/solution.py
@@ -16,6 +16,8 @@
 BF16 = jnp.bfloat16
 F32 = jnp.float32
 VMEM_BYTES = 20 * 1024 * 1024
+MATMUL_VMEM_BYTES = 16 * 1024 * 1024
+SMALL_VMEM_BYTES = 8 * 1024 * 1024
 SCALE = 0.1
 
 
@@ -91,7 +93,7 @@
         in_specs=[tile, tile],
         out_specs=tile,
         out_shape=jax.ShapeDtypeStruct((rows, cols), BF16),
-        compiler_params=pltpu.CompilerParams(vmem_limit_bytes=VMEM_BYTES),
+        compiler_params=pltpu.CompilerParams(vmem_limit_bytes=SMALL_VMEM_BYTES),
         cost_estimate=lasting(2.2),
         name="add",
     )(left, right)
@@ -118,7 +120,7 @@
             out_specs=[out, out],
         ),
         out_shape=[shape, shape],
-        compiler_params=pltpu.CompilerParams(vmem_limit_bytes=VMEM_BYTES),
+        compiler_params=pltpu.CompilerParams(vmem_limit_bytes=SMALL_VMEM_BYTES),
         cost_estimate=lasting(2.4),
         name="split_add",
     )(side, own, other, own, other)
@@ -149,7 +151,7 @@
             out_specs=pl.BlockSpec(tile, lambda i, side: (i, 0)),
         ),
         out_shape=jax.ShapeDtypeStruct((2 * rows, cols), F32),
-        compiler_params=pltpu.CompilerParams(vmem_limit_bytes=VMEM_BYTES),
+        compiler_params=pltpu.CompilerParams(vmem_limit_bytes=SMALL_VMEM_BYTES),
         cost_estimate=lasting(4.0),
         name="join",
     )(side, total, rest)
@@ -230,7 +232,7 @@
         in_specs=[pl.BlockSpec(memory_space=pltpu.SMEM), whole, whole],
         out_specs=pl.BlockSpec((rows, cols), lambda i: (i, 0)),
         out_shape=jax.ShapeDtypeStruct((2 * rows, cols), straight.dtype),
-        compiler_params=pltpu.CompilerParams(vmem_limit_bytes=VMEM_BYTES),
+        compiler_params=pltpu.CompilerParams(vmem_limit_bytes=SMALL_VMEM_BYTES),
         cost_estimate=lasting(1.4),
         name="place_rows",
     )(jnp.reshape(odd, (1,)).astype(jnp.int32), straight, around)
@@ -352,7 +354,7 @@
             jax.ShapeDtypeStruct((rows, width), BF16),
             jax.ShapeDtypeStruct((rows, 1), F32),
         ],
-        compiler_params=pltpu.CompilerParams(vmem_limit_bytes=32 * 1024 * 1024),
+        compiler_params=pltpu.CompilerParams(vmem_limit_bytes=VMEM_BYTES),
         cost_estimate=lasting(5),
         name="attend_out",
     )(x, ctx_a, ctx_b, wo_a, wo_b, gain)
@@ -514,7 +516,7 @@
         in_specs=[left_spec(b) for b in lefts] + [right_spec(b) for b in rights],
         out_specs=pl.BlockSpec((width_left, tn), lambda j: (0, j)),
         out_shape=out,
-        compiler_params=pltpu.CompilerParams(vmem_limit_bytes=VMEM_BYTES),
+        compiler_params=pltpu.CompilerParams(vmem_limit_bytes=MATMUL_VMEM_BYTES),
         cost_estimate=lasting(7.5),
         name=name,
     )(*[b[0] for b in lefts], *[b[0] for b in rights])
@@ -563,7 +565,7 @@
         in_specs=[whole] * len(lefts) + specs * len(lefts),
         out_specs=[pl.BlockSpec((rows // 2, tn), lambda j: (0, j))] * 2,
         out_shape=[out] * 2,
-        compiler_params=pltpu.CompilerParams(vmem_limit_bytes=VMEM_BYTES),
+        compiler_params=pltpu.CompilerParams(vmem_limit_bytes=MATMUL_VMEM_BYTES),
         cost_estimate=lasting(8.5),
         name=name,
     )(*lefts, *flat)

time: 555 us -> 558 us (level)
  local copies, waits for them, and re-layouts: 28.4 us -> 34.1 us
    unnamed x213, local copies, waits for them, and re-layouts: 12.5 us -> 18.1 us
  transfers between devices with their start and end apart: 62 -> 62, of which waited for: 31 -> 31; matrix products, arithmetic and copies ran while one was open for 12% -> 11% of each run, Pallas kernels for 21% -> 21%
where the time goes in v5:
time: 558 us; the launch traced here: 550 us
  waiting for transfers between devices  235 us (42%)
  Pallas kernels  151 us (27%)
  starting transfers between devices  71.5 us (13%)
  local copies, waits for them, and re-layouts  34.1 us (6%)
  other arithmetic  33.5 us (6%)
  matrix products  22.6 us (4%)
    ppermute x11, waiting for transfers between devices, swap_pair(): return lax.ppermute(value, 'dp', [(i, i ^ 1) for i in range(count)])  72.2 us
    ppermute x18, waiting for transfers between devices, swap_row(): return lax.ppermute(value, 'row', [(0, 1), (1, 0)])  67.1 us
    ppermute x4, waiting for transfers between devices, swap_mirror(): return lax.ppermute(value, 'dp', [(i, count - 1 - i) for i in range(count)])  61.6 us
    pallas_call x6, Pallas kernels, weight_grad(): pl.pallas_call(weight_grad_kernel, grid=(pl.cdiv(width_right, tn),), in_s...  37 us
    pallas_call x2, Pallas kernels, feed(): pl.pallas_call(functools.partial(feed_kernel, tm=min(512, rows)), grid=(p...  34.3 us
    ppermute x12, waiting for transfers between devices, swap_far(): return lax.ppermute(value, 'col', [(0, 2), (2, 0), (1, 3), (3, 1)])  33.7 us
    ppermute x18, starting transfers between devices, swap_row(): return lax.ppermute(value, 'row', [(0, 1), (1, 0)])  32.7 us
    pallas_call x4, Pallas kernels, project(): pl.pallas_call(functools.partial(project_kernel, lefts=len(lefts), multip...  31.5 us
  transfers between devices with their start and end apart: 62, of which 31 were waited for; matrix products, arithmetic and copies ran while one was open for 11% of the time, Pallas kernels for 21%

profile of v5, /device:TPU:0, one launch (start us, length us, event | category | flops | bytes accessed | tf_op | source)
XLA Modules:
  0.0 550.3 jit_solution(8140223490628617196)
XLA Ops:
  16.2 8.4 %collective-permute-done.1 = f32[3584]{0:T(1024)} collective-permute-done((f32[3584]{0:T(1024)}, f32[3584]{0:T(1024)}, u32[]{:S(2)}, u32[]{:S(2)}) %collective-permute-start.1) | collective-permute-done | bytes 14368 | tf_op jit(solution)/shard_map/ppermute | solution.py:36
  41.7 7.8 %collective-permute-done.3 = bf16[768,640]{1,0:T(8,128)(2,1)S(1)} collective-permute-done((bf16[768,640]{1,0:T(8,128)(2,1)}, bf16[768,640]{1,0:T(8,128)(2,1)S(1)}, u32[]{:S(2)}, u32[]{:S(2)}) %collective-permute-start.3) | collective-permute-done | bytes 983072 | tf_op jit(solution)/shard_map/ppermute | solution.py:36
  54.2 13.6 %collective-permute-done.7 = bf16[512,256]{1,0:T(8,128)(2,1)S(1)} collective-permute-done((bf16[512,256]{1,0:T(8,128)(2,1)S(1)}, bf16[512,256]{1,0:T(8,128)(2,1)S(1)}, u32[]{:S(2)}, u32[]{:S(2)}) %collective-permute-start.7) | collective-permute-done | bytes 262176 | tf_op jit(solution)/shard_map/ppermute | solution.py:36
  78.5 6.3 %attend_forward.1 = (bf16[512,768]{1,0:T(8,128)(2,1)S(1)}, bf16[512,768]{1,0:T(8,128)(2,1)S(1)}, f32[512,128]{1,0:T(8,128)S(1)}) custom-call(s32[1]{0:T(128)} %bitcast.start, bf16[512,768]{1,0:T(8,128)(2,1)S(1)} %convolution_convert_fusion.8.q_a, bf16[512,768]{1,0:T(8,128)(2,1)S(1)} %convolution_convert_fusion.7.q_b, ...), custom_call_target="tpu_custom_call" | custom-call | flops 920000000 | bytes 2952000 | tf_op jit(solution)/shard_map/attend_forward/pallas_call | solution.py:312
  89.6 6.4 %collective-permute-start.19 = (bf16[576,768]{1,0:T(8,128)(2,1)S(1)}, bf16[576,768]{1,0:T(8,128)(2,1)S(1)}, u32[]{:S(2)}, u32[]{:S(2)}) collective-permute-start(bf16[576,768]{1,0:T(8,128)(2,1)S(1)} %copy-done.84), channel_id=1, source_target_pairs={{0,4},{4,0},{1,5},{5,1},{2,6},{6,2},{3,7},{7,3},{8,12},{12,8},{9,1... | collective-permute-start | bytes 2654216 | tf_op jit(solution)/shard_map/ppermute | solution.py:36
  111.5 6.7 %collective-permute-start.17 = (bf16[512,768]{1,0:T(8,128)(2,1)S(1)}, bf16[512,768]{1,0:T(8,128)(2,1)S(1)}, u32[]{:S(2)}, u32[]{:S(2)}) collective-permute-start(bf16[512,768]{1,0:T(8,128)(2,1)S(1)} %copy-done.87), channel_id=1, source_target_pairs={{0,4},{4,0},{1,5},{5,1},{2,6},{6,2},{3,7},{7,3},{8,12},{12,8},{9,1... | collective-permute-start | bytes 2359304 | tf_op jit(solution)/shard_map/ppermute | solution.py:36
  118.1 6.5 %collective-permute-done.19.straight = bf16[576,768]{1,0:T(8,128)(2,1)S(1)} collective-permute-done((bf16[576,768]{1,0:T(8,128)(2,1)S(1)}, bf16[576,768]{1,0:T(8,128)(2,1)S(1)}, u32[]{:S(2)}, u32[]{:S(2)}) %collective-permute-start.19) | collective-permute-done | bytes 884768 | tf_op jit(solution)/shard_map/ppermute | solution.py:36
  124.6 7.3 %collective-permute-done.20.around = bf16[384,1152]{1,0:T(8,128)(2,1)S(1)} collective-permute-done((bf16[384,1152]{1,0:T(8,128)(2,1)S(1)}, bf16[384,1152]{1,0:T(8,128)(2,1)S(1)}, u32[]{:S(2)}, u32[]{:S(2)}) %collective-permute-start.20) | collective-permute-done | bytes 884768 | tf_op jit(solution)/shard_map/ppermute | solution.py:65
  131.9 5.9 %collective-permute-done.21.n2_a.refs_2_ = bf16[512,1536]{1,0:T(8,128)(2,1)S(1)} collective-permute-done((bf16[512,1536]{1,0:T(8,128)(2,1)S(1)}, bf16[512,1536]{1,0:T(8,128)(2,1)S(1)}, u32[]{:S(2)}, u32[]{:S(2)}) %collective-permute-start.21) | collective-permute-done | bytes 1572896 | tf_op jit(solution)/shard_map/ppermute | solution.py:44
  142.9 16.9 %collective-permute-done.26.dy_b.refs_6_ = bf16[512,768]{1,0:T(8,128)(2,1)S(1)} collective-permute-done((bf16[512,768]{1,0:T(8,128)(2,1)S(1)}, bf16[512,768]{1,0:T(8,128)(2,1)S(1)}, u32[]{:S(2)}, u32[]{:S(2)}) %collective-permute-start.26) | collective-permute-done | bytes 786464 | tf_op jit(solution)/shard_map/ppermute | solution.py:44
  163.2 17.2 %feed.2 = (bf16[1024,1152]{1,0:T(8,128)(2,1)S(1)}, bf16[1024,1152]{1,0:T(8,128)(2,1)S(1)}, bf16[1024,1152]{1,0:T(8,128)(2,1)S(1)}) custom-call(bf16[512,1536]{1,0:T(8,128)(2,1)S(1)} %get-tuple-element.160.n2_a.refs_0_, bf16[512,1536]{1,0:T(8,128)(2,1)S(1)} %collective-permute-done.14.n2_b.refs_1_, bf16[512,768]{1,0:T(8,128)(2,1)} %get-tuple-element.165.dy_a.refs_4_, ...), custom_call_target="tpu_custom_call" | custom-call | flops 2012499968 | bytes 6457500 | tf_op jit(solution)/shard_map/feed/pallas_call | solution.py:473
  181.9 17.2 %feed.3 = (bf16[1024,1152]{1,0:T(8,128)(2,1)S(1)}, bf16[1024,1152]{1,0:T(8,128)(2,1)S(1)}, bf16[1024,1152]{1,0:T(8,128)(2,1)S(1)}) custom-call(bf16[512,1536]{1,0:T(8,128)(2,1)S(1)} %collective-permute-done.21.n2_a.refs_2_, bf16[512,1536]{1,0:T(8,128)(2,1)S(1)} %collective-permute-done.25.n2_b.refs_3_, bf16[512,768]{1,0:T(8,128)(2,1)} %collective-permute-done.4.dy_a.refs_6_, ...), custom_call_target="tpu_custom_call" | custom-call | flops 2012499968 | bytes 6457500 | tf_op jit(solution)/shard_map/feed/pallas_call | solution.py:473
  199.1 7.0 %w_gate_grad.2 = bf16[768,1152]{1,0:T(8,128)(2,1)} custom-call(bf16[512,1536]{1,0:T(8,128)(2,1)S(1)} %get-tuple-element.160.n2_a.refs_0_, bf16[512,1536]{1,0:T(8,128)(2,1)S(1)} %collective-permute-done.14.n2_b.refs_1_, bf16[512,1536]{1,0:T(8,128)(2,1)S(1)} %collective-permute-done.21.n2_a.refs_2_, ...), custom_call_target="tpu_custom_call" | custom-call | flops 862499968 | bytes 2767500 | tf_op jit(solution)/shard_map/w_gate_grad/pallas_call | solution.py:513
  206.1 9.6 %feed_back.2 = (bf16[512,1536]{1,0:T(8,128)(2,1)S(1)}, bf16[512,1536]{1,0:T(8,128)(2,1)S(1)}) custom-call(bf16[1024,1152]{1,0:T(8,128)(2,1)S(1)} %get-tuple-element.188.refs_6_.refs_7_.refs_0_, bf16[1024,1152]{1,0:T(8,128)(2,1)S(1)} %get-tuple-element.197.refs_1_.refs_6_.refs_7_, bf16[768,1152]{1,0:T(8,128)(2,1)S(1)} %copy-done.22, ...), custom_call_target="tpu_custom_call" | custom-call | flops 977500032 | bytes 3136500 | tf_op jit(solution)/shard_map/feed_back/pallas_call | solution.py:560
  217.4 6.5 %w_gate_grad.3.own_a.own_b = bf16[768,1152]{1,0:T(8,128)(2,1)S(1)} custom-call(bf16[512,1536]{1,0:T(8,128)(2,1)S(1)} %get-tuple-element.160.n2_a.refs_0_, bf16[512,1536]{1,0:T(8,128)(2,1)S(1)} %collective-permute-done.14.n2_b.refs_1_, bf16[512,1536]{1,0:T(8,128)(2,1)S(1)} %collective-permute-done.21.n2_a.refs_2_, ...), custom_call_target="tpu_custom_call" | custom-call | flops 862499968 | bytes 2767500 | tf_op jit(solution)/shard_map/w_gate_grad/pallas_call | solution.py:513
  228.0 6.5 %w_up_grad.2 = bf16[768,1152]{1,0:T(8,128)(2,1)S(1)} custom-call(bf16[512,1536]{1,0:T(8,128)(2,1)S(1)} %get-tuple-element.160.n2_a.refs_0_, bf16[512,1536]{1,0:T(8,128)(2,1)S(1)} %collective-permute-done.14.n2_b.refs_1_, bf16[512,1536]{1,0:T(8,128)(2,1)S(1)} %collective-permute-done.21.n2_a.refs_2_, ...), custom_call_target="tpu_custom_call" | custom-call | flops 862499968 | bytes 2767500 | tf_op jit(solution)/shard_map/w_up_grad/pallas_call | solution.py:513
  235.8 10.4 %feed_back.3 = (bf16[512,1536]{1,0:T(8,128)(2,1)S(1)}, bf16[512,1536]{1,0:T(8,128)(2,1)}) custom-call(bf16[1024,1152]{1,0:T(8,128)(2,1)S(1)} %get-tuple-element.191.refs_4_.refs_5_.refs_0_, bf16[1024,1152]{1,0:T(8,128)(2,1)S(1)} %get-tuple-element.182.refs_4_.refs_5_.refs_1_, bf16[768,1152]{1,0:T(8,128)(2,1)S(1)} %copy-done.22, ...), custom_call_target="tpu_custom_call" | custom-call | flops 977500032 | bytes 3136500 | tf_op jit(solution)/shard_map/feed_back/pallas_call | solution.py:560
  248.2 9.4 %collective-permute-done.31.other_a.other_b = bf16[768,1152]{1,0:T(8,128)(2,1)} collective-permute-done((bf16[768,1152]{1,0:T(8,128)(2,1)}, bf16[768,1152]{1,0:T(8,128)(2,1)}, u32[]{:S(2)}, u32[]{:S(2)}) %collective-permute-start.31) | collective-permute-done | bytes 1769504 | tf_op jit(solution)/shard_map/ppermute | solution.py:36
  265.5 6.5 %w_up_grad.3.own_a.own_b = bf16[768,1152]{1,0:T(8,128)(2,1)S(1)} custom-call(bf16[512,1536]{1,0:T(8,128)(2,1)S(1)} %copy-done.10, bf16[512,1536]{1,0:T(8,128)(2,1)S(1)} %copy-done.12, bf16[512,1536]{1,0:T(8,128)(2,1)S(1)} %copy-done.14, bf16[512,1536]{1,0:T(8,128)(2,1)S(1)} %copy-done.16, bf16[1024,1152]{1,0:T(8,128)(2,1)S(1)} %get-tuple-element.182.refs_4_.refs_5_.refs_1_, ...), custom_call_target="tpu_custom_call" | custom-call | flops 862499968 | bytes 2767500 | tf_op jit(solution)/shard_map/w_up_grad/pallas_call | solution.py:513
  299.9 5.7 %w_down_grad.3.own_a.own_b = bf16[1152,768]{1,0:T(8,128)(2,1)S(1)} custom-call(bf16[1024,1152]{1,0:T(8,128)(2,1)S(1)} %copy-done.3, bf16[1024,1152]{1,0:T(8,128)(2,1)S(1)} %copy-done.3, bf16[1024,1152]{1,0:T(8,128)(2,1)S(1)} %copy-done.5, bf16[1024,1152]{1,0:T(8,128)(2,1)S(1)} %copy-done.5, bf16[512,768]{1,0:T(8,128)(2,1)} %get-tuple-element.165.dy_a.refs_4_, ...), custom_call_target="tpu_custom_call" | custom-call | flops 862499968 | bytes 2767500 | tf_op jit(solution)/shard_map/w_down_grad/pallas_call | solution.py:513
  313.0 14.8 %attend_backward.1 = (bf16[512,768]{1,0:T(8,128)(2,1)S(1)}, bf16[512,768]{1,0:T(8,128)(2,1)S(1)}, f32[2048,256]{1,0:T(8,128)S(1)}) custom-call(s32[1]{0:T(128)} %bitcast.start, bf16[512,768]{1,0:T(8,128)(2,1)S(1)} %copy-done.67, bf16[512,768]{1,0:T(8,128)(2,1)S(1)} %copy-done.69, bf16[2048,256]{1,0:T(8,128)(2,1)S(1)} %copy-done.53, s32[512,1]{1,0:T(8,128)S(1)} %copy-done.63, ...), custom_call_target="tpu_custom_call" | custom-call | flops 2300000000 | bytes 7380000 | tf_op jit(solution)/shard_map/attend_backward/pallas_call | solution.py:417
  331.6 19.9 %collective-permute-done.37.left = bf16[384,1152]{1,0:T(8,128)(2,1)S(1)} collective-permute-done((bf16[384,1152]{1,0:T(8,128)(2,1)S(1)}, bf16[384,1152]{1,0:T(8,128)(2,1)S(1)}, u32[]{:S(2)}, u32[]{:S(2)}) %collective-permute-start.37) | collective-permute-done | bytes 884768 | tf_op jit(solution)/shard_map/ppermute | solution.py:70
  363.3 5.8 %down.2 = (bf16[512,1536]{1,0:T(8,128)(2,1)S(1)}, bf16[512,1536]{1,0:T(8,128)(2,1)S(1)}) custom-call(bf16[1024,1152]{1,0:T(8,128)(2,1)S(1)} %copy-done.5, bf16[1152,768]{1,0:T(8,128)(2,1)S(1)} %copy-done.19, bf16[1152,768]{1,0:T(8,128)(2,1)S(1)} %copy-done.7), custom_call_target="tpu_custom_call" | custom-call | flops 977500032 | bytes 3136500 | tf_op jit(solution)/shard_map/down/pallas_call | solution.py:560
  373.1 6.6 %collective-permute-done.44.rest = bf16[384,1152]{1,0:T(8,128)(2,1)S(1)} collective-permute-done((bf16[384,1152]{1,0:T(8,128)(2,1)S(1)}, bf16[384,1152]{1,0:T(8,128)(2,1)S(1)}, u32[]{:S(2)}, u32[]{:S(2)}) %collective-permute-start.44) | collective-permute-done | bytes 884768 | tf_op jit(solution)/shard_map/ppermute | solution.py:65
  385.3 5.9 %fusion.4 = (f32[512]{0:T(512)}, bf16[1536]{0:T(1024)(128)(2,1)S(1)}, f32[512,1536]{1,0:T(8,128)}) fusion(f32[1536]{0:T(1024)S(1)} %pad_maximum_fusion.12, bf16[512,768]{1,0:T(8,128)(2,1)} %collective-permute-done, bf16[512,768]{1,0:T(8,128)(2,1)S(1)} %copy-done.73, f32[512]{0:T(512)} %add_rsqrt_fusion, f32[512,1536]{1,0:T(8,128)S(1)} %fusion.10, ...), kind=kOutput, calls=%fused_computation.14 | convolution fusion | flops 1226831872 | bytes 14169088 | tf_op jit(solution)/shard_map/dot_general | solution.py:52
  401.3 15.9 %collective-permute-done.39.left = bf16[576,768]{1,0:T(8,128)(2,1)} collective-permute-done((bf16[576,768]{1,0:T(8,128)(2,1)}, bf16[576,768]{1,0:T(8,128)(2,1)}, u32[]{:S(2)}, u32[]{:S(2)}) %collective-permute-start.39) | collective-permute-done | bytes 884768 | tf_op jit(solution)/shard_map/ppermute | solution.py:65
  435.2 25.1 %collective-permute-done.53.left = bf16[576,768]{1,0:T(8,128)(2,1)S(1)} collective-permute-done((bf16[576,768]{1,0:T(8,128)(2,1)S(1)}, bf16[576,768]{1,0:T(8,128)(2,1)S(1)}, u32[]{:S(2)}, u32[]{:S(2)}) %collective-permute-start.53) | collective-permute-done | bytes 884768 | tf_op jit(solution)/shard_map/ppermute | solution.py:70
  467.1 20.1 %collective-permute-done.56.left = bf16[384,1152]{1,0:T(8,128)(2,1)S(1)} collective-permute-done((bf16[384,1152]{1,0:T(8,128)(2,1)S(1)}, bf16[384,1152]{1,0:T(8,128)(2,1)S(1)}, u32[]{:S(2)}, u32[]{:S(2)}) %collective-permute-start.56) | collective-permute-done | bytes 884768 | tf_op jit(solution)/shard_map/ppermute | solution.py:65
  490.1 6.1 %collective-permute-done.55 = bf16[512,1536]{1,0:T(8,128)(2,1)S(1)} collective-permute-done((bf16[512,1536]{1,0:T(8,128)(2,1)S(1)}, bf16[512,1536]{1,0:T(8,128)(2,1)S(1)}, u32[]{:S(2)}, u32[]{:S(2)}) %collective-permute-start.55) | collective-permute-done | bytes 1572896 | tf_op jit(solution)/shard_map/ppermute | solution.py:44
  496.9 8.8 %collective-permute-done.58.rest = bf16[576,768]{1,0:T(8,128)(2,1)S(1)} collective-permute-done((bf16[576,768]{1,0:T(8,128)(2,1)S(1)}, bf16[576,768]{1,0:T(8,128)(2,1)S(1)}, u32[]{:S(2)}, u32[]{:S(2)}) %collective-permute-start.58) | collective-permute-done | bytes 884768 | tf_op jit(solution)/shard_map/ppermute | solution.py:65
  509.9 15.7 %collective-permute-done.60.left = bf16[384,1152]{1,0:T(8,128)(2,1)S(1)} collective-permute-done((bf16[384,1152]{1,0:T(8,128)(2,1)S(1)}, bf16[384,1152]{1,0:T(8,128)(2,1)S(1)}, u32[]{:S(2)}, u32[]{:S(2)}) %collective-permute-start.60) | collective-permute-done | bytes 884768 | tf_op jit(solution)/shard_map/ppermute | solution.py:70
  530.5 11.0 %collective-permute-done.57 = bf16[512,768]{1,0:T(8,128)(2,1)S(1)} collective-permute-done((bf16[512,768]{1,0:T(8,128)(2,1)S(1)}, bf16[512,768]{1,0:T(8,128)(2,1)S(1)}, u32[]{:S(2)}, u32[]{:S(2)}) %collective-permute-start.57) | collective-permute-done | bytes 786464 | tf_op jit(solution)/shard_map/ppermute | solution.py:36
  (424 shorter events, 210.5 us)
Async XLA Ops:
  10.3 31.4 %collective-permute-start.2 = (bf16[768,384]{1,0:T(8,128)(2,1)}, bf16[768,384]{1,0:T(8,128)(2,1)}, u32[]{:S(2)}, u32[]{:S(2)}) collective-permute-start(bf16[768,384]{1,0:T(8,128)(2,1)} %param.13), channel_id=1, source_target_pairs={{0,2},{2,0},{1,3},{3,1},{4,6},{6,4},{5,7},{7,5},{8,10},{10,8},{9,1... | collective-permute-start | bytes 1769480 | tf_op jit(solution)/shard_map/ppermute | solution.py:44
  24.6 24.9 %collective-permute-start.3 = (bf16[768,640]{1,0:T(8,128)(2,1)}, bf16[768,640]{1,0:T(8,128)(2,1)S(1)}, u32[]{:S(2)}, u32[]{:S(2)}) collective-permute-start(bf16[768,640]{1,0:T(8,128)(2,1)} %pad_maximum_fusion.6), channel_id=1, source_target_pairs={{0,4},{4,0},{1,5},{5,1},{2,6},{6,2},{3,7},{7,3},{8,12},{12,8},{9,1... | collective-permute-start | bytes 2949128 | tf_op jit(solution)/shard_map/ppermute | solution.py:36
  29.1 38.8 %collective-permute-start.6 = (bf16[384,768]{1,0:T(8,128)(2,1)}, bf16[384,768]{1,0:T(8,128)(2,1)S(1)}, u32[]{:S(2)}, u32[]{:S(2)}) collective-permute-start(bf16[384,768]{1,0:T(8,128)(2,1)} %param.15), channel_id=1, source_target_pairs={{0,4},{4,0},{1,5},{5,1},{2,6},{6,2},{3,7},{7,3},{8,12},{12,8},{9,1... | collective-permute-start | bytes 1769480 | tf_op jit(solution)/shard_map/ppermute | solution.py:36
  31.1 36.8 %collective-permute-start.8 = (bf16[384,768]{1,0:T(8,128)(2,1)}, bf16[384,768]{1,0:T(8,128)(2,1)S(1)}, u32[]{:S(2)}, u32[]{:S(2)}) collective-permute-start(bf16[384,768]{1,0:T(8,128)(2,1)} %param.15), channel_id=1, source_target_pairs={{0,2},{2,0},{1,3},{3,1},{4,6},{6,4},{5,7},{7,5},{8,10},{10,8},{9,1... | collective-permute-start | bytes 1769480 | tf_op jit(solution)/shard_map/ppermute | solution.py:44
  53.7 33.0 %collective-permute-start.12 = (bf16[384,1152]{1,0:T(8,128)(2,1)S(1)}, bf16[384,1152]{1,0:T(8,128)(2,1)S(1)}, u32[]{:S(2)}, u32[]{:S(2)}) collective-permute-start(bf16[384,1152]{1,0:T(8,128)(2,1)S(1)} %copy-done.86), channel_id=1, source_target_pairs={{0,4},{4,0},{1,5},{5,1},{2,6},{6,2},{3,7},{7,3},{8,12},{12,8},{9,1... | collective-permute-start | bytes 2654216 | tf_op jit(solution)/shard_map/ppermute | solution.py:36
  72.3 33.3 %collective-permute-start.15 = (bf16[384,1152]{1,0:T(8,128)(2,1)S(1)}, bf16[384,1152]{1,0:T(8,128)(2,1)S(1)}, u32[]{:S(2)}, u32[]{:S(2)}) collective-permute-start(bf16[384,1152]{1,0:T(8,128)(2,1)S(1)} %copy-done.85), channel_id=1, source_target_pairs={{0,4},{4,0},{1,5},{5,1},{2,6},{6,2},{3,7},{7,3},{8,12},{12,8},{9,1... | collective-permute-start | bytes 2654216 | tf_op jit(solution)/shard_map/ppermute | solution.py:36
  89.6 35.0 %collective-permute-start.19 = (bf16[576,768]{1,0:T(8,128)(2,1)S(1)}, bf16[576,768]{1,0:T(8,128)(2,1)S(1)}, u32[]{:S(2)}, u32[]{:S(2)}) collective-permute-start(bf16[576,768]{1,0:T(8,128)(2,1)S(1)} %copy-done.84), channel_id=1, source_target_pairs={{0,4},{4,0},{1,5},{5,1},{2,6},{6,2},{3,7},{7,3},{8,12},{12,8},{9,1... | collective-permute-start | bytes 2654216 | tf_op jit(solution)/shard_map/ppermute | solution.py:36
  101.0 36.8 %collective-permute-start.21 = (bf16[512,1536]{1,0:T(8,128)(2,1)S(1)}, bf16[512,1536]{1,0:T(8,128)(2,1)S(1)}, u32[]{:S(2)}, u32[]{:S(2)}) collective-permute-start(bf16[512,1536]{1,0:T(8,128)(2,1)S(1)} %get-tuple-element.160.n2_a.refs_0_), channel_id=1, source_target_pairs={{0,2},{2,0},{1,3},{3,1},{4,6},{6,4},{5,7},{7,5},{8,10},{10,8},{9,1... | collective-permute-start | bytes 4718600 | tf_op jit(solution)/shard_map/ppermute | solution.py:44
  111.5 28.2 %collective-permute-start.17 = (bf16[512,768]{1,0:T(8,128)(2,1)S(1)}, bf16[512,768]{1,0:T(8,128)(2,1)S(1)}, u32[]{:S(2)}, u32[]{:S(2)}) collective-permute-start(bf16[512,768]{1,0:T(8,128)(2,1)S(1)} %copy-done.87), channel_id=1, source_target_pairs={{0,4},{4,0},{1,5},{5,1},{2,6},{6,2},{3,7},{7,3},{8,12},{12,8},{9,1... | collective-permute-start | bytes 2359304 | tf_op jit(solution)/shard_map/ppermute | solution.py:36
  139.8 42.1 %collective-permute-start.25 = (bf16[512,1536]{1,0:T(8,128)(2,1)S(1)}, bf16[512,1536]{1,0:T(8,128)(2,1)S(1)}, u32[]{:S(2)}, u32[]{:S(2)}) collective-permute-start(bf16[512,1536]{1,0:T(8,128)(2,1)S(1)} %collective-permute-done.21.n2_a.refs_2_), channel_id=1, source_target_pairs={{0,1},{1,0},{2,3},{3,2},{4,5},{5,4},{6,7},{7,6},{8,9},{9,8},{10,11... | collective-permute-start | bytes 4718600 | tf_op jit(solution)/shard_map/ppermute | solution.py:40
  215.8 41.8 %collective-permute-start.31 = (bf16[768,1152]{1,0:T(8,128)(2,1)}, bf16[768,1152]{1,0:T(8,128)(2,1)}, u32[]{:S(2)}, u32[]{:S(2)}) collective-permute-start(bf16[768,1152]{1,0:T(8,128)(2,1)} %w_gate_grad.2), channel_id=1, source_target_pairs={{0,4},{4,0},{1,5},{5,1},{2,6},{6,2},{3,7},{7,3},{8,12},{12,8},{9,1... | collective-permute-start | bytes 5308424 | tf_op jit(solution)/shard_map/ppermute | solution.py:36
  226.7 46.5 %collective-permute-start.30 = (bf16[512,1536]{1,0:T(8,128)(2,1)}, bf16[512,1536]{1,0:T(8,128)(2,1)}, u32[]{:S(2)}, u32[]{:S(2)}) collective-permute-start(bf16[512,1536]{1,0:T(8,128)(2,1)} %add_convert_fusion), channel_id=1, source_target_pairs={{0,2},{2,0},{1,3},{3,1},{4,6},{6,4},{5,7},{7,5},{8,10},{10,8},{9,1... | collective-permute-start | bytes 4718600 | tf_op jit(solution)/shard_map/ppermute | solution.py:44
  247.5 25.8 %collective-permute-start.29 = (bf16[512,1536]{1,0:T(8,128)(2,1)}, bf16[512,1536]{1,0:T(8,128)(2,1)}, u32[]{:S(2)}, u32[]{:S(2)}) collective-permute-start(bf16[512,1536]{1,0:T(8,128)(2,1)} %get-tuple-element.193), channel_id=1, source_target_pairs={{0,1},{1,0},{2,3},{3,2},{4,5},{5,4},{6,7},{7,6},{8,9},{9,8},{10,11... | collective-permute-start | bytes 4718600 | tf_op jit(solution)/shard_map/ppermute | solution.py:40
  247.6 47.5 %collective-permute-start.32 = (bf16[768,1152]{1,0:T(8,128)(2,1)}, bf16[768,1152]{1,0:T(8,128)(2,1)}, u32[]{:S(2)}, u32[]{:S(2)}) collective-permute-start(bf16[768,1152]{1,0:T(8,128)(2,1)} %copy-done.49), channel_id=1, source_target_pairs={{0,4},{4,0},{1,5},{5,1},{2,6},{6,2},{3,7},{7,3},{8,12},{12,8},{9,1... | collective-permute-start | bytes 5308424 | tf_op jit(solution)/shard_map/ppermute | solution.py:36
  298.3 53.8 %collective-permute-start.34 = (bf16[1152,768]{1,0:T(8,128)(2,1)S(1)}, bf16[1152,768]{1,0:T(8,128)(2,1)S(1)}, u32[]{:S(2)}, u32[]{:S(2)}) collective-permute-start(bf16[1152,768]{1,0:T(8,128)(2,1)S(1)} %w_down_grad.2), channel_id=1, source_target_pairs={{0,4},{4,0},{1,5},{5,1},{2,6},{6,2},{3,7},{7,3},{8,12},{12,8},{9,1... | collective-permute-start | bytes 5308424 | tf_op jit(solution)/shard_map/ppermute | solution.py:36
  308.0 43.7 %collective-permute-start.36 = (bf16[1536,384]{1,0:T(8,128)(2,1)S(1)}, bf16[1536,384]{1,0:T(8,128)(2,1)S(1)}, u32[]{:S(2)}, u32[]{:S(2)}) collective-permute-start(bf16[1536,384]{1,0:T(8,128)(2,1)S(1)} %get-tuple-element.303), channel_id=1, source_target_pairs={{0,2},{2,0},{1,3},{3,1},{4,6},{6,4},{5,7},{7,5},{8,10},{10,8},{9,1... | collective-permute-start | bytes 3538952 | tf_op jit(solution)/shard_map/ppermute | solution.py:44
  310.5 41.0 %collective-permute-start.37 = (bf16[384,1152]{1,0:T(8,128)(2,1)S(1)}, bf16[384,1152]{1,0:T(8,128)(2,1)S(1)}, u32[]{:S(2)}, u32[]{:S(2)}) collective-permute-start(bf16[384,1152]{1,0:T(8,128)(2,1)S(1)} %add.182.right), channel_id=1, source_target_pairs={{0,24},{8,16},{16,8},{24,0},{1,25},{9,17},{17,9},{25,1},{2,26},{10... | collective-permute-start | bytes 2654216 | tf_op jit(solution)/shard_map/ppermute | solution.py:70
  357.2 42.2 %collective-permute-start.40 = (bf16[384,1152]{1,0:T(8,128)(2,1)}, bf16[384,1152]{1,0:T(8,128)(2,1)}, u32[]{:S(2)}, u32[]{:S(2)}) collective-permute-start(bf16[384,1152]{1,0:T(8,128)(2,1)} %add.184.right), channel_id=1, source_target_pairs={{0,24},{8,16},{16,8},{24,0},{1,25},{9,17},{17,9},{25,1},{2,26},{10... | collective-permute-start | bytes 2654216 | tf_op jit(solution)/shard_map/ppermute | solution.py:70
  361.3 55.9 %collective-permute-start.39 = (bf16[576,768]{1,0:T(8,128)(2,1)}, bf16[576,768]{1,0:T(8,128)(2,1)}, u32[]{:S(2)}, u32[]{:S(2)}) collective-permute-start(bf16[576,768]{1,0:T(8,128)(2,1)} %get-tuple-element.219), channel_id=1, source_target_pairs={{0,8},{8,0},{16,24},{24,16},{1,9},{9,1},{17,25},{25,17},{2,10},{10... | collective-permute-start | bytes 2654216 | tf_op jit(solution)/shard_map/ppermute | solution.py:65
  379.7 48.6 %collective-permute-start.46 = (bf16[1536,384]{1,0:T(8,128)(2,1)}, bf16[1536,384]{1,0:T(8,128)(2,1)}, u32[]{:S(2)}, u32[]{:S(2)}) collective-permute-start(bf16[1536,384]{1,0:T(8,128)(2,1)} %get-tuple-element.301), channel_id=1, source_target_pairs={{0,2},{2,0},{1,3},{3,1},{4,6},{6,4},{5,7},{7,5},{8,10},{10,8},{9,1... | collective-permute-start | bytes 3538952 | tf_op jit(solution)/shard_map/ppermute | solution.py:44
  394.0 38.0 %collective-permute-start.48 = (bf16[512,1536]{1,0:T(8,128)(2,1)S(1)}, bf16[512,1536]{1,0:T(8,128)(2,1)S(1)}, u32[]{:S(2)}, u32[]{:S(2)}) collective-permute-start(bf16[512,1536]{1,0:T(8,128)(2,1)S(1)} %copy-done.65), channel_id=1, source_target_pairs={{0,1},{1,0},{2,3},{3,2},{4,5},{5,4},{6,7},{7,6},{8,9},{9,8},{10,11... | collective-permute-start | bytes 4718600 | tf_op jit(solution)/shard_map/ppermute | solution.py:40
  394.0 35.7 %collective-permute-start.45 = (bf16[768,384]{1,0:T(8,128)(2,1)S(1)}, bf16[768,384]{1,0:T(8,128)(2,1)S(1)}, u32[]{:S(2)}, u32[]{:S(2)}) collective-permute-start(bf16[768,384]{1,0:T(8,128)(2,1)S(1)} %get-tuple-element.313), channel_id=1, source_target_pairs={{0,4},{4,0},{1,5},{5,1},{2,6},{6,2},{3,7},{7,3},{8,12},{12,8},{9,1... | collective-permute-start | bytes 1769480 | tf_op jit(solution)/shard_map/ppermute | solution.py:36
  401.2 34.0 %collective-permute-start.54 = (bf16[384,1152]{1,0:T(8,128)(2,1)S(1)}, bf16[384,1152]{1,0:T(8,128)(2,1)S(1)}, u32[]{:S(2)}, u32[]{:S(2)}) collective-permute-start(bf16[384,1152]{1,0:T(8,128)(2,1)S(1)} %add.188.total), channel_id=1, source_target_pairs={{0,8},{8,0},{16,24},{24,16},{1,9},{9,1},{17,25},{25,17},{2,10},{10... | collective-permute-start | bytes 2654216 | tf_op jit(solution)/shard_map/ppermute | solution.py:65
  418.5 41.8 %collective-permute-start.53 = (bf16[576,768]{1,0:T(8,128)(2,1)S(1)}, bf16[576,768]{1,0:T(8,128)(2,1)S(1)}, u32[]{:S(2)}, u32[]{:S(2)}) collective-permute-start(bf16[576,768]{1,0:T(8,128)(2,1)S(1)} %add.189.right), channel_id=1, source_target_pairs={{0,24},{8,16},{16,8},{24,0},{1,25},{9,17},{17,9},{25,1},{2,26},{10... | collective-permute-start | bytes 2654216 | tf_op jit(solution)/shard_map/ppermute | solution.py:70
  430.3 33.4 %collective-permute-start.50 = (bf16[768,384]{1,0:T(8,128)(2,1)S(1)}, bf16[768,384]{1,0:T(8,128)(2,1)S(1)}, u32[]{:S(2)}, u32[]{:S(2)}) collective-permute-start(bf16[768,384]{1,0:T(8,128)(2,1)S(1)} %get-tuple-element.308), channel_id=1, source_target_pairs={{0,4},{4,0},{1,5},{5,1},{2,6},{6,2},{3,7},{7,3},{8,12},{12,8},{9,1... | collective-permute-start | bytes 1769480 | tf_op jit(solution)/shard_map/ppermute | solution.py:36
  432.0 31.7 %collective-permute-start.51 = (bf16[768,384]{1,0:T(8,128)(2,1)S(1)}, bf16[768,384]{1,0:T(8,128)(2,1)S(1)}, u32[]{:S(2)}, u32[]{:S(2)}) collective-permute-start(bf16[768,384]{1,0:T(8,128)(2,1)S(1)} %get-tuple-element.310), channel_id=1, source_target_pairs={{0,4},{4,0},{1,5},{5,1},{2,6},{6,2},{3,7},{7,3},{8,12},{12,8},{9,1... | collective-permute-start | bytes 1769480 | tf_op jit(solution)/shard_map/ppermute | solution.py:36
  433.2 30.6 %collective-permute-start.52 = (bf16[768,384]{1,0:T(8,128)(2,1)S(1)}, bf16[768,384]{1,0:T(8,128)(2,1)S(1)}, u32[]{:S(2)}, u32[]{:S(2)}) collective-permute-start(bf16[768,384]{1,0:T(8,128)(2,1)S(1)} %add.193), channel_id=1, source_target_pairs={{0,2},{2,0},{1,3},{3,1},{4,6},{6,4},{5,7},{7,5},{8,10},{10,8},{9,1... | collective-permute-start | bytes 1769480 | tf_op jit(solution)/shard_map/ppermute | solution.py:44
  435.2 31.5 %collective-permute-start.49 = (bf16[512,1536]{1,0:T(8,128)(2,1)S(1)}, bf16[512,1536]{1,0:T(8,128)(2,1)S(1)}, u32[]{:S(2)}, u32[]{:S(2)}) collective-permute-start(bf16[512,1536]{1,0:T(8,128)(2,1)S(1)} %get-tuple-element.240), channel_id=1, source_target_pairs={{0,1},{1,0},{2,3},{3,2},{4,5},{5,4},{6,7},{7,6},{8,9},{9,8},{10,11... | collective-permute-start | bytes 4718600 | tf_op jit(solution)/shard_map/ppermute | solution.py:40
  460.2 36.0 %collective-permute-start.55 = (bf16[512,1536]{1,0:T(8,128)(2,1)S(1)}, bf16[512,1536]{1,0:T(8,128)(2,1)S(1)}, u32[]{:S(2)}, u32[]{:S(2)}) collective-permute-start(bf16[512,1536]{1,0:T(8,128)(2,1)S(1)} %add.192), channel_id=1, source_target_pairs={{0,2},{2,0},{1,3},{3,1},{4,6},{6,4},{5,7},{7,5},{8,10},{10,8},{9,1... | collective-permute-start | bytes 4718600 | tf_op jit(solution)/shard_map/ppermute | solution.py:44
  466.6 39.1 %collective-permute-start.58 = (bf16[576,768]{1,0:T(8,128)(2,1)S(1)}, bf16[576,768]{1,0:T(8,128)(2,1)S(1)}, u32[]{:S(2)}, u32[]{:S(2)}) collective-permute-start(bf16[576,768]{1,0:T(8,128)(2,1)S(1)} %add.194.total), channel_id=1, source_target_pairs={{0,8},{8,0},{16,24},{24,16},{1,9},{9,1},{17,25},{25,17},{2,10},{10... | collective-permute-start | bytes 2654216 | tf_op jit(solution)/shard_map/ppermute | solution.py:65
  487.4 38.2 %collective-permute-start.60 = (bf16[384,1152]{1,0:T(8,128)(2,1)S(1)}, bf16[384,1152]{1,0:T(8,128)(2,1)S(1)}, u32[]{:S(2)}, u32[]{:S(2)}) collective-permute-start(bf16[384,1152]{1,0:T(8,128)(2,1)S(1)} %add.196.right), channel_id=1, source_target_pairs={{0,24},{8,16},{16,8},{24,0},{1,25},{9,17},{17,9},{25,1},{2,26},{10... | collective-permute-start | bytes 2654216 | tf_op jit(solution)/shard_map/ppermute | solution.py:70
  509.4 32.1 %collective-permute-start.57 = (bf16[512,768]{1,0:T(8,128)(2,1)S(1)}, bf16[512,768]{1,0:T(8,128)(2,1)S(1)}, u32[]{:S(2)}, u32[]{:S(2)}) collective-permute-start(bf16[512,768]{1,0:T(8,128)(2,1)S(1)} %slice.158), channel_id=1, source_target_pairs={{0,4},{4,0},{1,5},{5,1},{2,6},{6,2},{3,7},{7,3},{8,12},{12,8},{9,1... | collective-permute-start | bytes 2359304 | tf_op jit(solution)/shard_map/ppermute | solution.py:36
  (136 other events, 1676.4 us)
